TPU v7x, 256 devices: a whole 4x4x8 slice. The times are simulated.
256 devices in a mesh: dp: 2 (over x_hi), expert: 4 (over x_lo, core), tensor: 32 (over z, y).
Axes of the slice: x: 4 (x_hi: 2, x_lo: 2; x = x_hi * 2 + x_lo), y: 4, z: 8, core: 2. Of those that a mesh axis runs over, the one named last changes fastest.
Arguments:
- tokens: bfloat16 [1024, 7168], P(('dp', 'expert', 'tensor')), may hold values from -6 to 6
- routes: int32 [1024, 2], P(('dp', 'expert', 'tensor')), may hold values from 0 to 3, all different within a row; in each aligned block of 128 rows (0 to 127, 128 to 255, ...) at most 96 rows name the same one
- route_gates: bfloat16 [1024, 2], P(('dp', 'expert', 'tensor')), may hold values from 0.19921875 to 1
- cotangent: bfloat16 [1024, 7168], P(('dp', 'expert', 'tensor')), may hold values from -6 to 6
- dense_gate: bfloat16 [4864, 7168], P('tensor'), may hold values from -0.0625 to 0.0625
- dense_up: bfloat16 [4864, 7168], P('tensor'), may hold values from -0.0625 to 0.0625
- dense_down: bfloat16 [4864, 7168], P('tensor'), may hold values from -0.078125 to 0.078125
- expert_gate: bfloat16 [4, 4864, 7168], P('expert', 'tensor', 'dp'), may hold values from -0.0625 to 0.0625
- expert_up: bfloat16 [4, 4864, 7168], P('expert', 'tensor', 'dp'), may hold values from -0.0625 to 0.0625
- expert_down: bfloat16 [4, 4864, 7168], P('expert', 'tensor', 'dp'), may hold values from -0.078125 to 0.078125
Outputs:
- mixed: bfloat16 [1024, 7168], P(('dp', 'expert', 'tensor'))
- grad_tokens: bfloat16 [1024, 7168], P(('dp', 'expert', 'tensor'))
- grad_expert_gate: bfloat16 [4, 4864, 7168], P('expert', 'tensor', 'dp')
- grad_expert_up: bfloat16 [4, 4864, 7168], P('expert', 'tensor', 'dp')
- grad_expert_down: bfloat16 [4, 4864, 7168], P('expert', 'tensor', 'dp')
Inputs may be any that keep to these rules, and one draw needn't show every extreme that they name: `routes`: in each aligned block of 128 rows (one group) the two experts of a row differ and no expert is named by more than 96 rows; in some block an expert is named by exactly 96 rows.
All inputs are finite; a program needn't handle non-finite values.
Results may differ from a plain program's by a relative error of at most 0.022.
Values may be sent and summed in bfloat16 or wider, within the bound.
No kernel may reach another device: no remote copies, remote signals or barrier semaphores. Data moves between devices by JAX's collectives and lax.ppermute only.
A program may use at most 128 MiB of HBM per device.

v0:
```python
import jax
import jax.numpy as jnp
from jax import lax
from jax.sharding import Mesh, PartitionSpec as P

BF = jnp.bfloat16
F32 = jnp.float32


def shift(value, axis, by):
    size = lax.axis_size(axis)
    return lax.ppermute(value, axis, [(i, (i + by) % size) for i in range(size)])


def swap(value, axes):
    size = 1
    for axis in axes:
        size *= lax.axis_size(axis)
    return lax.ppermute(value, axes, [(i, size - 1 - i) for i in range(size)])


def gather(block, axis):
    size = lax.axis_size(axis)
    wide = jnp.broadcast_to(block[None], (size,) + block.shape)
    return lax.all_to_all(wide, axis, 0, 0, tiled=True).reshape(-1, block.shape[1])


def scatter(part, axis):
    size = lax.axis_size(axis)
    landed = lax.all_to_all(part.reshape(size, -1, part.shape[1]), axis, 0, 0, tiled=True)
    return jnp.sum(landed.astype(F32), axis=0)


def in_order(data, mine, other):
    return jnp.where(data == 0, jnp.concatenate([mine, other], axis=0), jnp.concatenate([other, mine], axis=0))


def finish(part, data):
    rows = part.shape[0] // 2
    own = jnp.where(data == 0, part[:rows], part[rows:])
    other = swap(jnp.where(data == 0, part[rows:], part[:rows]), ("dp",))
    return jnp.where(
        data == 0, jnp.concatenate([own, other], axis=1), jnp.concatenate([other, own], axis=1)
    ).astype(BF)


def dot(left, right, dims):
    return lax.dot_general(left, right, (dims, ((), ())), preferred_element_type=F32)


def per_device(
    tokens, routes, route_gates, cotangent, dense_gate, dense_up, dense_down,
    expert_gate, expert_up, expert_down,
):
    width = expert_gate.shape[2]
    hidden = expert_gate.shape[1]
    hidden_half = hidden // 2
    data, near, core = (lax.axis_index(name) for name in ("dp", "xlo", "core"))
    experts = lax.axis_size("xlo") * lax.axis_size("core")
    rows = tokens.shape[0]

    def columns(array, at):
        return lax.dynamic_slice_in_dim(array, at * width, width, axis=1)

    ids = jnp.arange(128, dtype=jnp.int32)
    weights_of = jnp.sum(
        jnp.where(routes[:, :, None] == ids[None, None, :], route_gates.astype(F32)[:, :, None], 0.0), axis=1
    ).astype(BF)
    tok_own = jnp.concatenate([columns(tokens, data), weights_of], axis=1)
    tok_far = jnp.concatenate([columns(tokens, 1 - data), weights_of], axis=1)
    cot = in_order(data, columns(cotangent, data), swap(columns(cotangent, 1 - data), ("dp",)))
    cot = gather(gather(cot, "z"), "y")
    cots = (cot, swap(cot, ("xlo",)))
    tok = jnp.concatenate(
        [
            in_order(data, tok_own, swap(tok_far, ("dp",))),
            in_order(data, swap(tok_own, ("xlo",)), swap(tok_far, ("dp", "xlo"))),
        ],
        axis=0,
    )
    pair = tok.shape[0] // 2
    tok = gather(tok, "z").reshape(-1, 2, pair, tok.shape[1])
    toks = [gather(tok[:, q].reshape(-1, tok.shape[3]), "y") for q in range(2)]

    expert_mine = jnp.stack([expert_gate[0], expert_up[0], expert_down[0]])
    expert_other = swap(expert_mine, ("core",))
    units = -(-(2 * hidden + hidden_half) // 128) * 128
    spare = jnp.zeros((units - 2 * hidden - hidden_half, width), BF)

    def pack(at, dense):
        dense_part = lax.dynamic_slice(dense, (near * hidden_half, data * width), (hidden_half, width))
        return [expert_mine[at], expert_other[at], dense_part, spare]

    gate_up = jnp.concatenate(pack(0, dense_gate) + pack(1, dense_up), axis=0)
    down = jnp.concatenate(pack(2, dense_down), axis=0)

    unit = jnp.arange(units, dtype=jnp.int32)[None]
    expert_id = near * lax.axis_size("core") + core
    terms = []
    for tok, cot in zip(toks, cots):
        weighting = tok[:, width:].astype(F32)
        tok = tok[:, :width]
        mine_w = jnp.sum(jnp.where(ids[None] == expert_id, weighting, 0.0), axis=1, keepdims=True)
        other_w = jnp.sum(jnp.where(ids[None] == expert_id + 1 - 2 * core, weighting, 0.0), axis=1, keepdims=True)
        scale = jnp.where(unit < hidden, mine_w, jnp.where(unit < 2 * hidden, other_w, 1.0))
        both = dot(tok, gate_up, ((1,), (1,))).astype(BF)
        both = both.astype(F32) + swap(both, ("dp",)).astype(F32)
        pre, lin = both[:, :units], both[:, units:]
        dact = dot(cot, down, ((1,), (1,))).astype(BF)
        dact = (dact.astype(F32) + swap(dact, ("dp",)).astype(F32)) * scale
        sig = jax.nn.sigmoid(pre)
        act = (pre * sig * lin * scale).astype(BF)
        gate_grad = (dact * lin * (sig * (1.0 + pre * (1.0 - sig)))).astype(BF)
        lin_grad = (dact * (pre * sig)).astype(BF)
        terms.append((tok, cot, act, gate_grad, lin_grad))

    mixed, grads = [], []
    for tok, cot, act, gate_grad, lin_grad in terms:
        both = jnp.concatenate([gate_grad, lin_grad], axis=1)
        grads.append(dot(both, gate_up, ((1,), (0,))).astype(BF))
        mixed.append(scatter(dot(act, down, ((1,), (0,))).astype(BF), "y").astype(BF))

    depth = lax.axis_size("z")
    mixed = jnp.concatenate([part.reshape(depth, pair, width) for part in mixed], axis=1)
    mixed = scatter(mixed.reshape(-1, width), "z")
    mixed = finish(mixed[:pair] + swap(mixed[pair:], ("xlo",)), data)

    grads = (grads[0].astype(F32) + swap(grads[1], ("xlo",)).astype(F32)).astype(BF)
    grads = finish(scatter(scatter(grads, "y").astype(BF), "z"), data)

    def weight_grad(lefts, rights):
        term = dot(lefts[0][:, :2 * hidden], rights[0], ((0,), (0,)))
        term = (term + dot(lefts[1][:, :2 * hidden], rights[1], ((0,), (0,)))).astype(BF)
        return (term[:hidden].astype(F32) + swap(term[hidden:], ("core",)).astype(F32)).astype(BF)[None]

    tok, cot, act, gate_grad, lin_grad = zip(*terms)
    return (
        mixed,
        grads,
        weight_grad(gate_grad, tok),
        weight_grad(lin_grad, tok),
        weight_grad(act, cot),
    )


def solution(mesh):
    fine = Mesh(mesh.devices.reshape(2, 2, 2, 8, 4), ("dp", "xlo", "core", "z", "y"))
    every = ("dp", "xlo", "core", "z", "y")
    row = P(every, None)
    dense = P(("z", "y"), None)
    expert = P(("xlo", "core"), ("z", "y"), "dp")
    return jax.shard_map(
        per_device,
        mesh=fine,
        in_specs=(row, row, row, row, dense, dense, dense, expert, expert, expert),
        out_specs=(row, row, expert, expert, expert),
        check_vma=False,
    )
```

profile of v0, /device:TPU:8, one launch (start us, length us, event | category | flops | bytes accessed | tf_op | source)
XLA Modules:
  0.0 345.0 jit_solution(13068985109826162252)
XLA Ops:
  11.8 8.5 %all-to-all-start.6 = ((bf16[8,8,3584]{2,1,0:T(8,128)(2,1)}), bf16[8,8,3584]{2,1,0:T(8,128)(2,1)S(1)}, u32[]{:S(2)}, u32[]{:S(2)}) async-start(bf16[8,8,3584]{2,1,0:T(8,128)(2,1)} %broadcast_in_dim.167), calls=%async_computation.6 | async-start | bytes 917504 | tf_op jit(solution)/shard_map/all_to_all | solution.py:25
  20.5 14.8 %all-to-all-done.6 = bf16[8,8,3584]{2,1,0:T(8,128)(2,1)S(1)} async-done(((bf16[8,8,3584]{2,1,0:T(8,128)(2,1)}), bf16[8,8,3584]{2,1,0:T(8,128)(2,1)S(1)}, u32[]{:S(2)}, u32[]{:S(2)}) %all-to-all-start.6) | async-done | bytes 458784 | tf_op jit(solution)/shard_map/all_to_all | solution.py:25
  35.3 27.4 %all_to_all.50 = bf16[8,16,3712]{2,1,0:T(8,128)(2,1)} all-to-all(bf16[8,16,3712]{2,1,0:T(8,128)(2,1)S(1)} %broadcast_in_dim.152), channel_id=1, replica_groups=mesh['dp'=2,'xlo'=2,'core'=2,'z'=8,'y'=4] {'z'}, dimensions={0} | all-to-all | bytes 1900544 | tf_op jit(solution)/shard_map/all_to_all | solution.py:25
  64.2 5.0 %all-to-all-start.7 = ((bf16[4,64,3584]{2,1,0:T(8,128)(2,1)}), bf16[4,64,3584]{2,1,0:T(8,128)(2,1)S(1)}, u32[]{:S(2)}, u32[]{:S(2)}) async-start(bf16[4,64,3584]{2,1,0:T(8,128)(2,1)} %broadcast_in_dim.169), calls=%async_computation.7 | async-start | bytes 3670016 | tf_op jit(solution)/shard_map/all_to_all | solution.py:25
  73.8 13.2 %all-to-all-done.7 = bf16[4,64,3584]{2,1,0:T(8,128)(2,1)S(1)} async-done(((bf16[4,64,3584]{2,1,0:T(8,128)(2,1)}), bf16[4,64,3584]{2,1,0:T(8,128)(2,1)S(1)}, u32[]{:S(2)}, u32[]{:S(2)}) %all-to-all-start.7) | async-done | bytes 1835040 | tf_op jit(solution)/shard_map/all_to_all | solution.py:25
  88.5 21.9 %all_to_all.51 = bf16[4,64,3712]{2,1,0:T(8,128)(2,1)} all-to-all(bf16[4,64,3712]{2,1,0:T(8,128)(2,1)S(1)} %broadcast_in_dim.164), channel_id=1, replica_groups=mesh['dp'=2,'xlo'=2,'core'=2,'z'=8,'y'=4] {'y'}, dimensions={0} | all-to-all | bytes 3801088 | tf_op jit(solution)/shard_map/all_to_all | solution.py:25
  111.9 5.0 %all-to-all-start.1 = ((bf16[4,64,3712]{2,1,0:T(8,128)(2,1)}), bf16[4,64,3712]{2,1,0:T(8,128)(2,1)S(1)}, u32[]{:S(2)}, u32[]{:S(2)}) async-start(bf16[4,64,3712]{2,1,0:T(8,128)(2,1)} %broadcast_in_dim.154), calls=%async_computation.1 | async-start | bytes 3801088 | tf_op jit(solution)/shard_map/all_to_all | solution.py:25
  124.1 9.1 %all-to-all-done.1 = bf16[4,64,3712]{2,1,0:T(8,128)(2,1)S(1)} async-done(((bf16[4,64,3712]{2,1,0:T(8,128)(2,1)}), bf16[4,64,3712]{2,1,0:T(8,128)(2,1)S(1)}, u32[]{:S(2)}, u32[]{:S(2)}) %all-to-all-start.1) | async-done | bytes 1900576 | tf_op jit(solution)/shard_map/all_to_all | solution.py:25
  137.9 31.9 %concatenate.69 = bf16[768,3584]{1,0:T(8,128)(2,1)} concatenate(bf16[152,3584]{1,0:T(8,128)(2,1)S(1)} %bitcast.55, bf16[152,3584]{1,0:T(8,128)(2,1)} %get-tuple-element.13, bf16[76,3584]{1,0:T(8,128)(2,1)} %dynamic_slice.23, bf16[4,3584]{1,0:T(4,128)(2,1)S(1)} %broadcast_in_dim.155, bf16[152,3584]{1,0:T(8,128)(2,1)} %bitcast.56, bf16[152,3584]{1,0:T(8,128)(2,1)} %get-tuple-element.12, ...), dimensions={0} | concatenate | bytes 11010048 | tf_op jit(solution)/shard_map/concatenate | solution.py:94
  169.9 5.6 %fusion.19 = bf16[256,768]{1,0:T(8,128)(2,1)} fusion(bf16[768,3584]{1,0:T(8,128)(2,1)} %concatenate.69, bf16[256,3712]{1,0:T(8,128)(2,1)} %bitcast.49), kind=kOutput, calls=%fused_computation.30 | convolution fusion | flops 1409482752 | bytes 7733248 | tf_op jit(solution)/shard_map/dot_general | solution.py:48
  177.1 5.3 %collective-permute-start.5 = (bf16[256,768]{1,0:T(8,128)(2,1)}, bf16[256,768]{1,0:T(8,128)(2,1)}, u32[]{:S(2)}, u32[]{:S(2)}) collective-permute-start(bf16[256,768]{1,0:T(8,128)(2,1)} %fusion.19), channel_id=1, source_target_pairs={{0,128},{128,0},{1,129},{129,1},{2,130},{130,2},{3,131},{131,3},{4... | collective-permute-start | bytes 1179656 | tf_op jit(solution)/shard_map/ppermute | solution.py:19
  183.7 3.7 %collective-permute-start.9 = (bf16[256,384]{1,0:T(8,128)(2,1)S(1)}, bf16[256,384]{1,0:T(8,128)(2,1)S(1)}, u32[]{:S(2)}, u32[]{:S(2)}) collective-permute-start(bf16[256,384]{1,0:T(8,128)(2,1)S(1)} %convolution_convert_fusion.5), channel_id=1, source_target_pairs={{0,128},{128,0},{1,129},{129,1},{2,130},{130,2},{3,131},{131,3},{4... | collective-permute-start | bytes 589832 | tf_op jit(solution)/shard_map/ppermute | solution.py:19
  187.4 8.0 %collective-permute-done.4 = bf16[256,768]{1,0:T(8,128)(2,1)S(1)} collective-permute-done((bf16[256,768]{1,0:T(8,128)(2,1)S(1)}, bf16[256,768]{1,0:T(8,128)(2,1)S(1)}, u32[]{:S(2)}, u32[]{:S(2)}) %collective-permute-start.4) | collective-permute-done | bytes 393248 | tf_op jit(solution)/shard_map/ppermute | solution.py:19
  200.2 5.9 %all-to-all-start.2 = ((bf16[4,64,3584]{2,1,0:T(8,128)(2,1)}), bf16[4,64,3584]{2,1,0:T(8,128)(2,1)}, u32[]{:S(2)}, u32[]{:S(2)}) async-start(bf16[4,64,3584]{2,1,0:T(8,128)(2,1)} %bitcast.60), calls=%async_computation.2 | async-start | bytes 3670016 | tf_op jit(solution)/shard_map/all_to_all | solution.py:30
  206.1 4.4 %fusion.34 = f32[304,3584]{1,0:T(8,128)} fusion(bf16[256,3584]{1,0:T(8,128)(2,1)} %bitcast.53, bf16[256,384]{1,0:T(8,128)(2,1)} %copy-done.14), kind=kOutput, calls=%fused_computation.66 | convolution fusion | flops 557842432 | bytes 6389760 | tf_op jit(solution)/shard_map/dot_general | solution.py:48
  228.7 4.9 %all-to-all-start.4 = ((bf16[4,64,3584]{2,1,0:T(8,128)(2,1)}), bf16[4,64,3584]{2,1,0:T(8,128)(2,1)}, u32[]{:S(2)}, u32[]{:S(2)}) async-start(bf16[4,64,3584]{2,1,0:T(8,128)(2,1)} %bitcast.13), calls=%async_computation.4 | async-start | bytes 3670016 | tf_op jit(solution)/shard_map/all_to_all | solution.py:30
  233.6 5.5 %convolution_convert_fusion = bf16[256,3584]{1,0:T(8,128)(2,1)} fusion(bf16[768,3584]{1,0:T(8,128)(2,1)} %concatenate.69, bf16[256,384]{1,0:T(8,128)(2,1)S(1)} %get-tuple-element.17, bf16[256,384]{1,0:T(8,128)(2,1)S(1)} %get-tuple-element.16), kind=kOutput, calls=%fused_computation.6 | convolution fusion | flops 1410990080 | bytes 7733248 | tf_op jit(solution)/shard_map/dot_general | solution.py:48
  254.8 8.3 %all-to-all-start.5 = ((bf16[8,16,3584]{2,1,0:T(8,128)(2,1)}), bf16[8,16,3584]{2,1,0:T(8,128)(2,1)S(1)}, u32[]{:S(2)}, u32[]{:S(2)}) async-start(bf16[8,16,3584]{2,1,0:T(8,128)(2,1)} %pad_maximum_fusion.2), calls=%async_computation.5 | async-start | bytes 1835008 | tf_op jit(solution)/shard_map/all_to_all | solution.py:30
  268.7 3.7 %collective-permute-done.12 = bf16[256,3584]{1,0:T(8,128)(2,1)} collective-permute-done((bf16[256,3584]{1,0:T(8,128)(2,1)}, bf16[256,3584]{1,0:T(8,128)(2,1)}, u32[]{:S(2)}, u32[]{:S(2)}) %collective-permute-start.12) | collective-permute-done | bytes 1835040 | tf_op jit(solution)/shard_map/ppermute | solution.py:19
  272.4 6.0 %fusion.5 = bf16[256,3584]{1,0:T(8,128)(2,1)} fusion(bf16[768,3584]{1,0:T(8,128)(2,1)} %concatenate.69, bf16[256,3584]{1,0:T(8,128)(2,1)} %collective-permute-done.12, bf16[256,384]{1,0:T(8,128)(2,1)S(1)} %copy-done.13, bf16[256,384]{1,0:T(8,128)(2,1)S(1)} %get-tuple-element.14), kind=kOutput, calls=%fused_computation.10 | convolution fusion | flops 1414660096 | bytes 9568256 | tf_op jit(solution)/shard_map/dot_general | solution.py:48
  278.4 11.4 %all-to-all-done.5 = bf16[8,16,3584]{2,1,0:T(8,128)(2,1)S(1)} async-done(((bf16[8,16,3584]{2,1,0:T(8,128)(2,1)}), bf16[8,16,3584]{2,1,0:T(8,128)(2,1)S(1)}, u32[]{:S(2)}, u32[]{:S(2)}) %all-to-all-start.5) | async-done | bytes 917536 | tf_op jit(solution)/shard_map/all_to_all | solution.py:30
  289.8 4.8 %all-to-all-start.8 = ((bf16[4,64,3584]{2,1,0:T(8,128)(2,1)}), bf16[4,64,3584]{2,1,0:T(8,128)(2,1)}, u32[]{:S(2)}, u32[]{:S(2)}) async-start(bf16[4,64,3584]{2,1,0:T(8,128)(2,1)} %bitcast.61), calls=%async_computation.8 | async-start | bytes 3670016 | tf_op jit(solution)/shard_map/all_to_all | solution.py:30
  299.6 17.5 %all-to-all-done.8 = bf16[4,64,3584]{2,1,0:T(8,128)(2,1)} async-done(((bf16[4,64,3584]{2,1,0:T(8,128)(2,1)}), bf16[4,64,3584]{2,1,0:T(8,128)(2,1)}, u32[]{:S(2)}, u32[]{:S(2)}) %all-to-all-start.8) | async-done | bytes 1835040 | tf_op jit(solution)/shard_map/all_to_all | solution.py:30
  325.4 13.4 %all-to-all-done.9 = bf16[8,8,3584]{2,1,0:T(8,128)(2,1)S(1)} async-done(((bf16[8,8,3584]{2,1,0:T(8,128)(2,1)}), bf16[8,8,3584]{2,1,0:T(8,128)(2,1)S(1)}, u32[]{:S(2)}, u32[]{:S(2)}) %all-to-all-start.9) | async-done | bytes 458784 | tf_op jit(solution)/shard_map/all_to_all | solution.py:30
  (133 shorter events, 98.5 us)
Async XLA Ops:
  1.4 9.5 %collective-permute-start.8 = (bf16[4,3584]{1,0:T(4,128)(2,1)S(1)}, bf16[4,3584]{1,0:T(4,128)(2,1)S(1)}, u32[]{:S(2)}, u32[]{:S(2)}) collective-permute-start(bf16[4,3584]{1,0:T(4,128)(2,1)S(1)} %get-tuple-element.25), channel_id=1, source_target_pairs={{0,128},{128,0},{1,129},{129,1},{2,130},{130,2},{3,131},{131,3},{4... | collective-permute-start | bytes 86024 | tf_op jit(solution)/shard_map/ppermute | solution.py:19
  6.8 13.6 %collective-permute-start.2 = (bf16[4,3712]{1,0:T(4,128)(2,1)S(1)}, bf16[4,3712]{1,0:T(4,128)(2,1)S(1)}, u32[]{:S(2)}, u32[]{:S(2)}) collective-permute-start(bf16[4,3712]{1,0:T(4,128)(2,1)S(1)} %get-tuple-element.31), channel_id=1, source_target_pairs={{0,192},{64,128},{128,64},{192,0},{1,193},{65,129},{129,65},{193,1... | collective-permute-start | bytes 89096 | tf_op jit(solution)/shard_map/ppermute | solution.py:19
  8.0 12.3 %collective-permute-start = (bf16[4,3712]{1,0:T(4,128)(2,1)S(1)}, bf16[4,3712]{1,0:T(4,128)(2,1)S(1)}, u32[]{:S(2)}, u32[]{:S(2)}) collective-permute-start(bf16[4,3712]{1,0:T(4,128)(2,1)S(1)} %get-tuple-element.31), channel_id=1, source_target_pairs={{0,128},{128,0},{1,129},{129,1},{2,130},{130,2},{3,131},{131,3},{4... | collective-permute-start | bytes 89096 | tf_op jit(solution)/shard_map/ppermute | solution.py:19
  9.5 10.8 %collective-permute-start.1 = (bf16[4,3712]{1,0:T(4,128)(2,1)S(1)}, bf16[4,3712]{1,0:T(4,128)(2,1)S(1)}, u32[]{:S(2)}, u32[]{:S(2)}) collective-permute-start(bf16[4,3712]{1,0:T(4,128)(2,1)S(1)} %get-tuple-element.30), channel_id=1, source_target_pairs={{0,64},{64,0},{1,65},{65,1},{2,66},{66,2},{3,67},{67,3},{4,68},{68... | collective-permute-start | bytes 89096 | tf_op jit(solution)/shard_map/ppermute | solution.py:19
  11.8 23.4 %all-to-all-start.6 = ((bf16[8,8,3584]{2,1,0:T(8,128)(2,1)}), bf16[8,8,3584]{2,1,0:T(8,128)(2,1)S(1)}, u32[]{:S(2)}, u32[]{:S(2)}) async-start(bf16[8,8,3584]{2,1,0:T(8,128)(2,1)} %broadcast_in_dim.167), calls=%async_computation.6 | async-start | bytes 917504 | tf_op jit(solution)/shard_map/all_to_all | solution.py:25
  64.2 22.8 %all-to-all-start.7 = ((bf16[4,64,3584]{2,1,0:T(8,128)(2,1)}), bf16[4,64,3584]{2,1,0:T(8,128)(2,1)S(1)}, u32[]{:S(2)}, u32[]{:S(2)}) async-start(bf16[4,64,3584]{2,1,0:T(8,128)(2,1)} %broadcast_in_dim.169), calls=%async_computation.7 | async-start | bytes 3670016 | tf_op jit(solution)/shard_map/all_to_all | solution.py:25
  72.9 61.3 %collective-permute-start.3 = (bf16[3,152,3584]{2,1,0:T(8,128)(2,1)}, bf16[3,152,3584]{2,1,0:T(8,128)(2,1)}, u32[]{:S(2)}, u32[]{:S(2)}) collective-permute-start(bf16[3,152,3584]{2,1,0:T(8,128)(2,1)} %pad_maximum_fusion), channel_id=1, source_target_pairs={{0,32},{32,0},{1,33},{33,1},{2,34},{34,2},{3,35},{35,3},{4,36},{36... | collective-permute-start | bytes 9805832 | tf_op jit(solution)/shard_map/ppermute | solution.py:19
  111.9 21.3 %all-to-all-start.1 = ((bf16[4,64,3712]{2,1,0:T(8,128)(2,1)}), bf16[4,64,3712]{2,1,0:T(8,128)(2,1)S(1)}, u32[]{:S(2)}, u32[]{:S(2)}) async-start(bf16[4,64,3712]{2,1,0:T(8,128)(2,1)} %broadcast_in_dim.154), calls=%async_computation.1 | async-start | bytes 3801088 | tf_op jit(solution)/shard_map/all_to_all | solution.py:25
  123.5 92.6 %collective-permute-start.10 = (bf16[256,3584]{1,0:T(8,128)(2,1)}, bf16[256,3584]{1,0:T(8,128)(2,1)}, u32[]{:S(2)}, u32[]{:S(2)}) collective-permute-start(bf16[256,3584]{1,0:T(8,128)(2,1)} %bitcast.52), channel_id=1, source_target_pairs={{0,64},{64,0},{1,65},{65,1},{2,66},{66,2},{3,67},{67,3},{4,68},{68... | collective-permute-start | bytes 5505032 | tf_op jit(solution)/shard_map/ppermute | solution.py:19
  177.1 45.0 %collective-permute-start.5 = (bf16[256,768]{1,0:T(8,128)(2,1)}, bf16[256,768]{1,0:T(8,128)(2,1)}, u32[]{:S(2)}, u32[]{:S(2)}) collective-permute-start(bf16[256,768]{1,0:T(8,128)(2,1)} %fusion.19), channel_id=1, source_target_pairs={{0,128},{128,0},{1,129},{129,1},{2,130},{130,2},{3,131},{131,3},{4... | collective-permute-start | bytes 1179656 | tf_op jit(solution)/shard_map/ppermute | solution.py:19
  182.5 13.0 %collective-permute-start.4 = (bf16[256,768]{1,0:T(8,128)(2,1)S(1)}, bf16[256,768]{1,0:T(8,128)(2,1)S(1)}, u32[]{:S(2)}, u32[]{:S(2)}) collective-permute-start(bf16[256,768]{1,0:T(8,128)(2,1)S(1)} %fusion.16), channel_id=1, source_target_pairs={{0,128},{128,0},{1,129},{129,1},{2,130},{130,2},{3,131},{131,3},{4... | collective-permute-start | bytes 1179656 | tf_op jit(solution)/shard_map/ppermute | solution.py:19
  183.7 13.8 %collective-permute-start.9 = (bf16[256,384]{1,0:T(8,128)(2,1)S(1)}, bf16[256,384]{1,0:T(8,128)(2,1)S(1)}, u32[]{:S(2)}, u32[]{:S(2)}) collective-permute-start(bf16[256,384]{1,0:T(8,128)(2,1)S(1)} %convolution_convert_fusion.5), channel_id=1, source_target_pairs={{0,128},{128,0},{1,129},{129,1},{2,130},{130,2},{3,131},{131,3},{4... | collective-permute-start | bytes 589832 | tf_op jit(solution)/shard_map/ppermute | solution.py:19
  200.2 28.5 %all-to-all-start.2 = ((bf16[4,64,3584]{2,1,0:T(8,128)(2,1)}), bf16[4,64,3584]{2,1,0:T(8,128)(2,1)}, u32[]{:S(2)}, u32[]{:S(2)}) async-start(bf16[4,64,3584]{2,1,0:T(8,128)(2,1)} %bitcast.60), calls=%async_computation.2 | async-start | bytes 3670016 | tf_op jit(solution)/shard_map/all_to_all | solution.py:30
  218.8 7.3 %collective-permute-start.11 = (bf16[256,384]{1,0:T(8,128)(2,1)S(1)}, bf16[256,384]{1,0:T(8,128)(2,1)S(1)}, u32[]{:S(2)}, u32[]{:S(2)}) collective-permute-start(bf16[256,384]{1,0:T(8,128)(2,1)S(1)} %convolution_convert_fusion.4), channel_id=1, source_target_pairs={{0,128},{128,0},{1,129},{129,1},{2,130},{130,2},{3,131},{131,3},{4... | collective-permute-start | bytes 589832 | tf_op jit(solution)/shard_map/ppermute | solution.py:19
  228.7 23.3 %all-to-all-start.4 = ((bf16[4,64,3584]{2,1,0:T(8,128)(2,1)}), bf16[4,64,3584]{2,1,0:T(8,128)(2,1)}, u32[]{:S(2)}, u32[]{:S(2)}) async-start(bf16[4,64,3584]{2,1,0:T(8,128)(2,1)} %bitcast.13), calls=%async_computation.4 | async-start | bytes 3670016 | tf_op jit(solution)/shard_map/all_to_all | solution.py:30
  239.1 33.2 %collective-permute-start.12 = (bf16[256,3584]{1,0:T(8,128)(2,1)}, bf16[256,3584]{1,0:T(8,128)(2,1)}, u32[]{:S(2)}, u32[]{:S(2)}) collective-permute-start(bf16[256,3584]{1,0:T(8,128)(2,1)} %convolution_convert_fusion), channel_id=1, source_target_pairs={{0,64},{64,0},{1,65},{65,1},{2,66},{66,2},{3,67},{67,3},{4,68},{68... | collective-permute-start | bytes 5505032 | tf_op jit(solution)/shard_map/ppermute | solution.py:19
  243.3 19.9 %collective-permute-start.14 = (bf16[152,3584]{1,0:T(8,128)(2,1)}, bf16[152,3584]{1,0:T(8,128)(2,1)}, u32[]{:S(2)}, u32[]{:S(2)}) collective-permute-start(bf16[152,3584]{1,0:T(8,128)(2,1)} %slice.150), channel_id=1, source_target_pairs={{0,32},{32,0},{1,33},{33,1},{2,34},{34,2},{3,35},{35,3},{4,36},{36... | collective-permute-start | bytes 3268616 | tf_op jit(solution)/shard_map/ppermute | solution.py:19
  245.2 21.0 %collective-permute-start.15 = (bf16[152,3584]{1,0:T(8,128)(2,1)}, bf16[152,3584]{1,0:T(8,128)(2,1)}, u32[]{:S(2)}, u32[]{:S(2)}) collective-permute-start(bf16[152,3584]{1,0:T(8,128)(2,1)} %slice.154), channel_id=1, source_target_pairs={{0,32},{32,0},{1,33},{33,1},{2,34},{34,2},{3,35},{35,3},{4,36},{36... | collective-permute-start | bytes 3268616 | tf_op jit(solution)/shard_map/ppermute | solution.py:19
  250.2 46.0 %collective-permute-start.16 = (bf16[152,3584]{1,0:T(8,128)(2,1)}, bf16[152,3584]{1,0:T(8,128)(2,1)}, u32[]{:S(2)}, u32[]{:S(2)}) collective-permute-start(bf16[152,3584]{1,0:T(8,128)(2,1)} %slice.158), channel_id=1, source_target_pairs={{0,32},{32,0},{1,33},{33,1},{2,34},{34,2},{3,35},{35,3},{4,36},{36... | collective-permute-start | bytes 3268616 | tf_op jit(solution)/shard_map/ppermute | solution.py:19
  254.8 34.9 %all-to-all-start.5 = ((bf16[8,16,3584]{2,1,0:T(8,128)(2,1)}), bf16[8,16,3584]{2,1,0:T(8,128)(2,1)S(1)}, u32[]{:S(2)}, u32[]{:S(2)}) async-start(bf16[8,16,3584]{2,1,0:T(8,128)(2,1)} %pad_maximum_fusion.2), calls=%async_computation.5 | async-start | bytes 1835008 | tf_op jit(solution)/shard_map/all_to_all | solution.py:30
  289.8 27.3 %all-to-all-start.8 = ((bf16[4,64,3584]{2,1,0:T(8,128)(2,1)}), bf16[4,64,3584]{2,1,0:T(8,128)(2,1)}, u32[]{:S(2)}, u32[]{:S(2)}) async-start(bf16[4,64,3584]{2,1,0:T(8,128)(2,1)} %bitcast.61), calls=%async_computation.8 | async-start | bytes 3670016 | tf_op jit(solution)/shard_map/all_to_all | solution.py:30
  319.7 19.0 %all-to-all-start.9 = ((bf16[8,8,3584]{2,1,0:T(8,128)(2,1)}), bf16[8,8,3584]{2,1,0:T(8,128)(2,1)S(1)}, u32[]{:S(2)}, u32[]{:S(2)}) async-start(bf16[8,8,3584]{2,1,0:T(8,128)(2,1)} %bitcast.18), calls=%async_computation.9 | async-start | bytes 917504 | tf_op jit(solution)/shard_map/all_to_all | solution.py:30
  323.3 17.7 %collective-permute-start.7 = (bf16[4,3584]{1,0:T(4,128)(2,1)S(1)}, bf16[4,3584]{1,0:T(4,128)(2,1)S(1)}, u32[]{:S(2)}, u32[]{:S(2)}) collective-permute-start(bf16[4,3584]{1,0:T(4,128)(2,1)S(1)} %get-tuple-element.27), channel_id=1, source_target_pairs={{0,128},{128,0},{1,129},{129,1},{2,130},{130,2},{3,131},{131,3},{4... | collective-permute-start | bytes 86024 | tf_op jit(solution)/shard_map/ppermute | solution.py:19
  338.8 5.5 %collective-permute-start.13 = (bf16[4,3584]{1,0:T(4,128)(2,1)S(1)}, bf16[4,3584]{1,0:T(4,128)(2,1)S(1)}, u32[]{:S(2)}, u32[]{:S(2)}) collective-permute-start(bf16[4,3584]{1,0:T(4,128)(2,1)S(1)} %get-tuple-element.23), channel_id=1, source_target_pairs={{0,128},{128,0},{1,129},{129,1},{2,130},{130,2},{3,131},{131,3},{4... | collective-permute-start | bytes 86024 | tf_op jit(solution)/shard_map/ppermute | solution.py:19
  (22 other events, 148.3 us)
where the time goes:
time: 348 us; the launch traced here: 345 us
  waiting for transfers between devices  99.5 us (29%)
  starting transfers between devices  72.7 us (21%)
  local copies, waits for them, and re-layouts  54.2 us (16%)
  blocking collectives  49.3 us (14%)
  matrix products  43.3 us (12%)
  other arithmetic  25 us (7%)
    all_to_all x2, blocking collectives, gather(): lax.all_to_all(wide, axis, 0, 0, tiled=True).reshape(-1, block.shape[1])  49.3 us
    dot_general x14, matrix products, dot(): lax.dot_general(left, right, (dims, ((), ())), preferred_element_type=F32)  43.3 us
    all_to_all x5, waiting for transfers between devices, scatter(): lax.all_to_all(part.reshape(size, -1, part.shape[1]), axis, 0, 0, tiled=T...  42.2 us
    all_to_all x3, waiting for transfers between devices, gather(): lax.all_to_all(wide, axis, 0, 0, tiled=True).reshape(-1, block.shape[1])  37.1 us
    concatenate x1, local copies, waits for them, and re-layouts, per_device(): gate_up = jnp.concatenate(pack(0, dense_gate) + pack(1, dense_up), axis=0)  31.9 us
    all_to_all x5, starting transfers between devices, scatter(): lax.all_to_all(part.reshape(size, -1, part.shape[1]), axis, 0, 0, tiled=T...  27.4 us
    ppermute x17, starting transfers between devices, swap(): return lax.ppermute(value, axes, [(i, size - 1 - i) for i in range(size)])  26.7 us
    ppermute x17, waiting for transfers between devices, swap(): return lax.ppermute(value, axes, [(i, size - 1 - i) for i in range(size)])  20.1 us
  transfers between devices with their start and end apart: 25, of which 12 were waited for; matrix products, arithmetic and copies ran while one was open for 34% of the time, Pallas kernels for 0%

commit v1 on v0

v1 whole, which is shorter than its diff:
```python
import jax
import jax.numpy as jnp
from jax import lax
from jax.sharding import Mesh, PartitionSpec as P

BF = jnp.bfloat16
F32 = jnp.float32


def swap(value, axes):
    size = 1
    for axis in axes:
        size *= lax.axis_size(axis)
    return lax.ppermute(value, axes, [(i, size - 1 - i) for i in range(size)])


def scatter(part, axis):
    size = lax.axis_size(axis)
    landed = lax.all_to_all(part.reshape(size, -1, part.shape[1]), axis, 0, 0, tiled=True)
    return jnp.sum(landed.astype(F32), axis=0)


def in_order(data, mine, other):
    return jnp.where(data == 0, jnp.concatenate([mine, other], axis=0), jnp.concatenate([other, mine], axis=0))


def gather(block, axis):
    size = lax.axis_size(axis)
    wide = jnp.broadcast_to(block[None], (size,) + block.shape)
    return lax.all_to_all(wide, axis, 0, 0, tiled=True)


def join(parts):
    return jnp.concatenate(parts, axis=0)


def stack_rows(parts, rows):
    total, start = None, 0
    for part in parts:
        here = lax.pad(part, jnp.zeros((), BF), ((start, rows - start - part.shape[0], 0), (0, 0, 0)))
        total = here if total is None else total + here
        start += part.shape[0]
    return total


def finish(part, data):
    rows = part.shape[0] // 2
    own = jnp.where(data == 0, part[:rows], part[rows:])
    other = swap(jnp.where(data == 0, part[rows:], part[:rows]), ("dp",))
    return jnp.where(
        data == 0, jnp.concatenate([own, other], axis=1), jnp.concatenate([other, own], axis=1)
    ).astype(BF)


def dot(left, right, dims):
    return lax.dot_general(left, right, (dims, ((), ())), preferred_element_type=F32)


def per_device(
    tokens, routes, route_gates, cotangent, dense_gate, dense_up, dense_down,
    expert_gate, expert_up, expert_down,
):
    width = expert_gate.shape[2]
    hidden = expert_gate.shape[1]
    data, near, core = (lax.axis_index(name) for name in ("dp", "xlo", "core"))
    rows = tokens.shape[0]
    depth = lax.axis_size("z")

    def columns(array, at):
        return lax.dynamic_slice_in_dim(array, at * width, width, axis=1)

    ids = jnp.arange(128, dtype=jnp.int32)
    weights_of = jnp.sum(
        jnp.where(routes[:, :, None] == ids[None, None, :], route_gates.astype(F32)[:, :, None], 0.0), axis=1
    ).astype(BF)
    blank = jnp.zeros_like(weights_of)
    tok_own = jnp.concatenate([columns(tokens, data), weights_of], axis=1)
    tok_far = jnp.concatenate([columns(tokens, 1 - data), weights_of], axis=1)
    cot_own = jnp.concatenate([columns(cotangent, data), blank], axis=1)
    cot_far = jnp.concatenate([columns(cotangent, 1 - data), blank], axis=1)
    by_dp = swap(join([tok_far, cot_far]), ("dp",))
    block = join([in_order(data, tok_own, by_dp[:rows]), in_order(data, cot_own, by_dp[rows:])])
    block = gather(block, "z").reshape(depth, 2, 2 * rows, -1)

    gate_up = jnp.concatenate([expert_gate, expert_up], axis=0)
    gate_up_x = swap(gate_up, ("xlo",))
    gate_up_c = swap(gate_up, ("core",))
    down = expert_down[0]
    down_c = swap(down, ("core",))
    down_x = swap(lax.optimization_barrier((down, gate_up_x))[0], ("xlo",))
    gate_up_b = swap(gate_up_x, ("core",))
    down_b = swap(down_x, ("core",))

    units = -(-5 * hidden // 128) * 128
    expert_units = 4 * hidden

    def pack(mine, by_core, by_x, by_both, dense):
        return stack_rows([mine, by_core, by_x, by_both, columns(dense, data)], units)

    gate, up = (
        pack(gate_up[at], gate_up_c[at], gate_up_x[at], gate_up_b[at], dense)
        for at, dense in ((0, dense_gate), (1, dense_up))
    )
    down = pack(down, down_c, down_x, down_b, dense_down)

    tok = gather(block[:, 0].reshape(-1, block.shape[3]), "y").reshape(-1, block.shape[3])
    cot = gather(block[:, 1, :, :width].reshape(-1, width), "y").reshape(-1, width)

    weighting = tok[:, width:].astype(F32)
    tok = tok[:, :width]
    expert_id = near * lax.axis_size("core") + core
    unit = jnp.arange(units, dtype=jnp.int32)[None]
    scale = jnp.ones((), F32)
    for at, other in enumerate((core, 1 - core, core, 1 - core)):
        place = (near if at < 2 else 1 - near) * 2 + other
        column = jnp.sum(jnp.where(ids[None] == place, weighting, 0.0), axis=1, keepdims=True)
        scale = jnp.where((unit >= at * hidden) & (unit < (at + 1) * hidden), column, scale)

    def over_width(left, right):
        part = dot(left, right, ((1,), (1,))).astype(BF)
        return part.astype(F32) + swap(part, ("dp",)).astype(F32)

    pre, lin = over_width(tok, gate), over_width(tok, up)
    sig = jax.nn.sigmoid(pre)
    act = (pre * sig * lin * scale).astype(BF)
    dact = over_width(cot, down) * scale
    gate_grad = (dact * lin * (sig * (1.0 + pre * (1.0 - sig)))).astype(BF)
    lin_grad = (dact * (pre * sig)).astype(BF)

    def far_grads(left, right):
        term = dot(left[:, :expert_units], right, ((0,), (0,))).astype(BF)
        mine, by_core, by_x, by_both = [term[i * hidden:(i + 1) * hidden] for i in range(4)]
        landed = swap(jnp.stack([by_core, by_both]), ("core",)).astype(F32)
        return mine.astype(F32) + landed[0], (by_x.astype(F32) + landed[1]).astype(BF)

    def whole_grad(near_part, far_part):
        return (near_part + swap(far_part, ("xlo",)).astype(F32)).astype(BF)[None]

    mixed = scatter(dot(act, down, ((1,), (0,))).astype(BF), "y").astype(BF)
    grads = (dot(gate_grad, gate, ((1,), (0,))) + dot(lin_grad, up, ((1,), (0,)))).astype(BF)
    down_near, down_far = far_grads(act, cot)
    grads, down_far = lax.optimization_barrier((grads, down_far))
    grad_down = whole_grad(down_near, down_far)
    grads = scatter(grads, "y").astype(BF)
    gate_near, gate_far = far_grads(gate_grad, tok)
    up_near, up_far = far_grads(lin_grad, tok)
    both = jnp.concatenate([mixed.reshape(depth, -1, width), grads.reshape(depth, -1, width)], axis=1)
    both, gate_far, up_far, grad_down = lax.optimization_barrier((both, gate_far, up_far, grad_down))
    grad_gate, grad_up = whole_grad(gate_near, gate_far), whole_grad(up_near, up_far)
    both = scatter(both.reshape(-1, width), "z")
    mixed, grads = finish(both[:2 * rows], data), finish(both[2 * rows:], data)
    return (mixed, grads, grad_gate, grad_up, grad_down)


def solution(mesh):
    fine = Mesh(mesh.devices.reshape(2, 2, 2, 8, 4), ("dp", "xlo", "core", "z", "y"))
    every = ("dp", "xlo", "core", "z", "y")
    row = P(every, None)
    dense = P(("z", "y"), None)
    expert = P(("xlo", "core"), ("z", "y"), "dp")
    return jax.shard_map(
        per_device,
        mesh=fine,
        in_specs=(row, row, row, row, dense, dense, dense, expert, expert, expert),
        out_specs=(row, row, expert, expert, expert),
        check_vma=False,
    )
```

time: 348 us -> 283 us (0.81)
  blocking collectives: 49.3 us -> 0 us
  waiting for transfers between devices: 99.5 us -> 129 us
  local copies, waits for them, and re-layouts: 54.2 us -> 32.7 us
  starting transfers between devices: 72.7 us -> 54.4 us
  matrix products: 43.3 us -> 27 us
  other arithmetic: 25 us -> 37.8 us
    ppermute x17 -> x18, waiting for transfers between devices: 20.1 us -> 111 us  [swap(): return lax.ppermute(value, axes, [(i, size - 1 - i) for i in range(size)])]
    all_to_all x2 -> x0, blocking collectives: 49.3 us -> none  [gather(): lax.all_to_all(wide, axis, 0, 0, tiled=True).reshape(-1, block.shape[1])]
    all_to_all x5 -> x3, waiting for transfers between devices: 42.2 us -> 3.34 us  [scatter(): lax.all_to_all(part.reshape(size, -1, part.shape[1]), axis, 0, 0, tiled=T...]
    concatenate x1 -> x2, local copies, waits for them, and re-layouts: 31.9 us -> 1.16 us  [the longest x1 1.14 us: per_device(): gate_up = jnp.concatenate([expert_gate, expert_up], axis=0)]
    all_to_all x3, waiting for transfers between devices: 37.1 us -> 14.7 us  [gather(): return lax.all_to_all(wide, axis, 0, 0, tiled=True)]
    convert_element_type x2 -> x7, other arithmetic: 0.62 us -> 17.5 us  [the longest x3 8.28 us: far_grads(): (by_x.astype(F32) + landed[1]).astype(BF)]
    dot_general x14 -> x9, matrix products: 43.3 us -> 27 us  [dot(): lax.dot_general(left, right, (dims, ((), ())), preferred_element_type=F32)]
    unnamed x42 -> x67, local copies, waits for them, and re-layouts: 1.04 us -> 11.5 us
  transfers between devices with their start and end apart: 25 -> 24, of which waited for: 12 -> 11; matrix products, arithmetic and copies ran while one was open for 34% -> 26% of each run, Pallas kernels for 0% -> 0%
where the time goes in v1:
time: 283 us; the launch traced here: 282 us
  waiting for transfers between devices  129 us (46%)
  starting transfers between devices  54.4 us (19%)
  other arithmetic  37.8 us (13%)
  local copies, waits for them, and re-layouts  32.7 us (12%)
  matrix products  27 us (10%)
    ppermute x18, waiting for transfers between devices, swap(): return lax.ppermute(value, axes, [(i, size - 1 - i) for i in range(size)])  111 us
    dot_general x9, matrix products, dot(): lax.dot_general(left, right, (dims, ((), ())), preferred_element_type=F32)  27 us
    all_to_all x3, starting transfers between devices, scatter(): lax.all_to_all(part.reshape(size, -1, part.shape[1]), axis, 0, 0, tiled=T...  19.3 us
    all_to_all x3, starting transfers between devices, gather(): return lax.all_to_all(wide, axis, 0, 0, tiled=True)  18.3 us
    ppermute x18, starting transfers between devices, swap(): return lax.ppermute(value, axes, [(i, size - 1 - i) for i in range(size)])  16.8 us
    all_to_all x3, waiting for transfers between devices, gather(): return lax.all_to_all(wide, axis, 0, 0, tiled=True)  14.7 us
    unnamed x67, local copies, waits for them, and re-layouts  11.5 us
    broadcast_in_dim x3, other arithmetic, whole_grad(): return (near_part + swap(far_part, ('xlo',)).astype(F32)).astype(BF)[None]  8.98 us
  transfers between devices with their start and end apart: 24, of which 11 were waited for; matrix products, arithmetic and copies ran while one was open for 26% of the time, Pallas kernels for 0%

profile of v1, /device:TPU:8, one launch (start us, length us, event | category | flops | bytes accessed | tf_op | source)
XLA Modules:
  0.0 281.6 jit_solution(6683983842574661689)
XLA Ops:
  3.2 3.1 %collective-permute-start = (bf16[8,3712]{1,0:T(8,128)(2,1)S(1)}, bf16[8,3712]{1,0:T(8,128)(2,1)S(1)}, u32[]{:S(2)}, u32[]{:S(2)}) collective-permute-start(bf16[8,3712]{1,0:T(8,128)(2,1)S(1)} %fusion.36), channel_id=1, source_target_pairs={{0,128},{128,0},{1,129},{129,1},{2,130},{130,2},{3,131},{131,3},{4... | collective-permute-start | bytes 178184 | tf_op jit(solution)/shard_map/ppermute | solution.py:14
  11.6 8.5 %all-to-all-start = ((bf16[8,16,3712]{2,1,0:T(8,128)(2,1)}), bf16[8,16,3712]{2,1,0:T(8,128)(2,1)S(1)}, u32[]{:S(2)}, u32[]{:S(2)}) async-start(bf16[8,16,3712]{2,1,0:T(8,128)(2,1)} %broadcast_in_dim.140), calls=%async_computation | async-start | bytes 1900544 | tf_op jit(solution)/shard_map/all_to_all | solution.py:30
  24.7 34.2 %collective-permute-done.2 = bf16[2,152,3584]{2,1,0:T(8,128)(2,1)} collective-permute-done((bf16[2,152,3584]{2,1,0:T(8,128)(2,1)}, bf16[2,152,3584]{2,1,0:T(8,128)(2,1)}, u32[]{:S(2)}, u32[]{:S(2)}) %collective-permute-start.2) | collective-permute-done | bytes 2179104 | tf_op jit(solution)/shard_map/ppermute | solution.py:14
  60.9 4.9 %all-to-all-start.3 = ((bf16[4,64,3584]{2,1,0:T(8,128)(2,1)}), bf16[4,64,3584]{2,1,0:T(8,128)(2,1)S(1)}, u32[]{:S(2)}, u32[]{:S(2)}) async-start(bf16[4,64,3584]{2,1,0:T(8,128)(2,1)} %broadcast_in_dim.157), calls=%async_computation.3 | async-start | bytes 3670016 | tf_op jit(solution)/shard_map/all_to_all | solution.py:30
  66.7 17.2 %collective-permute-done.7 = bf16[152,3584]{1,0:T(8,128)(2,1)} collective-permute-done((bf16[152,3584]{1,0:T(8,128)(2,1)}, bf16[152,3584]{1,0:T(8,128)(2,1)}, u32[]{:S(2)}, u32[]{:S(2)}) %collective-permute-start.7) | collective-permute-done | bytes 1089568 | tf_op jit(solution)/shard_map/ppermute | solution.py:14
  91.9 4.9 %all-to-all-start.1 = ((bf16[4,64,3712]{2,1,0:T(8,128)(2,1)}), bf16[4,64,3712]{2,1,0:T(8,128)(2,1)S(1)}, u32[]{:S(2)}, u32[]{:S(2)}) async-start(bf16[4,64,3712]{2,1,0:T(8,128)(2,1)} %broadcast_in_dim.142), calls=%async_computation.1 | async-start | bytes 3801088 | tf_op jit(solution)/shard_map/all_to_all | solution.py:30
  96.8 4.5 %convolution_convert_fusion.4 = bf16[256,768]{1,0:T(8,128)(2,1)} fusion(bf16[256,3584]{1,0:T(8,128)(2,1)} %bitcast.104, bf16[152,3584]{1,0:T(8,128)(2,1)S(1)} %copy-done.14, bf16[152,3584]{1,0:T(8,128)(2,1)} %collective-permute-done.8, bf16[152,3584]{1,0:T(8,128)(2,1)} %collective-permute-done.7, bf16[152,3584]{1,0:T(8,128)(2,1)} %collective-permute-done.6, ...), kind=kOutput, calls=%fused_computation.34 | convolution fusion | flops 1437007872 | bytes 7675904 | tf_op jit(solution)/shard_map/dot_general | solution.py:56
  105.5 14.7 %all-to-all-done.1 = bf16[4,64,3712]{2,1,0:T(8,128)(2,1)S(1)} async-done(((bf16[4,64,3712]{2,1,0:T(8,128)(2,1)}), bf16[4,64,3712]{2,1,0:T(8,128)(2,1)S(1)}, u32[]{:S(2)}, u32[]{:S(2)}) %all-to-all-start.1) | async-done | bytes 1900576 | tf_op jit(solution)/shard_map/all_to_all | solution.py:30
  120.3 4.8 %convolution_convert_fusion.6 = bf16[256,768]{1,0:T(8,128)(2,1)S(1)} fusion(bf16[256,3712]{1,0:T(8,128)(2,1)S(1)} %bitcast.99, bf16[152,3584]{1,0:T(8,128)(2,1)S(1)} %copy-done.10, bf16[152,3584]{1,0:T(8,128)(2,1)} %get-tuple-element.34, bf16[152,3584]{1,0:T(8,128)(2,1)} %get-tuple-element.32, bf16[152,3584]{1,0:T(8,128)(2,1)} %get-tuple-element.30, ...), kind=kOutput, calls=%fused_computation.36 | convolution fusion | flops 1437007872 | bytes 7675904 | tf_op jit(solution)/shard_map/dot_general | solution.py:56
  130.8 7.9 %collective-permute-done.4 = bf16[256,768]{1,0:T(8,128)(2,1)S(1)} collective-permute-done((bf16[256,768]{1,0:T(8,128)(2,1)S(1)}, bf16[256,768]{1,0:T(8,128)(2,1)S(1)}, u32[]{:S(2)}, u32[]{:S(2)}) %collective-permute-start.4) | collective-permute-done | bytes 393248 | tf_op jit(solution)/shard_map/ppermute | solution.py:14
  138.7 6.8 %collective-permute-done.5 = bf16[256,768]{1,0:T(8,128)(2,1)S(1)} collective-permute-done((bf16[256,768]{1,0:T(8,128)(2,1)S(1)}, bf16[256,768]{1,0:T(8,128)(2,1)S(1)}, u32[]{:S(2)}, u32[]{:S(2)}) %collective-permute-start.5) | collective-permute-done | bytes 393248 | tf_op jit(solution)/shard_map/ppermute | solution.py:14
  148.2 3.4 %convolution_convert_fusion.2 = bf16[608,3584]{1,0:T(8,128)(2,1)} fusion(bf16[256,3584]{1,0:T(8,128)(2,1)S(1)} %bitcast.105, bf16[256,768]{1,0:T(8,128)(2,1)S(1)} %get-tuple-element.35), kind=kOutput, calls=%fused_computation.2 | convolution fusion | flops 1117863936 | bytes 6520832 | tf_op jit(solution)/shard_map/dot_general | solution.py:56
  151.6 4.3 %convolution_convert_fusion.3 = bf16[256,3584]{1,0:T(8,128)(2,1)} fusion(bf16[256,768]{1,0:T(8,128)(2,1)S(1)} %get-tuple-element.35, bf16[152,3584]{1,0:T(8,128)(2,1)S(1)} %copy-done.15, bf16[152,3584]{1,0:T(8,128)(2,1)} %collective-permute-done.8, bf16[152,3584]{1,0:T(8,128)(2,1)} %collective-permute-done.7, bf16[152,3584]{1,0:T(8,128)(2,1)} %collective-permute-done.6, ...), kind=kOutput, calls=%fused_computation.8 | convolution fusion | flops 1437728768 | bytes 7675904 | tf_op jit(solution)/shard_map/dot_general | solution.py:56
  155.9 5.8 %all-to-all-start.2 = ((bf16[4,64,3584]{2,1,0:T(8,128)(2,1)}), bf16[4,64,3584]{2,1,0:T(8,128)(2,1)}, u32[]{:S(2)}, u32[]{:S(2)}) async-start(bf16[4,64,3584]{2,1,0:T(8,128)(2,1)} %bitcast.110), calls=%async_computation.2 | async-start | bytes 3670016 | tf_op jit(solution)/shard_map/all_to_all | solution.py:19
  178.1 3.4 %fusion = bf16[256,3584]{1,0:T(8,128)(2,1)} fusion(f32[256,3584]{1,0:T(8,128)S(1)} %fusion.40, bf16[256,768]{1,0:T(8,128)(2,1)S(1)} %get-tuple-element.36, bf16[152,3584]{1,0:T(8,128)(2,1)S(1)} %copy-done.11, bf16[152,3584]{1,0:T(8,128)(2,1)S(1)} %copy-done.26, bf16[152,3584]{1,0:T(8,128)(2,1)S(1)} %copy-done.20, bf16[152,3584]{1,0:T(8,128)(2,1)S(1)} %copy-done.21, ...), kind=kOutput, calls=%fused_computation.7 | convolution fusion | flops 1438646272 | bytes 11345920 | tf_op jit(solution)/shard_map/dot_general | solution.py:56
  191.3 5.0 %all-to-all-start.4 = ((bf16[4,64,3584]{2,1,0:T(8,128)(2,1)}), bf16[4,64,3584]{2,1,0:T(8,128)(2,1)S(1)}, u32[]{:S(2)}, u32[]{:S(2)}) async-start(bf16[4,64,3584]{2,1,0:T(8,128)(2,1)} %bitcast.111), calls=%async_computation.4 | async-start | bytes 3670016 | tf_op jit(solution)/shard_map/all_to_all | solution.py:19
  199.0 3.4 %fusion.13 = bf16[152,3584]{1,0:T(8,128)(2,1)} fusion(f32[2,152,3584]{2,1,0:T(8,128)S(1)} %convert_element_type.150, bf16[608,3584]{1,0:T(8,128)(2,1)} %copy-done.3), kind=kLoop, calls=%fused_computation.26 | loop fusion | flops 1634304 | bytes 4358144 | tf_op jit(solution)/shard_map/convert_element_type | solution.py:134
  209.2 11.8 %collective-permute-done.13 = bf16[152,3584]{1,0:T(8,128)(2,1)S(1)} collective-permute-done((bf16[152,3584]{1,0:T(8,128)(2,1)}, bf16[152,3584]{1,0:T(8,128)(2,1)S(1)}, u32[]{:S(2)}, u32[]{:S(2)}) %collective-permute-start.13) | collective-permute-done | bytes 1089568 | tf_op jit(solution)/shard_map/ppermute | solution.py:14
  225.6 8.5 %all-to-all-start.5 = ((bf16[8,16,3584]{2,1,0:T(8,128)(2,1)}), bf16[8,16,3584]{2,1,0:T(8,128)(2,1)S(1)}, u32[]{:S(2)}, u32[]{:S(2)}) async-start(bf16[8,16,3584]{2,1,0:T(8,128)(2,1)} %pad_maximum_fusion.3), calls=%async_computation.5 | async-start | bytes 1835008 | tf_op jit(solution)/shard_map/all_to_all | solution.py:19
  235.5 16.7 %collective-permute-done.16 = bf16[152,3584]{1,0:T(8,128)(2,1)S(1)} collective-permute-done((bf16[152,3584]{1,0:T(8,128)(2,1)}, bf16[152,3584]{1,0:T(8,128)(2,1)S(1)}, u32[]{:S(2)}, u32[]{:S(2)}) %collective-permute-start.16) | collective-permute-done | bytes 1089568 | tf_op jit(solution)/shard_map/ppermute | solution.py:14
  252.1 3.2 %fusion.21 = bf16[1,152,3584]{2,1,0:T(8,128)(2,1)} fusion(bf16[152,3584]{1,0:T(8,128)(2,1)S(1)} %collective-permute-done.16, f32[2,152,3584]{2,1,0:T(8,128)} %copy-done.5, bf16[608,3584]{1,0:T(8,128)(2,1)} %copy-done.3), kind=kLoop, calls=%fused_computation.42 | loop fusion | flops 2723840 | bytes 5447680 | tf_op jit(solution)/shard_map/broadcast_in_dim | solution.py:137
  259.8 12.6 %collective-permute-done.17 = bf16[152,3584]{1,0:T(8,128)(2,1)S(1)} collective-permute-done((bf16[152,3584]{1,0:T(8,128)(2,1)}, bf16[152,3584]{1,0:T(8,128)(2,1)S(1)}, u32[]{:S(2)}, u32[]{:S(2)}) %collective-permute-start.17) | collective-permute-done | bytes 1089568 | tf_op jit(solution)/shard_map/ppermute | solution.py:14
  272.4 3.2 %fusion.22 = bf16[1,152,3584]{2,1,0:T(8,128)(2,1)} fusion(bf16[152,3584]{1,0:T(8,128)(2,1)S(1)} %collective-permute-done.17, f32[2,152,3584]{2,1,0:T(8,128)} %copy-done.4, bf16[608,3584]{1,0:T(8,128)(2,1)} %copy-done.2), kind=kLoop, calls=%fused_computation.43 | loop fusion | flops 2723840 | bytes 5447680 | tf_op jit(solution)/shard_map/broadcast_in_dim | solution.py:137
  277.4 3.5 %collective-permute-done.14 = bf16[4,3584]{1,0:T(4,128)(2,1)S(1)} collective-permute-done((bf16[4,3584]{1,0:T(4,128)(2,1)S(1)}, bf16[4,3584]{1,0:T(4,128)(2,1)S(1)}, u32[]{:S(2)}, u32[]{:S(2)}) %collective-permute-start.14) | collective-permute-done | bytes 28704 | tf_op jit(solution)/shard_map/ppermute | solution.py:14
  (150 shorter events, 84.3 us)
Async XLA Ops:
  3.2 7.2 %collective-permute-start = (bf16[8,3712]{1,0:T(8,128)(2,1)S(1)}, bf16[8,3712]{1,0:T(8,128)(2,1)S(1)}, u32[]{:S(2)}, u32[]{:S(2)}) collective-permute-start(bf16[8,3712]{1,0:T(8,128)(2,1)S(1)} %fusion.36), channel_id=1, source_target_pairs={{0,128},{128,0},{1,129},{129,1},{2,130},{130,2},{3,131},{131,3},{4... | collective-permute-start | bytes 178184 | tf_op jit(solution)/shard_map/ppermute | solution.py:14
  9.8 49.2 %collective-permute-start.2 = (bf16[2,152,3584]{2,1,0:T(8,128)(2,1)}, bf16[2,152,3584]{2,1,0:T(8,128)(2,1)}, u32[]{:S(2)}, u32[]{:S(2)}) collective-permute-start(bf16[2,152,3584]{2,1,0:T(8,128)(2,1)} %constant_dynamic-update-slice_fusion), channel_id=1, source_target_pairs={{0,64},{64,0},{1,65},{65,1},{2,66},{66,2},{3,67},{67,3},{4,68},{68... | collective-permute-start | bytes 6537224 | tf_op jit(solution)/shard_map/ppermute | solution.py:14
  11.6 48.0 %all-to-all-start = ((bf16[8,16,3712]{2,1,0:T(8,128)(2,1)}), bf16[8,16,3712]{2,1,0:T(8,128)(2,1)S(1)}, u32[]{:S(2)}, u32[]{:S(2)}) async-start(bf16[8,16,3712]{2,1,0:T(8,128)(2,1)} %broadcast_in_dim.140), calls=%async_computation | async-start | bytes 1900544 | tf_op jit(solution)/shard_map/all_to_all | solution.py:30
  20.0 66.9 %collective-permute-start.1 = (bf16[2,152,3584]{2,1,0:T(8,128)(2,1)}, bf16[2,152,3584]{2,1,0:T(8,128)(2,1)}, u32[]{:S(2)}, u32[]{:S(2)}) collective-permute-start(bf16[2,152,3584]{2,1,0:T(8,128)(2,1)} %constant_dynamic-update-slice_fusion), channel_id=1, source_target_pairs={{0,32},{32,0},{1,33},{33,1},{2,34},{34,2},{3,35},{35,3},{4,36},{36... | collective-permute-start | bytes 6537224 | tf_op jit(solution)/shard_map/ppermute | solution.py:14
  20.1 76.8 %collective-permute-start.6 = (bf16[152,3584]{1,0:T(8,128)(2,1)}, bf16[152,3584]{1,0:T(8,128)(2,1)}, u32[]{:S(2)}, u32[]{:S(2)}) collective-permute-start(bf16[152,3584]{1,0:T(8,128)(2,1)} %bitcast.11), channel_id=1, source_target_pairs={{0,32},{32,0},{1,33},{33,1},{2,34},{34,2},{3,35},{35,3},{4,36},{36... | collective-permute-start | bytes 3268616 | tf_op jit(solution)/shard_map/ppermute | solution.py:14
  58.9 24.9 %collective-permute-start.7 = (bf16[152,3584]{1,0:T(8,128)(2,1)}, bf16[152,3584]{1,0:T(8,128)(2,1)}, u32[]{:S(2)}, u32[]{:S(2)}) collective-permute-start(bf16[152,3584]{1,0:T(8,128)(2,1)} %bitcast.11), channel_id=1, source_target_pairs={{0,64},{64,0},{1,65},{65,1},{2,66},{66,2},{3,67},{67,3},{4,68},{68... | collective-permute-start | bytes 3268616 | tf_op jit(solution)/shard_map/ppermute | solution.py:14
  60.9 29.1 %all-to-all-start.3 = ((bf16[4,64,3584]{2,1,0:T(8,128)(2,1)}), bf16[4,64,3584]{2,1,0:T(8,128)(2,1)S(1)}, u32[]{:S(2)}, u32[]{:S(2)}) async-start(bf16[4,64,3584]{2,1,0:T(8,128)(2,1)} %broadcast_in_dim.157), calls=%async_computation.3 | async-start | bytes 3670016 | tf_op jit(solution)/shard_map/all_to_all | solution.py:30
  66.7 35.8 %collective-permute-start.3 = (bf16[2,152,3584]{2,1,0:T(8,128)(2,1)}, bf16[2,152,3584]{2,1,0:T(8,128)(2,1)}, u32[]{:S(2)}, u32[]{:S(2)}) collective-permute-start(bf16[2,152,3584]{2,1,0:T(8,128)(2,1)} %collective-permute-done.2), channel_id=1, source_target_pairs={{0,32},{32,0},{1,33},{33,1},{2,34},{34,2},{3,35},{35,3},{4,36},{36... | collective-permute-start | bytes 6537224 | tf_op jit(solution)/shard_map/ppermute | solution.py:14
  83.8 13.0 %collective-permute-start.8 = (bf16[152,3584]{1,0:T(8,128)(2,1)}, bf16[152,3584]{1,0:T(8,128)(2,1)}, u32[]{:S(2)}, u32[]{:S(2)}) collective-permute-start(bf16[152,3584]{1,0:T(8,128)(2,1)} %collective-permute-done.7), channel_id=1, source_target_pairs={{0,32},{32,0},{1,33},{33,1},{2,34},{34,2},{3,35},{35,3},{4,36},{36... | collective-permute-start | bytes 3268616 | tf_op jit(solution)/shard_map/ppermute | solution.py:14
  91.9 28.3 %all-to-all-start.1 = ((bf16[4,64,3712]{2,1,0:T(8,128)(2,1)}), bf16[4,64,3712]{2,1,0:T(8,128)(2,1)S(1)}, u32[]{:S(2)}, u32[]{:S(2)}) async-start(bf16[4,64,3712]{2,1,0:T(8,128)(2,1)} %broadcast_in_dim.142), calls=%async_computation.1 | async-start | bytes 3801088 | tf_op jit(solution)/shard_map/all_to_all | solution.py:30
  101.3 29.5 %collective-permute-start.9 = (bf16[256,768]{1,0:T(8,128)(2,1)}, bf16[256,768]{1,0:T(8,128)(2,1)}, u32[]{:S(2)}, u32[]{:S(2)}) collective-permute-start(bf16[256,768]{1,0:T(8,128)(2,1)} %convolution_convert_fusion.4), channel_id=1, source_target_pairs={{0,128},{128,0},{1,129},{129,1},{2,130},{130,2},{3,131},{131,3},{4... | collective-permute-start | bytes 1179656 | tf_op jit(solution)/shard_map/ppermute | solution.py:14
  125.1 13.6 %collective-permute-start.4 = (bf16[256,768]{1,0:T(8,128)(2,1)S(1)}, bf16[256,768]{1,0:T(8,128)(2,1)S(1)}, u32[]{:S(2)}, u32[]{:S(2)}) collective-permute-start(bf16[256,768]{1,0:T(8,128)(2,1)S(1)} %convolution_convert_fusion.6), channel_id=1, source_target_pairs={{0,128},{128,0},{1,129},{129,1},{2,130},{130,2},{3,131},{131,3},{4... | collective-permute-start | bytes 1179656 | tf_op jit(solution)/shard_map/ppermute | solution.py:14
  128.0 17.5 %collective-permute-start.5 = (bf16[256,768]{1,0:T(8,128)(2,1)S(1)}, bf16[256,768]{1,0:T(8,128)(2,1)S(1)}, u32[]{:S(2)}, u32[]{:S(2)}) collective-permute-start(bf16[256,768]{1,0:T(8,128)(2,1)S(1)} %convolution_convert_fusion.5), channel_id=1, source_target_pairs={{0,128},{128,0},{1,129},{129,1},{2,130},{130,2},{3,131},{131,3},{4... | collective-permute-start | bytes 1179656 | tf_op jit(solution)/shard_map/ppermute | solution.py:14
  155.9 26.9 %all-to-all-start.2 = ((bf16[4,64,3584]{2,1,0:T(8,128)(2,1)}), bf16[4,64,3584]{2,1,0:T(8,128)(2,1)}, u32[]{:S(2)}, u32[]{:S(2)}) async-start(bf16[4,64,3584]{2,1,0:T(8,128)(2,1)} %bitcast.110), calls=%async_computation.2 | async-start | bytes 3670016 | tf_op jit(solution)/shard_map/all_to_all | solution.py:19
  165.0 19.7 %collective-permute-start.10 = (bf16[2,152,3584]{2,1,0:T(8,128)(2,1)}, bf16[2,152,3584]{2,1,0:T(8,128)(2,1)}, u32[]{:S(2)}, u32[]{:S(2)}) collective-permute-start(bf16[2,152,3584]{2,1,0:T(8,128)(2,1)} %pad_maximum_fusion), channel_id=1, source_target_pairs={{0,32},{32,0},{1,33},{33,1},{2,34},{34,2},{3,35},{35,3},{4,36},{36... | collective-permute-start | bytes 6537224 | tf_op jit(solution)/shard_map/ppermute | solution.py:14
  171.2 25.6 %collective-permute-start.11 = (bf16[2,152,3584]{2,1,0:T(8,128)(2,1)}, bf16[2,152,3584]{2,1,0:T(8,128)(2,1)}, u32[]{:S(2)}, u32[]{:S(2)}) collective-permute-start(bf16[2,152,3584]{2,1,0:T(8,128)(2,1)} %pad_maximum_fusion.1), channel_id=1, source_target_pairs={{0,32},{32,0},{1,33},{33,1},{2,34},{34,2},{3,35},{35,3},{4,36},{36... | collective-permute-start | bytes 6537224 | tf_op jit(solution)/shard_map/ppermute | solution.py:14
  176.7 25.8 %collective-permute-start.12 = (bf16[2,152,3584]{2,1,0:T(8,128)(2,1)}, bf16[2,152,3584]{2,1,0:T(8,128)(2,1)}, u32[]{:S(2)}, u32[]{:S(2)}) collective-permute-start(bf16[2,152,3584]{2,1,0:T(8,128)(2,1)} %pad_maximum_fusion.2), channel_id=1, source_target_pairs={{0,32},{32,0},{1,33},{33,1},{2,34},{34,2},{3,35},{35,3},{4,36},{36... | collective-permute-start | bytes 6537224 | tf_op jit(solution)/shard_map/ppermute | solution.py:14
  191.3 32.3 %all-to-all-start.4 = ((bf16[4,64,3584]{2,1,0:T(8,128)(2,1)}), bf16[4,64,3584]{2,1,0:T(8,128)(2,1)S(1)}, u32[]{:S(2)}, u32[]{:S(2)}) async-start(bf16[4,64,3584]{2,1,0:T(8,128)(2,1)} %bitcast.111), calls=%async_computation.4 | async-start | bytes 3670016 | tf_op jit(solution)/shard_map/all_to_all | solution.py:19
  196.3 24.7 %collective-permute-start.13 = (bf16[152,3584]{1,0:T(8,128)(2,1)}, bf16[152,3584]{1,0:T(8,128)(2,1)S(1)}, u32[]{:S(2)}, u32[]{:S(2)}) collective-permute-start(bf16[152,3584]{1,0:T(8,128)(2,1)} %fusion.15), channel_id=1, source_target_pairs={{0,64},{64,0},{1,65},{65,1},{2,66},{66,2},{3,67},{67,3},{4,68},{68... | collective-permute-start | bytes 3268616 | tf_op jit(solution)/shard_map/ppermute | solution.py:14
  225.0 27.2 %collective-permute-start.16 = (bf16[152,3584]{1,0:T(8,128)(2,1)}, bf16[152,3584]{1,0:T(8,128)(2,1)S(1)}, u32[]{:S(2)}, u32[]{:S(2)}) collective-permute-start(bf16[152,3584]{1,0:T(8,128)(2,1)} %fusion.13), channel_id=1, source_target_pairs={{0,64},{64,0},{1,65},{65,1},{2,66},{66,2},{3,67},{67,3},{4,68},{68... | collective-permute-start | bytes 3268616 | tf_op jit(solution)/shard_map/ppermute | solution.py:14
  225.6 31.9 %all-to-all-start.5 = ((bf16[8,16,3584]{2,1,0:T(8,128)(2,1)}), bf16[8,16,3584]{2,1,0:T(8,128)(2,1)S(1)}, u32[]{:S(2)}, u32[]{:S(2)}) async-start(bf16[8,16,3584]{2,1,0:T(8,128)(2,1)} %pad_maximum_fusion.3), calls=%async_computation.5 | async-start | bytes 1835008 | tf_op jit(solution)/shard_map/all_to_all | solution.py:19
  234.0 38.3 %collective-permute-start.17 = (bf16[152,3584]{1,0:T(8,128)(2,1)}, bf16[152,3584]{1,0:T(8,128)(2,1)S(1)}, u32[]{:S(2)}, u32[]{:S(2)}) collective-permute-start(bf16[152,3584]{1,0:T(8,128)(2,1)} %fusion.11), channel_id=1, source_target_pairs={{0,64},{64,0},{1,65},{65,1},{2,66},{66,2},{3,67},{67,3},{4,68},{68... | collective-permute-start | bytes 3268616 | tf_op jit(solution)/shard_map/ppermute | solution.py:14
  257.7 19.1 %collective-permute-start.15 = (bf16[4,3584]{1,0:T(4,128)(2,1)S(1)}, bf16[4,3584]{1,0:T(4,128)(2,1)S(1)}, u32[]{:S(2)}, u32[]{:S(2)}) collective-permute-start(bf16[4,3584]{1,0:T(4,128)(2,1)S(1)} %get-tuple-element.39), channel_id=1, source_target_pairs={{0,128},{128,0},{1,129},{129,1},{2,130},{130,2},{3,131},{131,3},{4... | collective-permute-start | bytes 86024 | tf_op jit(solution)/shard_map/ppermute | solution.py:14
  275.6 5.4 %collective-permute-start.14 = (bf16[4,3584]{1,0:T(4,128)(2,1)S(1)}, bf16[4,3584]{1,0:T(4,128)(2,1)S(1)}, u32[]{:S(2)}, u32[]{:S(2)}) collective-permute-start(bf16[4,3584]{1,0:T(4,128)(2,1)S(1)} %get-tuple-element.41), channel_id=1, source_target_pairs={{0,128},{128,0},{1,129},{129,1},{2,130},{130,2},{3,131},{131,3},{4... | collective-permute-start | bytes 86024 | tf_op jit(solution)/shard_map/ppermute | solution.py:14
  (33 other events, 220.4 us)

commit v2 on v1

v2 whole, which is shorter than its diff:
```python
import jax
import jax.numpy as jnp
from jax import lax
from jax.sharding import Mesh, PartitionSpec as P

BF = jnp.bfloat16
F32 = jnp.float32


def swap(value, axes):
    size = 1
    for axis in axes:
        size *= lax.axis_size(axis)
    return lax.ppermute(value, axes, [(i, size - 1 - i) for i in range(size)])


def scatter(part, axis):
    size = lax.axis_size(axis)
    landed = lax.all_to_all(part.reshape(size, -1, part.shape[1]), axis, 0, 0, tiled=True)
    return jnp.sum(landed.astype(F32), axis=0)


def gather(block, axis):
    size = lax.axis_size(axis)
    wide = jnp.broadcast_to(block[None], (size,) + block.shape)
    return lax.all_to_all(wide, axis, 0, 0, tiled=True)


def join(parts):
    return jnp.concatenate(parts, axis=0)


def stack_rows(parts, rows):
    total, start = None, 0
    for part in parts:
        here = lax.pad(part, jnp.zeros((), BF), ((start, rows - start - part.shape[0], 0), (0, 0, 0)))
        total = here if total is None else total + here
        start += part.shape[0]
    return total


def dot(left, right, dims):
    return lax.dot_general(left, right, (dims, ((), ())), preferred_element_type=F32)


def per_device(
    tokens, routes, route_gates, cotangent, dense_gate, dense_up, dense_down,
    expert_gate, expert_up, expert_down,
):
    width = expert_gate.shape[2]
    hidden = expert_gate.shape[1]
    data, near, core = (lax.axis_index(name) for name in ("dp", "xlo", "core"))
    rows = tokens.shape[0]
    halves, depth = lax.axis_size("dp"), lax.axis_size("z")

    gate_up = jnp.concatenate([expert_gate, expert_up], axis=0)
    gate_up_x = swap(gate_up, ("xlo",))
    gate_up_c = swap(gate_up, ("core",))
    down_x = swap(expert_down[0], ("xlo",))
    down_c = swap(expert_down[0], ("core",))

    def pack(mine, by_core, dense):
        dense = lax.dynamic_slice_in_dim(dense, data * width, width, axis=1)
        return stack_rows([mine, by_core, dense], 3 * hidden)

    gate_a = pack(expert_gate[0], gate_up_c[0], dense_gate)
    up_a = pack(expert_up[0], gate_up_c[1], dense_up)
    down_a = pack(expert_down[0], down_c, dense_down)

    ids = jnp.arange(128, dtype=jnp.int32)
    weights_of = jnp.sum(
        jnp.where(routes[:, :, None] == ids[None, None, :], route_gates.astype(F32)[:, :, None], 0.0), axis=1
    ).astype(BF)
    both = join([tokens, cotangent])
    marks = join([weights_of, jnp.zeros_like(weights_of)])
    both = jnp.stack([jnp.concatenate([both[:, i * width:(i + 1) * width], marks], axis=1) for i in range(halves)])
    wide = jnp.broadcast_to(both[:, None], (halves, depth) + both.shape[1:]).reshape((-1,) + both.shape[1:])
    block = lax.all_to_all(wide, ("dp", "z"), 0, 0, tiled=True)
    block, gate_a, up_a, down_a = lax.optimization_barrier((block, gate_a, up_a, down_a))

    tok = gather(block[:, :rows].reshape(-1, block.shape[2]), "y").reshape(-1, block.shape[2])
    tok, block, gate_up_x, down_x = lax.optimization_barrier((tok, block, gate_up_x, down_x))
    cot = gather(block[:, rows:, :width].reshape(-1, width), "y").reshape(-1, width)

    gate_up_b = swap(gate_up_x, ("core",))
    gate_b = stack_rows([gate_up_x[0], gate_up_b[0]], 2 * hidden)
    up_b = stack_rows([gate_up_x[1], gate_up_b[1]], 2 * hidden)
    down_b = stack_rows([down_x, swap(down_x, ("core",))], 2 * hidden)

    weighting = tok[:, width:].astype(F32)
    tok = tok[:, :width]

    def weight_column(chip, other):
        place = chip * lax.axis_size("core") + other
        return jnp.sum(jnp.where(ids[None] == place, weighting, 0.0), axis=1, keepdims=True)

    unit = jnp.arange(3 * hidden, dtype=jnp.int32)[None]
    scale_a = jnp.where(
        unit < hidden, weight_column(near, core), jnp.where(unit < 2 * hidden, weight_column(near, 1 - core), 1.0)
    )
    scale_b = jnp.where(
        unit[:, :2 * hidden] < hidden, weight_column(1 - near, core), weight_column(1 - near, 1 - core)
    )

    def over_width(left, right):
        part = dot(left, right, ((1,), (1,))).astype(BF)
        return part.astype(F32) + swap(part, ("dp",)).astype(F32)

    def forward(gate, up, scale):
        pre, lin = over_width(tok, gate), over_width(tok, up)
        return pre, lin, (jax.nn.silu(pre) * lin * scale).astype(BF)

    def backward(pre, lin, down, scale):
        dact = over_width(cot, down) * scale
        sig = jax.nn.sigmoid(pre)
        return (dact * lin * (sig * (1.0 + pre * (1.0 - sig)))).astype(BF), (dact * (pre * sig)).astype(BF)

    pre_a, lin_a, act_a = forward(gate_a, up_a, scale_a)
    pre_b, lin_b, act_b = forward(gate_b, up_b, scale_b)
    grad_a, lin_grad_a = backward(pre_a, lin_a, down_a, scale_a)
    grad_b, lin_grad_b = backward(pre_b, lin_b, down_b, scale_b)

    def times(*pairs):
        return sum(dot(left, right, ((1,), (0,))) for left, right in pairs).astype(BF)

    mixed = scatter(times((act_a, down_a), (act_b, down_b)), "y").astype(BF)
    grads = times((grad_a, gate_a), (lin_grad_a, up_a), (grad_b, gate_b), (lin_grad_b, up_b))

    def far_grads(left_a, left_b, right):
        ours = jnp.concatenate([left_a[:, :hidden], left_b[:, :hidden]], axis=1)
        theirs = jnp.concatenate([left_a[:, hidden:2 * hidden], left_b[:, hidden:]], axis=1)
        ours, theirs = [dot(left, right, ((0,), (0,))).astype(BF) for left in (ours, theirs)]
        theirs = swap(theirs, ("core",))
        return ours, theirs, (ours[hidden:].astype(F32) + theirs[hidden:].astype(F32)).astype(BF)

    def whole_grad(ours, theirs, far):
        far = swap(far, ("xlo",))
        return (ours[:hidden].astype(F32) + theirs[:hidden].astype(F32) + far.astype(F32)).astype(BF)[None]

    parts = [far_grads(act_a, act_b, cot), far_grads(grad_a, grad_b, tok), far_grads(lin_grad_a, lin_grad_b, tok)]
    grads, parts = lax.optimization_barrier((grads, parts))
    grad_down, grad_gate, grad_up = [whole_grad(*part) for part in parts]
    grads = scatter(grads, "y").astype(BF)
    both = jnp.concatenate([part.reshape(halves * depth, rows, width) for part in (mixed, grads)], axis=1)
    both = lax.all_to_all(both, ("dp", "z"), 0, 0, tiled=True).astype(F32)
    both = jnp.sum(both.reshape(halves, depth, 2 * rows, width), axis=1).astype(BF)
    both = jnp.concatenate([both[i] for i in range(halves)], axis=1)
    return (both[:rows], both[rows:], grad_gate, grad_up, grad_down)


def solution(mesh):
    fine = Mesh(mesh.devices.reshape(2, 2, 2, 8, 4), ("dp", "xlo", "core", "z", "y"))
    every = ("dp", "xlo", "core", "z", "y")
    row = P(every, None)
    dense = P(("z", "y"), None)
    expert = P(("xlo", "core"), ("z", "y"), "dp")
    return jax.shard_map(
        per_device,
        mesh=fine,
        in_specs=(row, row, row, row, dense, dense, dense, expert, expert, expert),
        out_specs=(row, row, expert, expert, expert),
        check_vma=False,
    )
```

time: 283 us -> 283 us (level)
  other arithmetic: 37.8 us -> 28.5 us
  matrix products: 27 us -> 35.2 us
  local copies, waits for them, and re-layouts: 32.7 us -> 27.8 us
  starting transfers between devices: 54.4 us -> 58.6 us
    all_to_all x0 -> x2, waiting for transfers between devices: none -> 36.3 us  [the longest x1 36.3 us: per_device(): block = lax.all_to_all(wide, ('dp', 'z'), 0, 0, tiled=True)]
    ppermute x18, waiting for transfers between devices: 111 us -> 84.1 us  [swap(): return lax.ppermute(value, axes, [(i, size - 1 - i) for i in range(size)])]
    all_to_all x0 -> x2, starting transfers between devices: none -> 20.6 us  [the longest x1 10.8 us: per_device(): block = lax.all_to_all(wide, ('dp', 'z'), 0, 0, tiled=True)]
    convert_element_type x9 -> x5, other arithmetic: 18.8 us -> 6.39 us  [the longest x3 4.48 us: far_grads(): (ours[hidden:].astype(F32) + theirs[hidden:].astype(F32)).astype(BF)]
    all_to_all x3 -> x2, starting transfers between devices: 18.3 us -> 9.71 us  [gather(): return lax.all_to_all(wide, axis, 0, 0, tiled=True)]
    all_to_all x3 -> x2, starting transfers between devices: 19.3 us -> 10.7 us  [scatter(): lax.all_to_all(part.reshape(size, -1, part.shape[1]), axis, 0, 0, tiled=T...]
    dot_general x9 -> x18, matrix products: 27 us -> 35.2 us  [dot(): lax.dot_general(left, right, (dims, ((), ())), preferred_element_type=F32)]
    add x0 -> x3, other arithmetic: none -> 6.72 us  [stack_rows(): total = here if total is None else total + here]
  transfers between devices with their start and end apart: 24 -> 24, of which waited for: 11 -> 9; matrix products, arithmetic and copies ran while one was open for 26% -> 25% of each run, Pallas kernels for 0% -> 0%
where the time goes in v2:
time: 283 us; the launch traced here: 282 us
  waiting for transfers between devices  130 us (46%)
  starting transfers between devices  58.6 us (21%)
  matrix products  35.2 us (12%)
  other arithmetic  28.5 us (10%)
  local copies, waits for them, and re-layouts  27.8 us (10%)
    ppermute x18, waiting for transfers between devices, swap(): return lax.ppermute(value, axes, [(i, size - 1 - i) for i in range(size)])  84.1 us
    all_to_all x1, waiting for transfers between devices, per_device(): block = lax.all_to_all(wide, ('dp', 'z'), 0, 0, tiled=True)  36.3 us
    dot_general x18, matrix products, dot(): lax.dot_general(left, right, (dims, ((), ())), preferred_element_type=F32)  35.2 us
    ppermute x18, starting transfers between devices, swap(): return lax.ppermute(value, axes, [(i, size - 1 - i) for i in range(size)])  17.5 us
    all_to_all x1, starting transfers between devices, per_device(): block = lax.all_to_all(wide, ('dp', 'z'), 0, 0, tiled=True)  10.8 us
    all_to_all x2, starting transfers between devices, scatter(): lax.all_to_all(part.reshape(size, -1, part.shape[1]), axis, 0, 0, tiled=T...  10.7 us
    all_to_all x2, waiting for transfers between devices, gather(): return lax.all_to_all(wide, axis, 0, 0, tiled=True)  9.88 us
    all_to_all x1, starting transfers between devices, per_device(): both = lax.all_to_all(both, ('dp', 'z'), 0, 0, tiled=True).astype(F32)  9.82 us
  transfers between devices with their start and end apart: 24, of which 9 were waited for; matrix products, arithmetic and copies ran while one was open for 25% of the time, Pallas kernels for 0%

profile of v2, /device:TPU:8, one launch (start us, length us, event | category | flops | bytes accessed | tf_op | source)
XLA Modules:
  0.0 281.6 jit_solution(3740366460952738912)
XLA Ops:
  7.5 10.8 %all-to-all-start = ((bf16[16,8,3712]{2,1,0:T(8,128)(2,1)}), bf16[16,8,3712]{2,1,0:T(8,128)(2,1)}, u32[]{:S(2)}, u32[]{:S(2)}) async-start(bf16[16,8,3712]{2,1,0:T(8,128)(2,1)} %bitcast.64), calls=%async_computation | async-start | bytes 1900544 | tf_op jit(solution)/shard_map/all_to_all | solution.py:78
  21.3 3.0 %pad_add_fusion = bf16[456,3584]{1,0:T(8,128)(2,1)} fusion(bf16[152,3584]{1,0:T(8,128)(2,1)S(1)} %get-tuple-element.75, bf16[152,3584]{1,0:T(8,128)(2,1)} %collective-permute-done.1, bf16[152,3584]{1,0:T(8,128)(2,1)} %bitcast.7), kind=kLoop, calls=%fused_computation.12 | loop fusion | flops 9805824 | bytes 6537216 | tf_op jit(solution)/shard_map/add | solution.py:37
  29.8 36.3 %all-to-all-done = bf16[16,8,3712]{2,1,0:T(8,128)(2,1)} async-done(((bf16[16,8,3712]{2,1,0:T(8,128)(2,1)}), bf16[16,8,3712]{2,1,0:T(8,128)(2,1)}, u32[]{:S(2)}, u32[]{:S(2)}) %all-to-all-start) | async-done | bytes 950304 | tf_op jit(solution)/shard_map/all_to_all | solution.py:78
  68.9 4.9 %all-to-all-start.1 = ((bf16[4,64,3712]{2,1,0:T(8,128)(2,1)}), bf16[4,64,3712]{2,1,0:T(8,128)(2,1)S(1)}, u32[]{:S(2)}, u32[]{:S(2)}) async-start(bf16[4,64,3712]{2,1,0:T(8,128)(2,1)} %broadcast_in_dim.148), calls=%async_computation.1 | async-start | bytes 3801088 | tf_op jit(solution)/shard_map/all_to_all | solution.py:26
  74.1 24.1 %collective-permute-done.3 = bf16[152,3584]{1,0:T(8,128)(2,1)} collective-permute-done((bf16[152,3584]{1,0:T(8,128)(2,1)}, bf16[152,3584]{1,0:T(8,128)(2,1)}, u32[]{:S(2)}, u32[]{:S(2)}) %collective-permute-start.3) | collective-permute-done | bytes 1089568 | tf_op jit(solution)/shard_map/ppermute | solution.py:14
  99.7 3.0 %convolution_convert_fusion.8 = bf16[256,456]{0,1:T(8,128)(2,1)S(1)} fusion(bf16[456,3584]{1,0:T(8,128)(2,1)} %pad_add_fusion.2, bf16[256,3712]{1,0:T(8,128)(2,1)S(1)} %bitcast.52), kind=kOutput, calls=%fused_computation.29 | convolution fusion | flops 836880384 | bytes 5337088 | tf_op jit(solution)/shard_map/dot_general | solution.py:43
  105.0 4.8 %all-to-all-start.3 = ((bf16[4,64,3584]{2,1,0:T(8,128)(2,1)}), bf16[4,64,3584]{2,1,0:T(8,128)(2,1)}, u32[]{:S(2)}, u32[]{:S(2)}) async-start(bf16[4,64,3584]{2,1,0:T(8,128)(2,1)} %broadcast_in_dim.163), calls=%async_computation.3 | async-start | bytes 3670016 | tf_op jit(solution)/shard_map/all_to_all | solution.py:26
  109.8 3.7 %convolution_convert_fusion.7 = bf16[256,456]{0,1:T(8,128)(2,1)} fusion(bf16[456,3584]{1,0:T(8,128)(2,1)} %pad_add_fusion.1, bf16[256,3712]{1,0:T(8,128)(2,1)S(1)} %bitcast.53), kind=kOutput, calls=%fused_computation.28 | convolution fusion | flops 836880384 | bytes 5337088 | tf_op jit(solution)/shard_map/dot_general | solution.py:43
  113.4 2.7 collective-permute-start.5
  119.5 9.9 %all-to-all-done.3 = bf16[4,64,3584]{2,1,0:T(8,128)(2,1)} async-done(((bf16[4,64,3584]{2,1,0:T(8,128)(2,1)}), bf16[4,64,3584]{2,1,0:T(8,128)(2,1)}, u32[]{:S(2)}, u32[]{:S(2)}) %all-to-all-start.3) | async-done | bytes 1835040 | tf_op jit(solution)/shard_map/all_to_all | solution.py:26
  129.4 3.5 %convolution_convert_fusion.6 = bf16[256,456]{0,1:T(8,128)(2,1)S(1)} fusion(bf16[256,3584]{1,0:T(8,128)(2,1)} %bitcast.14, bf16[456,3584]{1,0:T(8,128)(2,1)} %pad_add_fusion), kind=kOutput, calls=%fused_computation.27 | convolution fusion | flops 836880384 | bytes 5337088 | tf_op jit(solution)/shard_map/dot_general | solution.py:43
  132.9 2.8 collective-permute-start.10
  135.8 3.0 %fusion.5 = bf16[256,304]{0,1:T(8,128)(2,1)S(1)} fusion(bf16[256,3584]{1,0:T(8,128)(2,1)} %bitcast.14, bf16[152,3584]{1,0:T(8,128)(2,1)} %collective-permute-done.9, bf16[152,3584]{1,0:T(8,128)(2,1)} %collective-permute-done.3), kind=kOutput, calls=%fused_computation.30 | convolution fusion | flops 562278400 | bytes 4169728 | tf_op jit(solution)/shard_map/dot_general | solution.py:43
  149.0 3.0 %convolution_add_fusion = f32[256,3584]{1,0:T(8,128)} fusion(f32[256,3584]{1,0:T(8,128)S(1)} %fusion.70, bf16[256,456]{0,1:T(8,128)(2,1)S(1)} %get-tuple-element.53, bf16[456,3584]{1,0:T(8,128)(2,1)S(1)} %copy-done.8), kind=kOutput, calls=%fused_computation | convolution fusion | flops 837681152 | bytes 10842112 | tf_op jit(solution)/shard_map/dot_general | solution.py:43
  165.1 4.0 %fusion = bf16[256,3584]{1,0:T(8,128)(2,1)} fusion(f32[256,3584]{1,0:T(8,128)S(1)} %fusion.69, bf16[256,304]{0,1:T(8,128)(2,1)S(1)} %get-tuple-element.54, bf16[152,3584]{1,0:T(8,128)(2,1)} %collective-permute-done.9, bf16[152,3584]{1,0:T(8,128)(2,1)} %collective-permute-done.3), kind=kOutput, calls=%fused_computation.10 | convolution fusion | flops 564035584 | bytes 7839744 | tf_op jit(solution)/shard_map/dot_general | solution.py:43
  169.2 5.9 %all-to-all-start.2 = ((bf16[4,64,3584]{2,1,0:T(8,128)(2,1)}), bf16[4,64,3584]{2,1,0:T(8,128)(2,1)}, u32[]{:S(2)}, u32[]{:S(2)}) async-start(bf16[4,64,3584]{2,1,0:T(8,128)(2,1)} %bitcast.61), calls=%async_computation.2 | async-start | bytes 3670016 | tf_op jit(solution)/shard_map/all_to_all | solution.py:19
  196.2 4.8 %all-to-all-start.4 = ((bf16[4,64,3584]{2,1,0:T(8,128)(2,1)}), bf16[4,64,3584]{2,1,0:T(8,128)(2,1)}, u32[]{:S(2)}, u32[]{:S(2)}) async-start(bf16[4,64,3584]{2,1,0:T(8,128)(2,1)} %bitcast.15), calls=%async_computation.4 | async-start | bytes 3670016 | tf_op jit(solution)/shard_map/all_to_all | solution.py:19
  205.2 17.6 %collective-permute-done.15 = bf16[152,3584]{1,0:T(8,128)(2,1)} collective-permute-done((bf16[152,3584]{1,0:T(8,128)(2,1)}, bf16[152,3584]{1,0:T(8,128)(2,1)}, u32[]{:S(2)}, u32[]{:S(2)}) %collective-permute-start.15) | collective-permute-done | bytes 1089568 | tf_op jit(solution)/shard_map/ppermute | solution.py:14
  222.8 2.9 %fusion.8 = bf16[1,152,3584]{2,1,0:T(8,128)(2,1)} fusion(bf16[152,3584]{1,0:T(8,128)(2,1)} %collective-permute-done.15, bf16[304,3584]{1,0:T(8,128)(2,1)} %copy-done.22, bf16[304,3584]{1,0:T(8,128)(2,1)S(1)} %copy-done.6), kind=kLoop, calls=%fused_computation.33 | loop fusion | flops 3268608 | bytes 4358144 | tf_op jit(solution)/shard_map/broadcast_in_dim | solution.py:138
  229.0 9.8 %all-to-all-start.5 = ((bf16[16,8,3584]{2,1,0:T(8,128)(2,1)}), bf16[16,8,3584]{2,1,0:T(8,128)(2,1)S(1)}, u32[]{:S(2)}, u32[]{:S(2)}) async-start(bf16[16,8,3584]{2,1,0:T(8,128)(2,1)} %pad_maximum_fusion), calls=%async_computation.5 | async-start | bytes 1835008 | tf_op jit(solution)/shard_map/all_to_all | solution.py:145
  238.9 11.7 %collective-permute-done.16 = bf16[152,3584]{1,0:T(8,128)(2,1)} collective-permute-done((bf16[152,3584]{1,0:T(8,128)(2,1)}, bf16[152,3584]{1,0:T(8,128)(2,1)}, u32[]{:S(2)}, u32[]{:S(2)}) %collective-permute-start.16) | collective-permute-done | bytes 1089568 | tf_op jit(solution)/shard_map/ppermute | solution.py:14
  250.6 3.4 %fusion.9 = bf16[1,152,3584]{2,1,0:T(8,128)(2,1)} fusion(bf16[152,3584]{1,0:T(8,128)(2,1)} %collective-permute-done.16, bf16[304,3584]{1,0:T(8,128)(2,1)} %copy-done.21, bf16[304,3584]{1,0:T(8,128)(2,1)} %copy-done.4), kind=kLoop, calls=%fused_computation.34 | loop fusion | flops 3268608 | bytes 4358144 | tf_op jit(solution)/shard_map/broadcast_in_dim | solution.py:138
  254.0 24.1 %collective-permute-done.17 = bf16[152,3584]{1,0:T(8,128)(2,1)} collective-permute-done((bf16[152,3584]{1,0:T(8,128)(2,1)}, bf16[152,3584]{1,0:T(8,128)(2,1)}, u32[]{:S(2)}, u32[]{:S(2)}) %collective-permute-start.17) | collective-permute-done | bytes 1089568 | tf_op jit(solution)/shard_map/ppermute | solution.py:14
  278.1 2.7 fusion.10
  (161 shorter events, 77.8 us)
Async XLA Ops:
  4.3 93.9 %collective-permute-start.2 = (bf16[2,152,3584]{2,1,0:T(8,128)(2,1)}, bf16[2,152,3584]{2,1,0:T(8,128)(2,1)}, u32[]{:S(2)}, u32[]{:S(2)}) collective-permute-start(bf16[2,152,3584]{2,1,0:T(8,128)(2,1)} %constant_dynamic-update-slice_fusion), channel_id=1, source_target_pairs={{0,64},{64,0},{1,65},{65,1},{2,66},{66,2},{3,67},{67,3},{4,68},{68... | collective-permute-start | bytes 6537224 | tf_op jit(solution)/shard_map/ppermute | solution.py:14
  5.8 18.6 %collective-permute-start = (bf16[2,152,3584]{2,1,0:T(8,128)(2,1)}, bf16[2,152,3584]{2,1,0:T(8,128)(2,1)}, u32[]{:S(2)}, u32[]{:S(2)}) collective-permute-start(bf16[2,152,3584]{2,1,0:T(8,128)(2,1)} %constant_dynamic-update-slice_fusion), channel_id=1, source_target_pairs={{0,32},{32,0},{1,33},{33,1},{2,34},{34,2},{3,35},{35,3},{4,36},{36... | collective-permute-start | bytes 6537224 | tf_op jit(solution)/shard_map/ppermute | solution.py:14
  5.8 15.5 %collective-permute-start.1 = (bf16[152,3584]{1,0:T(8,128)(2,1)}, bf16[152,3584]{1,0:T(8,128)(2,1)}, u32[]{:S(2)}, u32[]{:S(2)}) collective-permute-start(bf16[152,3584]{1,0:T(8,128)(2,1)} %bitcast.7), channel_id=1, source_target_pairs={{0,32},{32,0},{1,33},{33,1},{2,34},{34,2},{3,35},{35,3},{4,36},{36... | collective-permute-start | bytes 3268616 | tf_op jit(solution)/shard_map/ppermute | solution.py:14
  7.5 58.6 %all-to-all-start = ((bf16[16,8,3712]{2,1,0:T(8,128)(2,1)}), bf16[16,8,3712]{2,1,0:T(8,128)(2,1)}, u32[]{:S(2)}, u32[]{:S(2)}) async-start(bf16[16,8,3712]{2,1,0:T(8,128)(2,1)} %bitcast.64), calls=%async_computation | async-start | bytes 1900544 | tf_op jit(solution)/shard_map/all_to_all | solution.py:78
  68.9 29.3 %all-to-all-start.1 = ((bf16[4,64,3712]{2,1,0:T(8,128)(2,1)}), bf16[4,64,3712]{2,1,0:T(8,128)(2,1)S(1)}, u32[]{:S(2)}, u32[]{:S(2)}) async-start(bf16[4,64,3712]{2,1,0:T(8,128)(2,1)} %broadcast_in_dim.148), calls=%async_computation.1 | async-start | bytes 3801088 | tf_op jit(solution)/shard_map/all_to_all | solution.py:26
  73.8 24.4 %collective-permute-start.3 = (bf16[152,3584]{1,0:T(8,128)(2,1)}, bf16[152,3584]{1,0:T(8,128)(2,1)}, u32[]{:S(2)}, u32[]{:S(2)}) collective-permute-start(bf16[152,3584]{1,0:T(8,128)(2,1)} %bitcast.7), channel_id=1, source_target_pairs={{0,64},{64,0},{1,65},{65,1},{2,66},{66,2},{3,67},{67,3},{4,68},{68... | collective-permute-start | bytes 3268616 | tf_op jit(solution)/shard_map/ppermute | solution.py:14
  102.7 37.2 %collective-permute-start.4 = (bf16[256,456]{0,1:T(8,128)(2,1)S(1)}, bf16[256,456]{0,1:T(8,128)(2,1)S(1)}, u32[]{:S(2)}, u32[]{:S(2)}) collective-permute-start(bf16[256,456]{0,1:T(8,128)(2,1)S(1)} %convolution_convert_fusion.8), channel_id=1, source_target_pairs={{0,128},{128,0},{1,129},{129,1},{2,130},{130,2},{3,131},{131,3},{4... | collective-permute-start | bytes 700424 | tf_op jit(solution)/shard_map/ppermute | solution.py:14
  105.0 24.4 %all-to-all-start.3 = ((bf16[4,64,3584]{2,1,0:T(8,128)(2,1)}), bf16[4,64,3584]{2,1,0:T(8,128)(2,1)}, u32[]{:S(2)}, u32[]{:S(2)}) async-start(bf16[4,64,3584]{2,1,0:T(8,128)(2,1)} %broadcast_in_dim.163), calls=%async_computation.3 | async-start | bytes 3670016 | tf_op jit(solution)/shard_map/all_to_all | solution.py:26
  113.4 26.4 %collective-permute-start.5 = (bf16[256,456]{0,1:T(8,128)(2,1)}, bf16[256,456]{0,1:T(8,128)(2,1)}, u32[]{:S(2)}, u32[]{:S(2)}) collective-permute-start(bf16[256,456]{0,1:T(8,128)(2,1)} %convolution_convert_fusion.7), channel_id=1, source_target_pairs={{0,128},{128,0},{1,129},{129,1},{2,130},{130,2},{3,131},{131,3},{4... | collective-permute-start | bytes 700424 | tf_op jit(solution)/shard_map/ppermute | solution.py:14
  116.2 19.6 %collective-permute-start.9 = (bf16[152,3584]{1,0:T(8,128)(2,1)}, bf16[152,3584]{1,0:T(8,128)(2,1)}, u32[]{:S(2)}, u32[]{:S(2)}) collective-permute-start(bf16[152,3584]{1,0:T(8,128)(2,1)} %collective-permute-done.3), channel_id=1, source_target_pairs={{0,32},{32,0},{1,33},{33,1},{2,34},{34,2},{3,35},{35,3},{4,36},{36... | collective-permute-start | bytes 3268616 | tf_op jit(solution)/shard_map/ppermute | solution.py:14
  116.2 35.9 %collective-permute-start.6 = (bf16[2,152,3584]{2,1,0:T(8,128)(2,1)}, bf16[2,152,3584]{2,1,0:T(8,128)(2,1)}, u32[]{:S(2)}, u32[]{:S(2)}) collective-permute-start(bf16[2,152,3584]{2,1,0:T(8,128)(2,1)} %collective-permute-done.2), channel_id=1, source_target_pairs={{0,32},{32,0},{1,33},{33,1},{2,34},{34,2},{3,35},{35,3},{4,36},{36... | collective-permute-start | bytes 6537224 | tf_op jit(solution)/shard_map/ppermute | solution.py:14
  132.9 9.3 %collective-permute-start.10 = (bf16[256,456]{0,1:T(8,128)(2,1)S(1)}, bf16[256,456]{0,1:T(8,128)(2,1)S(1)}, u32[]{:S(2)}, u32[]{:S(2)}) collective-permute-start(bf16[256,456]{0,1:T(8,128)(2,1)S(1)} %convolution_convert_fusion.6), channel_id=1, source_target_pairs={{0,128},{128,0},{1,129},{129,1},{2,130},{130,2},{3,131},{131,3},{4... | collective-permute-start | bytes 700424 | tf_op jit(solution)/shard_map/ppermute | solution.py:14
  138.8 21.1 %collective-permute-start.11 = (bf16[256,304]{0,1:T(8,128)(2,1)S(1)}, bf16[256,304]{0,1:T(8,128)(2,1)S(1)}, u32[]{:S(2)}, u32[]{:S(2)}) collective-permute-start(bf16[256,304]{0,1:T(8,128)(2,1)S(1)} %fusion.5), channel_id=1, source_target_pairs={{0,128},{128,0},{1,129},{129,1},{2,130},{130,2},{3,131},{131,3},{4... | collective-permute-start | bytes 466952 | tf_op jit(solution)/shard_map/ppermute | solution.py:14
  154.8 6.7 %collective-permute-start.7 = (bf16[256,304]{0,1:T(8,128)(2,1)S(1)}, bf16[256,304]{0,1:T(8,128)(2,1)S(1)}, u32[]{:S(2)}, u32[]{:S(2)}) collective-permute-start(bf16[256,304]{0,1:T(8,128)(2,1)S(1)} %fusion.7), channel_id=1, source_target_pairs={{0,128},{128,0},{1,129},{129,1},{2,130},{130,2},{3,131},{131,3},{4... | collective-permute-start | bytes 466952 | tf_op jit(solution)/shard_map/ppermute | solution.py:14
  157.3 6.8 %collective-permute-start.8 = (bf16[256,304]{0,1:T(8,128)(2,1)S(1)}, bf16[256,304]{0,1:T(8,128)(2,1)S(1)}, u32[]{:S(2)}, u32[]{:S(2)}) collective-permute-start(bf16[256,304]{0,1:T(8,128)(2,1)S(1)} %fusion.6), channel_id=1, source_target_pairs={{0,128},{128,0},{1,129},{129,1},{2,130},{130,2},{3,131},{131,3},{4... | collective-permute-start | bytes 466952 | tf_op jit(solution)/shard_map/ppermute | solution.py:14
  169.2 27.0 %all-to-all-start.2 = ((bf16[4,64,3584]{2,1,0:T(8,128)(2,1)}), bf16[4,64,3584]{2,1,0:T(8,128)(2,1)}, u32[]{:S(2)}, u32[]{:S(2)}) async-start(bf16[4,64,3584]{2,1,0:T(8,128)(2,1)} %bitcast.61), calls=%async_computation.2 | async-start | bytes 3670016 | tf_op jit(solution)/shard_map/all_to_all | solution.py:19
  177.4 13.3 %collective-permute-start.12 = (bf16[304,3584]{1,0:T(8,128)(2,1)S(1)}, bf16[304,3584]{1,0:T(8,128)(2,1)S(1)}, u32[]{:S(2)}, u32[]{:S(2)}) collective-permute-start(bf16[304,3584]{1,0:T(8,128)(2,1)S(1)} %convolution_convert_fusion.4), channel_id=1, source_target_pairs={{0,32},{32,0},{1,33},{33,1},{2,34},{34,2},{3,35},{35,3},{4,36},{36... | collective-permute-start | bytes 6537224 | tf_op jit(solution)/shard_map/ppermute | solution.py:14
  178.3 13.8 %collective-permute-start.13 = (bf16[304,3584]{1,0:T(8,128)(2,1)S(1)}, bf16[304,3584]{1,0:T(8,128)(2,1)S(1)}, u32[]{:S(2)}, u32[]{:S(2)}) collective-permute-start(bf16[304,3584]{1,0:T(8,128)(2,1)S(1)} %convolution_convert_fusion.2), channel_id=1, source_target_pairs={{0,32},{32,0},{1,33},{33,1},{2,34},{34,2},{3,35},{35,3},{4,36},{36... | collective-permute-start | bytes 6537224 | tf_op jit(solution)/shard_map/ppermute | solution.py:14
  179.6 14.2 %collective-permute-start.14 = (bf16[304,3584]{1,0:T(8,128)(2,1)S(1)}, bf16[304,3584]{1,0:T(8,128)(2,1)S(1)}, u32[]{:S(2)}, u32[]{:S(2)}) collective-permute-start(bf16[304,3584]{1,0:T(8,128)(2,1)S(1)} %convolution_convert_fusion), channel_id=1, source_target_pairs={{0,32},{32,0},{1,33},{33,1},{2,34},{34,2},{3,35},{35,3},{4,36},{36... | collective-permute-start | bytes 6537224 | tf_op jit(solution)/shard_map/ppermute | solution.py:14
  195.6 27.2 %collective-permute-start.15 = (bf16[152,3584]{1,0:T(8,128)(2,1)}, bf16[152,3584]{1,0:T(8,128)(2,1)}, u32[]{:S(2)}, u32[]{:S(2)}) collective-permute-start(bf16[152,3584]{1,0:T(8,128)(2,1)} %add_convert_fusion.4), channel_id=1, source_target_pairs={{0,64},{64,0},{1,65},{65,1},{2,66},{66,2},{3,67},{67,3},{4,68},{68... | collective-permute-start | bytes 3268616 | tf_op jit(solution)/shard_map/ppermute | solution.py:14
  196.2 29.6 %all-to-all-start.4 = ((bf16[4,64,3584]{2,1,0:T(8,128)(2,1)}), bf16[4,64,3584]{2,1,0:T(8,128)(2,1)}, u32[]{:S(2)}, u32[]{:S(2)}) async-start(bf16[4,64,3584]{2,1,0:T(8,128)(2,1)} %bitcast.15), calls=%async_computation.4 | async-start | bytes 3670016 | tf_op jit(solution)/shard_map/all_to_all | solution.py:19
  203.0 47.5 %collective-permute-start.16 = (bf16[152,3584]{1,0:T(8,128)(2,1)}, bf16[152,3584]{1,0:T(8,128)(2,1)}, u32[]{:S(2)}, u32[]{:S(2)}) collective-permute-start(bf16[152,3584]{1,0:T(8,128)(2,1)} %add_convert_fusion.3), channel_id=1, source_target_pairs={{0,64},{64,0},{1,65},{65,1},{2,66},{66,2},{3,67},{67,3},{4,68},{68... | collective-permute-start | bytes 3268616 | tf_op jit(solution)/shard_map/ppermute | solution.py:14
  204.6 73.5 %collective-permute-start.17 = (bf16[152,3584]{1,0:T(8,128)(2,1)}, bf16[152,3584]{1,0:T(8,128)(2,1)}, u32[]{:S(2)}, u32[]{:S(2)}) collective-permute-start(bf16[152,3584]{1,0:T(8,128)(2,1)} %add_convert_fusion.5), channel_id=1, source_target_pairs={{0,64},{64,0},{1,65},{65,1},{2,66},{66,2},{3,67},{67,3},{4,68},{68... | collective-permute-start | bytes 3268616 | tf_op jit(solution)/shard_map/ppermute | solution.py:14
  229.0 51.8 %all-to-all-start.5 = ((bf16[16,8,3584]{2,1,0:T(8,128)(2,1)}), bf16[16,8,3584]{2,1,0:T(8,128)(2,1)S(1)}, u32[]{:S(2)}, u32[]{:S(2)}) async-start(bf16[16,8,3584]{2,1,0:T(8,128)(2,1)} %pad_maximum_fusion), calls=%async_computation.5 | async-start | bytes 1835008 | tf_op jit(solution)/shard_map/all_to_all | solution.py:145
  (35 other events, 253.3 us)

commit v3 on v2

--- a/solution.py
+++ b/solution.py
@@ -20,6 +20,10 @@
     return jnp.sum(landed.astype(F32), axis=0)
 
 
+def in_order(data, mine, other):
+    return jnp.where(data == 0, jnp.concatenate([mine, other], axis=0), jnp.concatenate([other, mine], axis=0))
+
+
 def gather(block, axis):
     size = lax.axis_size(axis)
     wide = jnp.broadcast_to(block[None], (size,) + block.shape)
@@ -39,6 +43,15 @@
     return total
 
 
+def finish(part, data):
+    rows = part.shape[0] // 2
+    own = jnp.where(data == 0, part[:rows], part[rows:])
+    other = swap(jnp.where(data == 0, part[rows:], part[:rows]), ("dp",))
+    return jnp.where(
+        data == 0, jnp.concatenate([own, other], axis=1), jnp.concatenate([other, own], axis=1)
+    ).astype(BF)
+
+
 def dot(left, right, dims):
     return lax.dot_general(left, right, (dims, ((), ())), preferred_element_type=F32)
 
@@ -51,41 +64,41 @@
     hidden = expert_gate.shape[1]
     data, near, core = (lax.axis_index(name) for name in ("dp", "xlo", "core"))
     rows = tokens.shape[0]
-    halves, depth = lax.axis_size("dp"), lax.axis_size("z")
+    depth = lax.axis_size("z")
 
-    gate_up = jnp.concatenate([expert_gate, expert_up], axis=0)
-    gate_up_x = swap(gate_up, ("xlo",))
-    gate_up_c = swap(gate_up, ("core",))
-    down_x = swap(expert_down[0], ("xlo",))
-    down_c = swap(expert_down[0], ("core",))
+    gate, up, down = expert_gate[0], expert_up[0], expert_down[0]
+    gate_x = swap(gate, ("xlo",))
 
-    def pack(mine, by_core, dense):
+    def pack(mine, dense):
         dense = lax.dynamic_slice_in_dim(dense, data * width, width, axis=1)
-        return stack_rows([mine, by_core, dense], 3 * hidden)
+        return stack_rows([mine, swap(mine, ("core",)), dense], 3 * hidden)
 
-    gate_a = pack(expert_gate[0], gate_up_c[0], dense_gate)
-    up_a = pack(expert_up[0], gate_up_c[1], dense_up)
-    down_a = pack(expert_down[0], down_c, dense_down)
+    def pack_far(theirs):
+        return stack_rows([theirs, swap(theirs, ("core",))], 2 * hidden)
+
+    gate_a, up_a, down_a = pack(gate, dense_gate), pack(up, dense_up), pack(down, dense_down)
 
     ids = jnp.arange(128, dtype=jnp.int32)
     weights_of = jnp.sum(
         jnp.where(routes[:, :, None] == ids[None, None, :], route_gates.astype(F32)[:, :, None], 0.0), axis=1
     ).astype(BF)
-    both = join([tokens, cotangent])
     marks = join([weights_of, jnp.zeros_like(weights_of)])
-    both = jnp.stack([jnp.concatenate([both[:, i * width:(i + 1) * width], marks], axis=1) for i in range(halves)])
-    wide = jnp.broadcast_to(both[:, None], (halves, depth) + both.shape[1:]).reshape((-1,) + both.shape[1:])
-    block = lax.all_to_all(wide, ("dp", "z"), 0, 0, tiled=True)
-    block, gate_a, up_a, down_a = lax.optimization_barrier((block, gate_a, up_a, down_a))
 
-    tok = gather(block[:, :rows].reshape(-1, block.shape[2]), "y").reshape(-1, block.shape[2])
-    tok, block, gate_up_x, down_x = lax.optimization_barrier((tok, block, gate_up_x, down_x))
-    cot = gather(block[:, rows:, :width].reshape(-1, width), "y").reshape(-1, width)
+    def columns(at):
+        both = lax.dynamic_slice_in_dim(join([tokens, cotangent]), at * width, width, axis=1)
+        return jnp.concatenate([both, marks], axis=1)
 
-    gate_up_b = swap(gate_up_x, ("core",))
-    gate_b = stack_rows([gate_up_x[0], gate_up_b[0]], 2 * hidden)
-    up_b = stack_rows([gate_up_x[1], gate_up_b[1]], 2 * hidden)
-    down_b = stack_rows([down_x, swap(down_x, ("core",))], 2 * hidden)
+    own, far = columns(data), swap(columns(1 - data), ("dp",))
+    block = join([in_order(data, own[:rows], far[:rows]), in_order(data, own[rows:], far[rows:])])
+    block = gather(block, "z").reshape(depth, 4 * rows, -1)
+    block, gate_x, gate_a, up_a, down_a, up = lax.optimization_barrier((block, gate_x, gate_a, up_a, down_a, up))
+    up_x = swap(up, ("xlo",))
+    tok = gather(block[:, :2 * rows].reshape(-1, block.shape[2]), "y").reshape(-1, block.shape[2])
+    gate_b = pack_far(gate_x)
+    block, tok, up_x, down = lax.optimization_barrier((block, tok, up_x, down))
+    down_x = swap(down, ("xlo",))
+    cot = gather(block[:, 2 * rows:, :width].reshape(-1, width), "y").reshape(-1, width)
+    up_b = pack_far(up_x)
 
     weighting = tok[:, width:].astype(F32)
     tok = tok[:, :width]
@@ -117,13 +130,15 @@
 
     pre_a, lin_a, act_a = forward(gate_a, up_a, scale_a)
     pre_b, lin_b, act_b = forward(gate_b, up_b, scale_b)
+    cot, down_x, act_a, act_b = lax.optimization_barrier((cot, down_x, act_a, act_b))
+    down_b = pack_far(down_x)
     grad_a, lin_grad_a = backward(pre_a, lin_a, down_a, scale_a)
     grad_b, lin_grad_b = backward(pre_b, lin_b, down_b, scale_b)
 
     def times(*pairs):
         return sum(dot(left, right, ((1,), (0,))) for left, right in pairs).astype(BF)
 
-    mixed = scatter(times((act_a, down_a), (act_b, down_b)), "y").astype(BF)
+    mixed = times((act_a, down_a), (act_b, down_b))
     grads = times((grad_a, gate_a), (lin_grad_a, up_a), (grad_b, gate_b), (lin_grad_b, up_b))
 
     def far_grads(left_a, left_b, right):
@@ -134,18 +149,29 @@
         return ours, theirs, (ours[hidden:].astype(F32) + theirs[hidden:].astype(F32)).astype(BF)
 
     def whole_grad(ours, theirs, far):
-        far = swap(far, ("xlo",))
         return (ours[:hidden].astype(F32) + theirs[:hidden].astype(F32) + far.astype(F32)).astype(BF)[None]
 
-    parts = [far_grads(act_a, act_b, cot), far_grads(grad_a, grad_b, tok), far_grads(lin_grad_a, lin_grad_b, tok)]
-    grads, parts = lax.optimization_barrier((grads, parts))
-    grad_down, grad_gate, grad_up = [whole_grad(*part) for part in parts]
+    down_ours, down_theirs, down_far = far_grads(act_a, act_b, cot)
+    mixed, down_far = lax.optimization_barrier((mixed, down_far))
+    down_far = swap(down_far, ("xlo",))
+    mixed = scatter(mixed, "y").astype(BF)
+    gate_ours, gate_theirs, gate_far = far_grads(grad_a, grad_b, tok)
+    grads, gate_far, mixed, down_far = lax.optimization_barrier((grads, gate_far, mixed, down_far))
+    gate_far = swap(gate_far, ("xlo",))
     grads = scatter(grads, "y").astype(BF)
-    both = jnp.concatenate([part.reshape(halves * depth, rows, width) for part in (mixed, grads)], axis=1)
-    both = lax.all_to_all(both, ("dp", "z"), 0, 0, tiled=True).astype(F32)
-    both = jnp.sum(both.reshape(halves, depth, 2 * rows, width), axis=1).astype(BF)
-    both = jnp.concatenate([both[i] for i in range(halves)], axis=1)
-    return (both[:rows], both[rows:], grad_gate, grad_up, grad_down)
+    up_ours, up_theirs, up_far = far_grads(lin_grad_a, lin_grad_b, tok)
+    both = jnp.concatenate([part.reshape(depth, 2 * rows, width) for part in (mixed, grads)], axis=1)
+    both, up_far, gate_far = lax.optimization_barrier((both, up_far, gate_far))
+    up_far = swap(up_far, ("xlo",))
+    both = scatter(both.reshape(-1, width), "z")
+    mixed, grads = finish(both[:2 * rows], data), finish(both[2 * rows:], data)
+    return (
+        mixed,
+        grads,
+        whole_grad(gate_ours, gate_theirs, gate_far),
+        whole_grad(up_ours, up_theirs, up_far),
+        whole_grad(down_ours, down_theirs, down_far),
+    )
 
 
 def solution(mesh):

time: 283 us -> 304 us (1.074)
  waiting for transfers between devices: 130 us -> 148 us
  matrix products: 35.2 us -> 50.5 us
  local copies, waits for them, and re-layouts: 27.8 us -> 13.8 us
  other arithmetic: 28.5 us -> 36.9 us
  starting transfers between devices: 58.6 us -> 52.5 us
    all_to_all x2 -> x3, waiting for transfers between devices: 0.01 us -> 44 us  [scatter(): lax.all_to_all(part.reshape(size, -1, part.shape[1]), axis, 0, 0, tiled=T...]
    all_to_all x2 -> x0, waiting for transfers between devices: 36.3 us -> none  [the longest x1 36.3 us: per_device(): block = lax.all_to_all(wide, ('dp', 'z'), 0, 0, tiled=True)]
    all_to_all x2 -> x0, starting transfers between devices: 20.6 us -> none  [the longest x1 10.8 us: per_device(): block = lax.all_to_all(wide, ('dp', 'z'), 0, 0, tiled=True)]
    dot_general x18, matrix products: 35.2 us -> 50.5 us  [dot(): lax.dot_general(left, right, (dims, ((), ())), preferred_element_type=F32)]
    all_to_all x2 -> x3, starting transfers between devices: 9.71 us -> 18.3 us  [gather(): return lax.all_to_all(wide, axis, 0, 0, tiled=True)]
    all_to_all x2 -> x3, waiting for transfers between devices: 9.88 us -> 16.3 us  [gather(): return lax.all_to_all(wide, axis, 0, 0, tiled=True)]
    squeeze x4 -> x0, local copies, waits for them, and re-layouts: 6.21 us -> none  [the longest x2 4.49 us: per_device(): up_b = stack_rows([gate_up_x[1], gate_up_b[1]], 2 * hidden)]
    slice x8, local copies, waits for them, and re-layouts: 5.41 us -> 0.12 us  [the longest x6 0.07 us: far_grads(): ours = jnp.concatenate([left_a[:, :hidden], left_b[:, :hidden]], axis=1)]
  transfers between devices with their start and end apart: 24 -> 30, of which waited for: 9 -> 15; matrix products, arithmetic and copies ran while one was open for 25% -> 30% of each run, Pallas kernels for 0% -> 0%
where the time goes in v3:
time: 304 us; the launch traced here: 303 us
  waiting for transfers between devices  148 us (49%)
  starting transfers between devices  52.5 us (17%)
  matrix products  50.5 us (17%)
  other arithmetic  36.9 us (12%)
  local copies, waits for them, and re-layouts  13.8 us (5%)
    ppermute x24, waiting for transfers between devices, swap(): return lax.ppermute(value, axes, [(i, size - 1 - i) for i in range(size)])  87.4 us
    dot_general x18, matrix products, dot(): lax.dot_general(left, right, (dims, ((), ())), preferred_element_type=F32)  50.5 us
    all_to_all x3, waiting for transfers between devices, scatter(): lax.all_to_all(part.reshape(size, -1, part.shape[1]), axis, 0, 0, tiled=T...  44 us
    ppermute x24, starting transfers between devices, swap(): return lax.ppermute(value, axes, [(i, size - 1 - i) for i in range(size)])  21 us
    all_to_all x3, starting transfers between devices, gather(): return lax.all_to_all(wide, axis, 0, 0, tiled=True)  18.3 us
    all_to_all x3, waiting for transfers between devices, gather(): return lax.all_to_all(wide, axis, 0, 0, tiled=True)  16.3 us
    all_to_all x3, starting transfers between devices, scatter(): lax.all_to_all(part.reshape(size, -1, part.shape[1]), axis, 0, 0, tiled=T...  13.2 us
    broadcast_in_dim x3, other arithmetic, whole_grad(): (ours[:hidden].astype(F32) + theirs[:hidden].astype(F32) + far.astype(F32...  9.39 us
  transfers between devices with their start and end apart: 30, of which 15 were waited for; matrix products, arithmetic and copies ran while one was open for 30% of the time, Pallas kernels for 0%

profile of v3, /device:TPU:8, one launch (start us, length us, event | category | flops | bytes accessed | tf_op | source)
XLA Modules:
  0.0 302.5 jit_solution(11621584163108001667)
XLA Ops:
  10.7 20.2 %collective-permute-done = bf16[8,3712]{1,0:T(8,128)(2,1)S(1)} collective-permute-done((bf16[8,3712]{1,0:T(8,128)(2,1)S(1)}, bf16[8,3712]{1,0:T(8,128)(2,1)S(1)}, u32[]{:S(2)}, u32[]{:S(2)}) %collective-permute-start) | collective-permute-done | bytes 59424 | tf_op jit(solution)/shard_map/ppermute | solution.py:14
  32.0 8.5 %all-to-all-start = ((bf16[8,16,3712]{2,1,0:T(8,128)(2,1)}), bf16[8,16,3712]{2,1,0:T(8,128)(2,1)}, u32[]{:S(2)}, u32[]{:S(2)}) async-start(bf16[8,16,3712]{2,1,0:T(8,128)(2,1)} %broadcast_in_dim.146), calls=%async_computation | async-start | bytes 1900544 | tf_op jit(solution)/shard_map/all_to_all | solution.py:30
  44.7 3.1 %pad_add_fusion = bf16[456,3584]{1,0:T(8,128)(2,1)} fusion(bf16[152,3584]{1,0:T(8,128)(2,1)S(1)} %copy-done.9, bf16[152,3584]{1,0:T(8,128)(2,1)} %collective-permute-done.4, bf16[152,3584]{1,0:T(8,128)(2,1)} %bitcast.2), kind=kLoop, calls=%fused_computation.12 | loop fusion | flops 9805824 | bytes 6537216 | tf_op jit(solution)/shard_map/add | solution.py:41
  50.7 16.3 %all-to-all-done = bf16[8,16,3712]{2,1,0:T(8,128)(2,1)} async-done(((bf16[8,16,3712]{2,1,0:T(8,128)(2,1)}), bf16[8,16,3712]{2,1,0:T(8,128)(2,1)}, u32[]{:S(2)}, u32[]{:S(2)}) %all-to-all-start) | async-done | bytes 950304 | tf_op jit(solution)/shard_map/all_to_all | solution.py:30
  69.6 5.0 %all-to-all-start.1 = ((bf16[4,64,3712]{2,1,0:T(8,128)(2,1)}), bf16[4,64,3712]{2,1,0:T(8,128)(2,1)S(1)}, u32[]{:S(2)}, u32[]{:S(2)}) async-start(bf16[4,64,3712]{2,1,0:T(8,128)(2,1)} %broadcast_in_dim.148), calls=%async_computation.1 | async-start | bytes 3801088 | tf_op jit(solution)/shard_map/all_to_all | solution.py:30
  74.9 25.2 %collective-permute-done.5 = bf16[152,3584]{1,0:T(8,128)(2,1)} collective-permute-done((bf16[152,3584]{1,0:T(8,128)(2,1)S(1)}, bf16[152,3584]{1,0:T(8,128)(2,1)}, u32[]{:S(2)}, u32[]{:S(2)}) %collective-permute-start.5) | collective-permute-done | bytes 1089568 | tf_op jit(solution)/shard_map/ppermute | solution.py:14
  106.9 4.8 %all-to-all-start.2 = ((bf16[4,64,3584]{2,1,0:T(8,128)(2,1)}), bf16[4,64,3584]{2,1,0:T(8,128)(2,1)}, u32[]{:S(2)}, u32[]{:S(2)}) async-start(bf16[4,64,3584]{2,1,0:T(8,128)(2,1)} %broadcast_in_dim.150), calls=%async_computation.2 | async-start | bytes 3670016 | tf_op jit(solution)/shard_map/all_to_all | solution.py:30
  115.9 3.2 %collective-permute-start.7 = (bf16[256,456]{0,1:T(8,128)(2,1)S(1)}, bf16[256,456]{0,1:T(8,128)(2,1)S(1)}, u32[]{:S(2)}, u32[]{:S(2)}) collective-permute-start(bf16[256,456]{0,1:T(8,128)(2,1)S(1)} %convolution_convert_fusion.8), channel_id=1, source_target_pairs={{0,128},{128,0},{1,129},{129,1},{2,130},{130,2},{3,131},{131,3},{4... | collective-permute-start | bytes 700424 | tf_op jit(solution)/shard_map/ppermute | solution.py:14
  122.2 3.3 %collective-permute-start.12 = (bf16[256,304]{0,1:T(8,128)(2,1)S(1)}, bf16[256,304]{0,1:T(8,128)(2,1)S(1)}, u32[]{:S(2)}, u32[]{:S(2)}) collective-permute-start(bf16[256,304]{0,1:T(8,128)(2,1)S(1)} %fusion.11), channel_id=1, source_target_pairs={{0,128},{128,0},{1,129},{129,1},{2,130},{130,2},{3,131},{131,3},{4... | collective-permute-start | bytes 466952 | tf_op jit(solution)/shard_map/ppermute | solution.py:14
  125.5 15.6 %collective-permute-done.7 = bf16[256,456]{0,1:T(8,128)(2,1)S(1)} collective-permute-done((bf16[256,456]{0,1:T(8,128)(2,1)S(1)}, bf16[256,456]{0,1:T(8,128)(2,1)S(1)}, u32[]{:S(2)}, u32[]{:S(2)}) %collective-permute-start.7) | collective-permute-done | bytes 233504 | tf_op jit(solution)/shard_map/ppermute | solution.py:14
  141.1 5.0 %collective-permute-done.8 = bf16[256,456]{0,1:T(8,128)(2,1)S(1)} collective-permute-done((bf16[256,456]{0,1:T(8,128)(2,1)S(1)}, bf16[256,456]{0,1:T(8,128)(2,1)S(1)}, u32[]{:S(2)}, u32[]{:S(2)}) %collective-permute-start.8) | collective-permute-done | bytes 233504 | tf_op jit(solution)/shard_map/ppermute | solution.py:14
  150.3 3.5 %convolution_convert_fusion.6 = bf16[256,456]{0,1:T(8,128)(2,1)S(1)} fusion(bf16[256,3584]{1,0:T(8,128)(2,1)} %bitcast.6, bf16[456,3584]{1,0:T(8,128)(2,1)} %pad_add_fusion), kind=kOutput, calls=%fused_computation.31 | convolution fusion | flops 836880384 | bytes 5337088 | tf_op jit(solution)/shard_map/dot_general | solution.py:56
  181.7 4.2 %fusion.6 = f32[256,3584]{1,0:T(8,128)} fusion(bf16[256,304]{0,1:T(8,128)(2,1)S(1)} %get-tuple-element.58, bf16[152,3584]{1,0:T(8,128)(2,1)S(1)} %copy-done.15, bf16[152,3584]{1,0:T(8,128)(2,1)} %collective-permute-done.5), kind=kOutput, calls=%fused_computation.27 | convolution fusion | flops 562200576 | bytes 6004736 | tf_op jit(solution)/shard_map/dot_general | solution.py:56
  185.8 4.6 %fusion.4 = f32[256,3584]{1,0:T(8,128)} fusion(bf16[256,304]{0,1:T(8,128)(2,1)S(1)} %get-tuple-element.57, bf16[152,3584]{1,0:T(8,128)(2,1)} %collective-permute-done.9, bf16[152,3584]{1,0:T(8,128)(2,1)} %collective-permute-done.1), kind=kOutput, calls=%fused_computation.25 | convolution fusion | flops 562200576 | bytes 6004736 | tf_op jit(solution)/shard_map/dot_general | solution.py:56
  192.2 4.8 %all-to-all-start.3 = ((bf16[4,64,3584]{2,1,0:T(8,128)(2,1)}), bf16[4,64,3584]{2,1,0:T(8,128)(2,1)}, u32[]{:S(2)}, u32[]{:S(2)}) async-start(bf16[4,64,3584]{2,1,0:T(8,128)(2,1)} %bitcast.45), calls=%async_computation.3 | async-start | bytes 3670016 | tf_op jit(solution)/shard_map/all_to_all | solution.py:19
  197.1 7.8 %fusion.2 = bf16[256,3584]{1,0:T(8,128)(2,1)} fusion(f32[256,3584]{1,0:T(8,128)} %fusion.6, f32[256,3584]{1,0:T(8,128)} %fusion.4, f32[256,3584]{1,0:T(8,128)} %fusion.76, bf16[256,456]{0,1:T(8,128)(2,1)S(1)} %get-tuple-element.55, bf16[456,3584]{1,0:T(8,128)(2,1)} %pad_add_fusion.2), kind=kOutput, calls=%fused_computation.10 | convolution fusion | flops 840433664 | bytes 16347136 | tf_op jit(solution)/shard_map/dot_general | solution.py:56
  209.8 9.8 %all-to-all-done.3 = bf16[4,64,3584]{2,1,0:T(8,128)(2,1)} async-done(((bf16[4,64,3584]{2,1,0:T(8,128)(2,1)}), bf16[4,64,3584]{2,1,0:T(8,128)(2,1)}, u32[]{:S(2)}, u32[]{:S(2)}) %all-to-all-start.3) | async-done | bytes 1835040 | tf_op jit(solution)/shard_map/all_to_all | solution.py:19
  221.3 9.3 %collective-permute-done.18 = bf16[152,3584]{1,0:T(8,128)(2,1)} collective-permute-done((bf16[152,3584]{1,0:T(8,128)(2,1)}, bf16[152,3584]{1,0:T(8,128)(2,1)}, u32[]{:S(2)}, u32[]{:S(2)}) %collective-permute-start.18) | collective-permute-done | bytes 1089568 | tf_op jit(solution)/shard_map/ppermute | solution.py:14
  230.7 4.8 %all-to-all-start.4 = ((bf16[4,64,3584]{2,1,0:T(8,128)(2,1)}), bf16[4,64,3584]{2,1,0:T(8,128)(2,1)}, u32[]{:S(2)}, u32[]{:S(2)}) async-start(bf16[4,64,3584]{2,1,0:T(8,128)(2,1)} %bitcast.44), calls=%async_computation.4 | async-start | bytes 3670016 | tf_op jit(solution)/shard_map/all_to_all | solution.py:19
  240.2 16.8 %all-to-all-done.4 = bf16[4,64,3584]{2,1,0:T(8,128)(2,1)} async-done(((bf16[4,64,3584]{2,1,0:T(8,128)(2,1)}), bf16[4,64,3584]{2,1,0:T(8,128)(2,1)}, u32[]{:S(2)}, u32[]{:S(2)}) %all-to-all-start.4) | async-done | bytes 1835040 | tf_op jit(solution)/shard_map/all_to_all | solution.py:19
  262.0 3.6 %all-to-all-start.5 = ((bf16[8,16,3584]{2,1,0:T(8,128)(2,1)}), bf16[8,16,3584]{2,1,0:T(8,128)(2,1)S(1)}, u32[]{:S(2)}, u32[]{:S(2)}) async-start(bf16[8,16,3584]{2,1,0:T(8,128)(2,1)} %pad_maximum_fusion), calls=%async_computation.5 | async-start | bytes 1835008 | tf_op jit(solution)/shard_map/all_to_all | solution.py:19
  265.6 3.4 %fusion.15 = bf16[1,152,3584]{2,1,0:T(8,128)(2,1)} fusion(bf16[152,3584]{1,0:T(8,128)(2,1)} %collective-permute-done.18, bf16[304,3584]{1,0:T(8,128)(2,1)} %copy-done.10, bf16[304,3584]{1,0:T(8,128)(2,1)} %copy-done.8), kind=kLoop, calls=%fused_computation.39 | loop fusion | flops 3268608 | bytes 4358144 | tf_op jit(solution)/shard_map/broadcast_in_dim | solution.py:152
  272.0 17.5 %all-to-all-done.5 = bf16[8,16,3584]{2,1,0:T(8,128)(2,1)S(1)} async-done(((bf16[8,16,3584]{2,1,0:T(8,128)(2,1)}), bf16[8,16,3584]{2,1,0:T(8,128)(2,1)S(1)}, u32[]{:S(2)}, u32[]{:S(2)}) %all-to-all-start.5) | async-done | bytes 917536 | tf_op jit(solution)/shard_map/all_to_all | solution.py:19
  293.2 3.3 %fusion.14 = bf16[1,152,3584]{2,1,0:T(8,128)(2,1)} fusion(bf16[152,3584]{1,0:T(8,128)(2,1)} %collective-permute-done.23, bf16[304,3584]{1,0:T(8,128)(2,1)} %collective-permute-done.19, bf16[304,3584]{1,0:T(8,128)(2,1)} %copy-done.5), kind=kLoop, calls=%fused_computation.38 | loop fusion | flops 3268608 | bytes 4358144 | tf_op jit(solution)/shard_map/broadcast_in_dim | solution.py:152
  (156 shorter events, 97.9 us)
Async XLA Ops:
  0.6 40.0 %collective-permute-start.2 = (bf16[152,3584]{1,0:T(8,128)(2,1)}, bf16[152,3584]{1,0:T(8,128)(2,1)}, u32[]{:S(2)}, u32[]{:S(2)}) collective-permute-start(bf16[152,3584]{1,0:T(8,128)(2,1)} %bitcast.48), channel_id=1, source_target_pairs={{0,32},{32,0},{1,33},{33,1},{2,34},{34,2},{3,35},{35,3},{4,36},{36... | collective-permute-start | bytes 3268616 | tf_op jit(solution)/shard_map/ppermute | solution.py:14
  0.8 50.0 %collective-permute-start.1 = (bf16[152,3584]{1,0:T(8,128)(2,1)}, bf16[152,3584]{1,0:T(8,128)(2,1)}, u32[]{:S(2)}, u32[]{:S(2)}) collective-permute-start(bf16[152,3584]{1,0:T(8,128)(2,1)} %bitcast.49), channel_id=1, source_target_pairs={{0,64},{64,0},{1,65},{65,1},{2,66},{66,2},{3,67},{67,3},{4,68},{68... | collective-permute-start | bytes 3268616 | tf_op jit(solution)/shard_map/ppermute | solution.py:14
  4.7 26.2 %collective-permute-start = (bf16[8,3712]{1,0:T(8,128)(2,1)S(1)}, bf16[8,3712]{1,0:T(8,128)(2,1)S(1)}, u32[]{:S(2)}, u32[]{:S(2)}) collective-permute-start(bf16[8,3712]{1,0:T(8,128)(2,1)S(1)} %get-tuple-element.82), channel_id=1, source_target_pairs={{0,128},{128,0},{1,129},{129,1},{2,130},{130,2},{3,131},{131,3},{4... | collective-permute-start | bytes 178184 | tf_op jit(solution)/shard_map/ppermute | solution.py:14
  7.5 40.3 %collective-permute-start.3 = (bf16[152,3584]{1,0:T(8,128)(2,1)}, bf16[152,3584]{1,0:T(8,128)(2,1)}, u32[]{:S(2)}, u32[]{:S(2)}) collective-permute-start(bf16[152,3584]{1,0:T(8,128)(2,1)} %bitcast.51), channel_id=1, source_target_pairs={{0,32},{32,0},{1,33},{33,1},{2,34},{34,2},{3,35},{35,3},{4,36},{36... | collective-permute-start | bytes 3268616 | tf_op jit(solution)/shard_map/ppermute | solution.py:14
  7.5 37.2 %collective-permute-start.4 = (bf16[152,3584]{1,0:T(8,128)(2,1)}, bf16[152,3584]{1,0:T(8,128)(2,1)}, u32[]{:S(2)}, u32[]{:S(2)}) collective-permute-start(bf16[152,3584]{1,0:T(8,128)(2,1)} %bitcast.2), channel_id=1, source_target_pairs={{0,32},{32,0},{1,33},{33,1},{2,34},{34,2},{3,35},{35,3},{4,36},{36... | collective-permute-start | bytes 3268616 | tf_op jit(solution)/shard_map/ppermute | solution.py:14
  32.0 35.0 %all-to-all-start = ((bf16[8,16,3712]{2,1,0:T(8,128)(2,1)}), bf16[8,16,3712]{2,1,0:T(8,128)(2,1)}, u32[]{:S(2)}, u32[]{:S(2)}) async-start(bf16[8,16,3712]{2,1,0:T(8,128)(2,1)} %broadcast_in_dim.146), calls=%async_computation | async-start | bytes 1900544 | tf_op jit(solution)/shard_map/all_to_all | solution.py:30
  69.6 30.6 %all-to-all-start.1 = ((bf16[4,64,3712]{2,1,0:T(8,128)(2,1)}), bf16[4,64,3712]{2,1,0:T(8,128)(2,1)S(1)}, u32[]{:S(2)}, u32[]{:S(2)}) async-start(bf16[4,64,3712]{2,1,0:T(8,128)(2,1)} %broadcast_in_dim.148), calls=%async_computation.1 | async-start | bytes 3801088 | tf_op jit(solution)/shard_map/all_to_all | solution.py:30
  74.6 25.5 %collective-permute-start.5 = (bf16[152,3584]{1,0:T(8,128)(2,1)S(1)}, bf16[152,3584]{1,0:T(8,128)(2,1)}, u32[]{:S(2)}, u32[]{:S(2)}) collective-permute-start(bf16[152,3584]{1,0:T(8,128)(2,1)S(1)} %bitcast.53), channel_id=1, source_target_pairs={{0,64},{64,0},{1,65},{65,1},{2,66},{66,2},{3,67},{67,3},{4,68},{68... | collective-permute-start | bytes 3268616 | tf_op jit(solution)/shard_map/ppermute | solution.py:14
  74.9 26.3 %collective-permute-start.9 = (bf16[152,3584]{1,0:T(8,128)(2,1)}, bf16[152,3584]{1,0:T(8,128)(2,1)}, u32[]{:S(2)}, u32[]{:S(2)}) collective-permute-start(bf16[152,3584]{1,0:T(8,128)(2,1)} %collective-permute-done.1), channel_id=1, source_target_pairs={{0,32},{32,0},{1,33},{33,1},{2,34},{34,2},{3,35},{35,3},{4,36},{36... | collective-permute-start | bytes 3268616 | tf_op jit(solution)/shard_map/ppermute | solution.py:14
  104.2 42.2 %collective-permute-start.10 = (bf16[256,304]{0,1:T(8,128)(2,1)}, bf16[256,304]{0,1:T(8,128)(2,1)}, u32[]{:S(2)}, u32[]{:S(2)}) collective-permute-start(bf16[256,304]{0,1:T(8,128)(2,1)} %fusion.12), channel_id=1, source_target_pairs={{0,128},{128,0},{1,129},{129,1},{2,130},{130,2},{3,131},{131,3},{4... | collective-permute-start | bytes 466952 | tf_op jit(solution)/shard_map/ppermute | solution.py:14
  105.0 45.3 %collective-permute-start.6 = (bf16[152,3584]{1,0:T(8,128)(2,1)}, bf16[152,3584]{1,0:T(8,128)(2,1)}, u32[]{:S(2)}, u32[]{:S(2)}) collective-permute-start(bf16[152,3584]{1,0:T(8,128)(2,1)} %bitcast.2), channel_id=1, source_target_pairs={{0,64},{64,0},{1,65},{65,1},{2,66},{66,2},{3,67},{67,3},{4,68},{68... | collective-permute-start | bytes 3268616 | tf_op jit(solution)/shard_map/ppermute | solution.py:14
  106.9 43.4 %all-to-all-start.2 = ((bf16[4,64,3584]{2,1,0:T(8,128)(2,1)}), bf16[4,64,3584]{2,1,0:T(8,128)(2,1)}, u32[]{:S(2)}, u32[]{:S(2)}) async-start(bf16[4,64,3584]{2,1,0:T(8,128)(2,1)} %broadcast_in_dim.150), calls=%async_computation.2 | async-start | bytes 3670016 | tf_op jit(solution)/shard_map/all_to_all | solution.py:30
  115.9 25.1 %collective-permute-start.7 = (bf16[256,456]{0,1:T(8,128)(2,1)S(1)}, bf16[256,456]{0,1:T(8,128)(2,1)S(1)}, u32[]{:S(2)}, u32[]{:S(2)}) collective-permute-start(bf16[256,456]{0,1:T(8,128)(2,1)S(1)} %convolution_convert_fusion.8), channel_id=1, source_target_pairs={{0,128},{128,0},{1,129},{129,1},{2,130},{130,2},{3,131},{131,3},{4... | collective-permute-start | bytes 700424 | tf_op jit(solution)/shard_map/ppermute | solution.py:14
  119.1 27.0 %collective-permute-start.8 = (bf16[256,456]{0,1:T(8,128)(2,1)S(1)}, bf16[256,456]{0,1:T(8,128)(2,1)S(1)}, u32[]{:S(2)}, u32[]{:S(2)}) collective-permute-start(bf16[256,456]{0,1:T(8,128)(2,1)S(1)} %convolution_convert_fusion.7), channel_id=1, source_target_pairs={{0,128},{128,0},{1,129},{129,1},{2,130},{130,2},{3,131},{131,3},{4... | collective-permute-start | bytes 700424 | tf_op jit(solution)/shard_map/ppermute | solution.py:14
  122.2 26.9 %collective-permute-start.12 = (bf16[256,304]{0,1:T(8,128)(2,1)S(1)}, bf16[256,304]{0,1:T(8,128)(2,1)S(1)}, u32[]{:S(2)}, u32[]{:S(2)}) collective-permute-start(bf16[256,304]{0,1:T(8,128)(2,1)S(1)} %fusion.11), channel_id=1, source_target_pairs={{0,128},{128,0},{1,129},{129,1},{2,130},{130,2},{3,131},{131,3},{4... | collective-permute-start | bytes 466952 | tf_op jit(solution)/shard_map/ppermute | solution.py:14
  157.0 33.5 %collective-permute-start.17 = (bf16[304,3584]{1,0:T(8,128)(2,1)S(1)}, bf16[304,3584]{1,0:T(8,128)(2,1)S(1)}, u32[]{:S(2)}, u32[]{:S(2)}) collective-permute-start(bf16[304,3584]{1,0:T(8,128)(2,1)S(1)} %convolution_convert_fusion.2), channel_id=1, source_target_pairs={{0,32},{32,0},{1,33},{33,1},{2,34},{34,2},{3,35},{35,3},{4,36},{36... | collective-permute-start | bytes 6537224 | tf_op jit(solution)/shard_map/ppermute | solution.py:14
  179.0 26.8 %collective-permute-start.16 = (bf16[304,3584]{1,0:T(8,128)(2,1)}, bf16[304,3584]{1,0:T(8,128)(2,1)}, u32[]{:S(2)}, u32[]{:S(2)}) collective-permute-start(bf16[304,3584]{1,0:T(8,128)(2,1)} %convolution_convert_fusion.4), channel_id=1, source_target_pairs={{0,32},{32,0},{1,33},{33,1},{2,34},{34,2},{3,35},{35,3},{4,36},{36... | collective-permute-start | bytes 6537224 | tf_op jit(solution)/shard_map/ppermute | solution.py:14
  181.1 55.5 %collective-permute-start.19 = (bf16[304,3584]{1,0:T(8,128)(2,1)}, bf16[304,3584]{1,0:T(8,128)(2,1)}, u32[]{:S(2)}, u32[]{:S(2)}) collective-permute-start(bf16[304,3584]{1,0:T(8,128)(2,1)} %convolution_convert_fusion), channel_id=1, source_target_pairs={{0,32},{32,0},{1,33},{33,1},{2,34},{34,2},{3,35},{35,3},{4,36},{36... | collective-permute-start | bytes 6537224 | tf_op jit(solution)/shard_map/ppermute | solution.py:14
  192.2 27.3 %all-to-all-start.3 = ((bf16[4,64,3584]{2,1,0:T(8,128)(2,1)}), bf16[4,64,3584]{2,1,0:T(8,128)(2,1)}, u32[]{:S(2)}, u32[]{:S(2)}) async-start(bf16[4,64,3584]{2,1,0:T(8,128)(2,1)} %bitcast.45), calls=%async_computation.3 | async-start | bytes 3670016 | tf_op jit(solution)/shard_map/all_to_all | solution.py:19
  204.8 25.9 %collective-permute-start.18 = (bf16[152,3584]{1,0:T(8,128)(2,1)}, bf16[152,3584]{1,0:T(8,128)(2,1)}, u32[]{:S(2)}, u32[]{:S(2)}) collective-permute-start(bf16[152,3584]{1,0:T(8,128)(2,1)} %add_convert_fusion.4), channel_id=1, source_target_pairs={{0,64},{64,0},{1,65},{65,1},{2,66},{66,2},{3,67},{67,3},{4,68},{68... | collective-permute-start | bytes 3268616 | tf_op jit(solution)/shard_map/ppermute | solution.py:14
  230.7 26.3 %all-to-all-start.4 = ((bf16[4,64,3584]{2,1,0:T(8,128)(2,1)}), bf16[4,64,3584]{2,1,0:T(8,128)(2,1)}, u32[]{:S(2)}, u32[]{:S(2)}) async-start(bf16[4,64,3584]{2,1,0:T(8,128)(2,1)} %bitcast.44), calls=%async_computation.4 | async-start | bytes 3670016 | tf_op jit(solution)/shard_map/all_to_all | solution.py:19
  236.2 24.8 %collective-permute-start.20 = (bf16[152,3584]{1,0:T(8,128)(2,1)}, bf16[152,3584]{1,0:T(8,128)(2,1)S(1)}, u32[]{:S(2)}, u32[]{:S(2)}) collective-permute-start(bf16[152,3584]{1,0:T(8,128)(2,1)} %add_convert_fusion.5), channel_id=1, source_target_pairs={{0,64},{64,0},{1,65},{65,1},{2,66},{66,2},{3,67},{67,3},{4,68},{68... | collective-permute-start | bytes 3268616 | tf_op jit(solution)/shard_map/ppermute | solution.py:14
  262.0 27.5 %all-to-all-start.5 = ((bf16[8,16,3584]{2,1,0:T(8,128)(2,1)}), bf16[8,16,3584]{2,1,0:T(8,128)(2,1)S(1)}, u32[]{:S(2)}, u32[]{:S(2)}) async-start(bf16[8,16,3584]{2,1,0:T(8,128)(2,1)} %pad_maximum_fusion), calls=%async_computation.5 | async-start | bytes 1835008 | tf_op jit(solution)/shard_map/all_to_all | solution.py:19
  269.0 24.2 %collective-permute-start.23 = (bf16[152,3584]{1,0:T(8,128)(2,1)}, bf16[152,3584]{1,0:T(8,128)(2,1)}, u32[]{:S(2)}, u32[]{:S(2)}) collective-permute-start(bf16[152,3584]{1,0:T(8,128)(2,1)} %add_convert_fusion.3), channel_id=1, source_target_pairs={{0,64},{64,0},{1,65},{65,1},{2,66},{66,2},{3,67},{67,3},{4,68},{68... | collective-permute-start | bytes 3268616 | tf_op jit(solution)/shard_map/ppermute | solution.py:14
  (34 other events, 280.5 us)

commit v4 on v3

v4 whole, which is shorter than its diff:
```python
import jax
import jax.numpy as jnp
from jax import lax
from jax.sharding import Mesh, PartitionSpec as P

BF = jnp.bfloat16
F32 = jnp.float32


def swap(value, axes):
    size = 1
    for axis in axes:
        size *= lax.axis_size(axis)
    return lax.ppermute(value, axes, [(i, size - 1 - i) for i in range(size)])


def scatter(part, axis):
    size = lax.axis_size(axis)
    landed = lax.all_to_all(part.reshape(size, -1, part.shape[1]), axis, 0, 0, tiled=True)
    return jnp.sum(landed.astype(F32), axis=0)


def in_order(data, mine, other):
    return jnp.where(data == 0, jnp.concatenate([mine, other], axis=0), jnp.concatenate([other, mine], axis=0))


def gather(block, axis):
    size = lax.axis_size(axis)
    wide = jnp.broadcast_to(block[None], (size,) + block.shape)
    return lax.all_to_all(wide, axis, 0, 0, tiled=True)


def join(parts):
    return jnp.concatenate(parts, axis=0)


def place(buffer, part, at):
    return lax.dynamic_update_slice_in_dim(buffer, part, at, axis=0)


def finish(part, data):
    rows = part.shape[0] // 2
    own = jnp.where(data == 0, part[:rows], part[rows:])
    other = swap(jnp.where(data == 0, part[rows:], part[:rows]), ("dp",))
    return jnp.where(
        data == 0, jnp.concatenate([own, other], axis=1), jnp.concatenate([other, own], axis=1)
    ).astype(BF)


def dot(left, right, dims):
    return lax.dot_general(left, right, (dims, ((), ())), preferred_element_type=F32)


def per_device(
    tokens, routes, route_gates, cotangent, dense_gate, dense_up, dense_down,
    expert_gate, expert_up, expert_down,
):
    width = expert_gate.shape[2]
    hidden = expert_gate.shape[1]
    data, near, core = (lax.axis_index(name) for name in ("dp", "xlo", "core"))
    rows = tokens.shape[0]
    depth = lax.axis_size("z")

    ids = jnp.arange(128, dtype=jnp.int32)
    weights_of = jnp.sum(
        jnp.where(routes[:, :, None] == ids[None, None, :], route_gates.astype(F32)[:, :, None], 0.0), axis=1
    ).astype(BF)
    marks = join([weights_of, jnp.zeros_like(weights_of)])

    def columns(at):
        both = lax.dynamic_slice_in_dim(join([tokens, cotangent]), at * width, width, axis=1)
        return jnp.concatenate([both, marks], axis=1)

    own, far = columns(data), swap(columns(1 - data), ("dp",))
    block = join([in_order(data, own[:rows], far[:rows]), in_order(data, own[rows:], far[rows:])])
    block = gather(block, "z").reshape(depth, 4 * rows, -1)

    gate, up, down = expert_gate[0], expert_up[0], expert_down[0]
    units = -(-5 * hidden // 128) * 128
    _, gate = lax.optimization_barrier((far, gate))
    gate_x = swap(gate, ("xlo",))

    def columns_of(dense):
        return lax.dynamic_slice_in_dim(dense, data * width, width, axis=1)

    def place_near(buffer, mine, dense, at):
        buffer = place(buffer, mine, at)
        buffer = place(buffer, swap(mine, ("core",)), at + 2 * hidden)
        return place(buffer, columns_of(dense), at + 4 * hidden)

    def place_far(buffer, theirs, at):
        buffer = place(buffer, theirs, at + hidden)
        return place(buffer, swap(theirs, ("core",)), at + 3 * hidden)

    pair = jnp.zeros((2 * units, width), BF)
    pair = place_near(place_near(pair, gate, dense_gate, 0), up, dense_up, units)
    last = place_near(jnp.zeros((units, width), BF), down, dense_down, 0)

    block, gate_x, pair, last, up = lax.optimization_barrier((block, gate_x, pair, last, up))
    up_x = swap(up, ("xlo",))
    tok = gather(block[:, :2 * rows].reshape(-1, block.shape[2]), "y").reshape(-1, block.shape[2])
    pair = place_far(pair, gate_x, 0)
    block, tok, up_x, down, pair = lax.optimization_barrier((block, tok, up_x, down, pair))
    down_x = swap(down, ("xlo",))
    cot = gather(block[:, 2 * rows:, :width].reshape(-1, width), "y").reshape(-1, width)
    pair = place_far(pair, up_x, units)

    weighting = tok[:, width:].astype(F32)
    tok = tok[:, :width]

    unit = jnp.arange(units, dtype=jnp.int32)[None]
    scale = jnp.ones((), F32)
    for at, chip, other in ((0, near, core), (1, 1 - near, core), (2, near, 1 - core), (3, 1 - near, 1 - core)):
        column = jnp.sum(
            jnp.where(ids[None] == chip * lax.axis_size("core") + other, weighting, 0.0), axis=1, keepdims=True
        )
        scale = jnp.where((unit >= at * hidden) & (unit < (at + 1) * hidden), column, scale)

    both = dot(tok, pair, ((1,), (1,))).astype(BF)
    both, down_x, cot = lax.optimization_barrier((both, down_x, cot))
    last = place_far(last, down_x, 0)
    dact = dot(cot, last, ((1,), (1,))).astype(BF)
    far_both, _ = lax.optimization_barrier((swap(both, ("dp",)), dact))
    both = both.astype(F32) + far_both.astype(F32)
    dact = dact.astype(F32) + swap(dact, ("dp",)).astype(F32)
    pre, lin = both[:, :units], both[:, units:]
    sig = jax.nn.sigmoid(pre)
    act = (pre * sig * lin * scale).astype(BF)
    gate_slope = lin * scale * (sig * (1.0 + pre * (1.0 - sig)))
    lin_slope = pre * sig * scale
    mixed = dot(act, last, ((1,), (0,))).astype(BF)

    def far_grads(left, right):
        ours = dot(left[:, :2 * hidden], right, ((0,), (0,))).astype(BF)
        theirs = swap(dot(left[:, 2 * hidden:4 * hidden], right, ((0,), (0,))).astype(BF), ("core",))
        return ours, theirs, (ours[hidden:].astype(F32) + theirs[hidden:].astype(F32)).astype(BF)

    def whole_grad(ours, theirs, far):
        return (ours[:hidden].astype(F32) + theirs[:hidden].astype(F32) + far.astype(F32)).astype(BF)[None]

    down_ours, down_theirs, down_far = far_grads(act, cot)
    mixed, down_far = lax.optimization_barrier((mixed, down_far))
    dact, _ = lax.optimization_barrier((dact, mixed))
    down_far = swap(down_far, ("xlo",))
    mixed = scatter(mixed, "y").astype(BF)
    slopes = jnp.concatenate([dact * gate_slope, dact * lin_slope], axis=1).astype(BF)
    grads = dot(slopes, pair, ((1,), (0,))).astype(BF)
    gate_ours, gate_theirs, gate_far = far_grads(slopes[:, :units], tok)
    grads, gate_far, mixed, down_far = lax.optimization_barrier((grads, gate_far, mixed, down_far))
    gate_far = swap(gate_far, ("xlo",))
    grads = scatter(grads, "y").astype(BF)
    up_ours, up_theirs, up_far = far_grads(slopes[:, units:], tok)
    both = jnp.concatenate([part.reshape(depth, 2 * rows, width) for part in (mixed, grads)], axis=1)
    both, up_far, gate_far = lax.optimization_barrier((both, up_far, gate_far))
    up_far = swap(up_far, ("xlo",))
    both = scatter(both.reshape(-1, width), "z")
    mixed, grads = finish(both[:2 * rows], data), finish(both[2 * rows:], data)
    return (
        mixed,
        grads,
        whole_grad(gate_ours, gate_theirs, gate_far),
        whole_grad(up_ours, up_theirs, up_far),
        whole_grad(down_ours, down_theirs, down_far),
    )


def solution(mesh):
    fine = Mesh(mesh.devices.reshape(2, 2, 2, 8, 4), ("dp", "xlo", "core", "z", "y"))
    every = ("dp", "xlo", "core", "z", "y")
    row = P(every, None)
    dense = P(("z", "y"), None)
    expert = P(("xlo", "core"), ("z", "y"), "dp")
    return jax.shard_map(
        per_device,
        mesh=fine,
        in_specs=(row, row, row, row, dense, dense, dense, expert, expert, expert),
        out_specs=(row, row, expert, expert, expert),
        check_vma=False,
    )
```

time: 304 us -> 270 us (0.89)
  waiting for transfers between devices: 148 us -> 118 us
  local copies, waits for them, and re-layouts: 13.8 us -> 37.6 us
  matrix products: 50.5 us -> 36.2 us
  other arithmetic: 36.9 us -> 26.9 us
  starting transfers between devices: 52.5 us -> 49.1 us
    dynamic_update_slice x0 -> x15, local copies, waits for them, and re-layouts: none -> 33 us  [place(): return lax.dynamic_update_slice_in_dim(buffer, part, at, axis=0)]
    ppermute x24 -> x20, waiting for transfers between devices: 87.4 us -> 62.7 us  [swap(): return lax.ppermute(value, axes, [(i, size - 1 - i) for i in range(size)])]
    dot_general x18 -> x10, matrix products: 50.5 us -> 36.2 us  [dot(): lax.dot_general(left, right, (dims, ((), ())), preferred_element_type=F32)]
    add x3 -> x2, other arithmetic: 8.91 us -> 0.29 us  [the longest x1 0.21 us: per_device(): both = both.astype(F32) + far_both.astype(F32)]
    all_to_all x3, waiting for transfers between devices: 16.3 us -> 10.5 us  [gather(): return lax.all_to_all(wide, axis, 0, 0, tiled=True)]
    ppermute x24 -> x20, starting transfers between devices: 21 us -> 16.8 us  [swap(): return lax.ppermute(value, axes, [(i, size - 1 - i) for i in range(size)])]
    unnamed x56 -> x24, local copies, waits for them, and re-layouts: 4.91 us -> 0.71 us
  transfers between devices with their start and end apart: 30 -> 26, of which waited for: 15 -> 12; matrix products, arithmetic and copies ran while one was open for 30% -> 33% of each run, Pallas kernels for 0% -> 0%
where the time goes in v4:
time: 270 us; the launch traced here: 269 us
  waiting for transfers between devices  118 us (44%)
  starting transfers between devices  49.1 us (18%)
  local copies, waits for them, and re-layouts  37.6 us (14%)
  matrix products  36.2 us (13%)
  other arithmetic  26.9 us (10%)
    ppermute x20, waiting for transfers between devices, swap(): return lax.ppermute(value, axes, [(i, size - 1 - i) for i in range(size)])  62.7 us
    all_to_all x3, waiting for transfers between devices, scatter(): lax.all_to_all(part.reshape(size, -1, part.shape[1]), axis, 0, 0, tiled=T...  44.8 us
    dot_general x10, matrix products, dot(): lax.dot_general(left, right, (dims, ((), ())), preferred_element_type=F32)  36.2 us
    dynamic_update_slice x15, local copies, waits for them, and re-layouts, place(): return lax.dynamic_update_slice_in_dim(buffer, part, at, axis=0)  33 us
    all_to_all x3, starting transfers between devices, gather(): return lax.all_to_all(wide, axis, 0, 0, tiled=True)  18.2 us
    ppermute x20, starting transfers between devices, swap(): return lax.ppermute(value, axes, [(i, size - 1 - i) for i in range(size)])  16.8 us
    all_to_all x3, starting transfers between devices, scatter(): lax.all_to_all(part.reshape(size, -1, part.shape[1]), axis, 0, 0, tiled=T...  14.2 us
    all_to_all x3, waiting for transfers between devices, gather(): return lax.all_to_all(wide, axis, 0, 0, tiled=True)  10.5 us
  transfers between devices with their start and end apart: 26, of which 12 were waited for; matrix products, arithmetic and copies ran while one was open for 33% of the time, Pallas kernels for 0%

profile of v4, /device:TPU:8, one launch (start us, length us, event | category | flops | bytes accessed | tf_op | source)
XLA Modules:
  0.0 268.7 jit_solution(170011394347199053)
XLA Ops:
  3.0 3.1 %collective-permute-start = (bf16[8,3712]{1,0:T(8,128)(2,1)S(1)}, bf16[8,3712]{1,0:T(8,128)(2,1)S(1)}, u32[]{:S(2)}, u32[]{:S(2)}) collective-permute-start(bf16[8,3712]{1,0:T(8,128)(2,1)S(1)} %get-tuple-element.72), channel_id=1, source_target_pairs={{0,128},{128,0},{1,129},{129,1},{2,130},{130,2},{3,131},{131,3},{4... | collective-permute-start | bytes 178184 | tf_op jit(solution)/shard_map/ppermute | solution.py:14
  6.6 4.0 %dynamic_update_slice.51 = bf16[768,3584]{1,0:T(8,128)(2,1)} pad(bf16[152,3584]{1,0:T(8,128)(2,1)} %bitcast.41, bf16[]{:T(256)} %constant.27.clone.1), padding=0_616x0_0 | pad | bytes 6594562 | tf_op jit(solution)/shard_map/dynamic_update_slice | solution.py:38
  10.6 6.2 %dynamic_update_slice.45 = bf16[1536,3584]{1,0:T(8,128)(2,1)} pad(bf16[152,3584]{1,0:T(8,128)(2,1)} %bitcast, bf16[]{:T(256)} %constant.27.clone.1), padding=0_1384x0_0 | pad | bytes 12099586 | tf_op jit(solution)/shard_map/dynamic_update_slice | solution.py:38
  18.5 8.5 %all-to-all-start = ((bf16[8,16,3712]{2,1,0:T(8,128)(2,1)}), bf16[8,16,3712]{2,1,0:T(8,128)(2,1)S(1)}, u32[]{:S(2)}, u32[]{:S(2)}) async-start(bf16[8,16,3712]{2,1,0:T(8,128)(2,1)} %broadcast_in_dim.142), calls=%async_computation | async-start | bytes 1900544 | tf_op jit(solution)/shard_map/all_to_all | solution.py:30
  37.3 6.2 %collective-permute-done.1 = bf16[152,3584]{1,0:T(8,128)(2,1)} collective-permute-done((bf16[152,3584]{1,0:T(8,128)(2,1)}, bf16[152,3584]{1,0:T(8,128)(2,1)}, u32[]{:S(2)}, u32[]{:S(2)}) %collective-permute-start.1) | collective-permute-done | bytes 1089568 | tf_op jit(solution)/shard_map/ppermute | solution.py:14
  43.5 10.5 %all-to-all-done = bf16[8,16,3712]{2,1,0:T(8,128)(2,1)S(1)} async-done(((bf16[8,16,3712]{2,1,0:T(8,128)(2,1)}), bf16[8,16,3712]{2,1,0:T(8,128)(2,1)S(1)}, u32[]{:S(2)}, u32[]{:S(2)}) %all-to-all-start) | async-done | bytes 950304 | tf_op jit(solution)/shard_map/all_to_all | solution.py:30
  55.5 4.9 %all-to-all-start.1 = ((bf16[4,64,3712]{2,1,0:T(8,128)(2,1)}), bf16[4,64,3712]{2,1,0:T(8,128)(2,1)S(1)}, u32[]{:S(2)}, u32[]{:S(2)}) async-start(bf16[4,64,3712]{2,1,0:T(8,128)(2,1)} %broadcast_in_dim.144), calls=%async_computation.1 | async-start | bytes 3801088 | tf_op jit(solution)/shard_map/all_to_all | solution.py:30
  66.4 20.1 %collective-permute-done.5 = bf16[152,3584]{1,0:T(8,128)(2,1)} collective-permute-done((bf16[152,3584]{1,0:T(8,128)(2,1)}, bf16[152,3584]{1,0:T(8,128)(2,1)}, u32[]{:S(2)}, u32[]{:S(2)}) %collective-permute-start.5) | collective-permute-done | bytes 1089568 | tf_op jit(solution)/shard_map/ppermute | solution.py:14
  88.0 4.8 %all-to-all-start.2 = ((bf16[4,64,3584]{2,1,0:T(8,128)(2,1)}), bf16[4,64,3584]{2,1,0:T(8,128)(2,1)}, u32[]{:S(2)}, u32[]{:S(2)}) async-start(bf16[4,64,3584]{2,1,0:T(8,128)(2,1)} %broadcast_in_dim.146), calls=%async_computation.2 | async-start | bytes 3670016 | tf_op jit(solution)/shard_map/all_to_all | solution.py:30
  98.8 8.0 %convolution_convert_fusion.8 = bf16[256,1536]{1,0:T(8,128)(2,1)} fusion(bf16[1536,3584]{1,0:T(8,128)(2,1)} %constant_dynamic-update-slice_fusion.9, bf16[256,3712]{1,0:T(8,128)(2,1)S(1)} %bitcast.28), kind=kOutput, calls=%fused_computation.8 | convolution fusion | flops 2818965504 | bytes 13631488 | tf_op jit(solution)/shard_map/dot_general | solution.py:51
  106.9 12.3 %collective-permute-done.8 = bf16[152,3584]{1,0:T(8,128)(2,1)S(1)} collective-permute-done((bf16[152,3584]{1,0:T(8,128)(2,1)}, bf16[152,3584]{1,0:T(8,128)(2,1)S(1)}, u32[]{:S(2)}, u32[]{:S(2)}) %collective-permute-start.8) | collective-permute-done | bytes 1089568 | tf_op jit(solution)/shard_map/ppermute | solution.py:14
  125.0 4.8 %convolution_convert_fusion.9 = bf16[256,768]{1,0:T(8,128)(2,1)S(1)} fusion(bf16[256,3584]{1,0:T(8,128)(2,1)} %bitcast.6, bf16[768,3584]{1,0:T(8,128)(2,1)} %constant_dynamic-update-slice_fusion.6), kind=kOutput, calls=%fused_computation.17 | convolution fusion | flops 1409482752 | bytes 7733248 | tf_op jit(solution)/shard_map/dot_general | solution.py:51
  129.8 11.4 %collective-permute-done.11 = bf16[256,1536]{1,0:T(8,128)(2,1)S(1)} collective-permute-done((bf16[256,1536]{1,0:T(8,128)(2,1)}, bf16[256,1536]{1,0:T(8,128)(2,1)S(1)}, u32[]{:S(2)}, u32[]{:S(2)}) %collective-permute-start.11) | collective-permute-done | bytes 786464 | tf_op jit(solution)/shard_map/ppermute | solution.py:14
  152.1 5.8 %collective-permute-done.10 = bf16[256,768]{1,0:T(8,128)(2,1)S(1)} collective-permute-done((bf16[256,768]{1,0:T(8,128)(2,1)S(1)}, bf16[256,768]{1,0:T(8,128)(2,1)S(1)}, u32[]{:S(2)}, u32[]{:S(2)}) %collective-permute-start.10) | collective-permute-done | bytes 393248 | tf_op jit(solution)/shard_map/ppermute | solution.py:14
  164.4 4.8 %all-to-all-start.3 = ((bf16[4,64,3584]{2,1,0:T(8,128)(2,1)}), bf16[4,64,3584]{2,1,0:T(8,128)(2,1)}, u32[]{:S(2)}, u32[]{:S(2)}) async-start(bf16[4,64,3584]{2,1,0:T(8,128)(2,1)} %bitcast.36), calls=%async_computation.3 | async-start | bytes 3670016 | tf_op jit(solution)/shard_map/all_to_all | solution.py:19
  171.4 8.3 %convolution_convert_fusion.7 = bf16[256,3584]{1,0:T(8,128)(2,1)} fusion(bf16[1536,3584]{1,0:T(8,128)(2,1)} %constant_dynamic-update-slice_fusion.9, bf16[256,768]{1,0:T(8,128)(2,1)S(1)} %get-tuple-element.60, bf16[256,768]{1,0:T(8,128)(2,1)S(1)} %get-tuple-element.59), kind=kOutput, calls=%fused_computation.7 | convolution fusion | flops 2821062656 | bytes 13631488 | tf_op jit(solution)/shard_map/dot_general | solution.py:51
  181.8 10.1 %all-to-all-done.3 = bf16[4,64,3584]{2,1,0:T(8,128)(2,1)} async-done(((bf16[4,64,3584]{2,1,0:T(8,128)(2,1)}), bf16[4,64,3584]{2,1,0:T(8,128)(2,1)}, u32[]{:S(2)}, u32[]{:S(2)}) %all-to-all-start.3) | async-done | bytes 1835040 | tf_op jit(solution)/shard_map/all_to_all | solution.py:19
  196.6 5.8 %all-to-all-start.4 = ((bf16[4,64,3584]{2,1,0:T(8,128)(2,1)}), bf16[4,64,3584]{2,1,0:T(8,128)(2,1)}, u32[]{:S(2)}, u32[]{:S(2)}) async-start(bf16[4,64,3584]{2,1,0:T(8,128)(2,1)} %bitcast.37), calls=%async_computation.4 | async-start | bytes 3670016 | tf_op jit(solution)/shard_map/all_to_all | solution.py:19
  207.0 17.2 %all-to-all-done.4 = bf16[4,64,3584]{2,1,0:T(8,128)(2,1)} async-done(((bf16[4,64,3584]{2,1,0:T(8,128)(2,1)}), bf16[4,64,3584]{2,1,0:T(8,128)(2,1)}, u32[]{:S(2)}, u32[]{:S(2)}) %all-to-all-start.4) | async-done | bytes 1835040 | tf_op jit(solution)/shard_map/all_to_all | solution.py:19
  228.5 3.6 %all-to-all-start.5 = ((bf16[8,16,3584]{2,1,0:T(8,128)(2,1)}), bf16[8,16,3584]{2,1,0:T(8,128)(2,1)S(1)}, u32[]{:S(2)}, u32[]{:S(2)}) async-start(bf16[8,16,3584]{2,1,0:T(8,128)(2,1)} %pad_maximum_fusion), calls=%async_computation.5 | async-start | bytes 1835008 | tf_op jit(solution)/shard_map/all_to_all | solution.py:19
  232.0 3.1 %fusion.2 = bf16[1,152,3584]{2,1,0:T(8,128)(2,1)} fusion(bf16[152,3584]{1,0:T(8,128)(2,1)} %collective-permute-done.14, bf16[304,3584]{1,0:T(8,128)(2,1)} %copy-done.6, bf16[304,3584]{1,0:T(8,128)(2,1)S(1)} %copy-done.4), kind=kLoop, calls=%fused_computation.20 | loop fusion | flops 3268608 | bytes 4358144 | tf_op jit(solution)/shard_map/broadcast_in_dim | solution.py:139
  235.7 3.1 %fusion = bf16[1,152,3584]{2,1,0:T(8,128)(2,1)} fusion(bf16[152,3584]{1,0:T(8,128)(2,1)} %collective-permute-done.16, bf16[304,3584]{1,0:T(8,128)(2,1)} %collective-permute-done.13, bf16[304,3584]{1,0:T(8,128)(2,1)S(1)} %copy-done.2), kind=kLoop, calls=%fused_computation.18 | loop fusion | flops 3268608 | bytes 4358144 | tf_op jit(solution)/shard_map/broadcast_in_dim | solution.py:139
  238.8 17.5 %all-to-all-done.5 = bf16[8,16,3584]{2,1,0:T(8,128)(2,1)S(1)} async-done(((bf16[8,16,3584]{2,1,0:T(8,128)(2,1)}), bf16[8,16,3584]{2,1,0:T(8,128)(2,1)S(1)}, u32[]{:S(2)}, u32[]{:S(2)}) %all-to-all-start.5) | async-done | bytes 917536 | tf_op jit(solution)/shard_map/all_to_all | solution.py:19
  264.5 3.5 %collective-permute-done.17 = bf16[4,3584]{1,0:T(4,128)(2,1)S(1)} collective-permute-done((bf16[4,3584]{1,0:T(4,128)(2,1)S(1)}, bf16[4,3584]{1,0:T(4,128)(2,1)S(1)}, u32[]{:S(2)}, u32[]{:S(2)}) %collective-permute-start.17) | collective-permute-done | bytes 28704 | tf_op jit(solution)/shard_map/ppermute | solution.py:14
  (112 shorter events, 80.2 us)
Async XLA Ops:
  3.0 7.6 %collective-permute-start = (bf16[8,3712]{1,0:T(8,128)(2,1)S(1)}, bf16[8,3712]{1,0:T(8,128)(2,1)S(1)}, u32[]{:S(2)}, u32[]{:S(2)}) collective-permute-start(bf16[8,3712]{1,0:T(8,128)(2,1)S(1)} %get-tuple-element.72), channel_id=1, source_target_pairs={{0,128},{128,0},{1,129},{129,1},{2,130},{130,2},{3,131},{131,3},{4... | collective-permute-start | bytes 178184 | tf_op jit(solution)/shard_map/ppermute | solution.py:14
  6.1 29.0 %collective-permute-start.3 = (bf16[152,3584]{1,0:T(8,128)(2,1)}, bf16[152,3584]{1,0:T(8,128)(2,1)S(1)}, u32[]{:S(2)}, u32[]{:S(2)}) collective-permute-start(bf16[152,3584]{1,0:T(8,128)(2,1)} %bitcast.38), channel_id=1, source_target_pairs={{0,32},{32,0},{1,33},{33,1},{2,34},{34,2},{3,35},{35,3},{4,36},{36... | collective-permute-start | bytes 3268616 | tf_op jit(solution)/shard_map/ppermute | solution.py:14
  6.1 20.9 %collective-permute-start.4 = (bf16[152,3584]{1,0:T(8,128)(2,1)}, bf16[152,3584]{1,0:T(8,128)(2,1)}, u32[]{:S(2)}, u32[]{:S(2)}) collective-permute-start(bf16[152,3584]{1,0:T(8,128)(2,1)} %bitcast.40), channel_id=1, source_target_pairs={{0,32},{32,0},{1,33},{33,1},{2,34},{34,2},{3,35},{35,3},{4,36},{36... | collective-permute-start | bytes 3268616 | tf_op jit(solution)/shard_map/ppermute | solution.py:14
  16.8 13.8 %collective-permute-start.2 = (bf16[152,3584]{1,0:T(8,128)(2,1)}, bf16[152,3584]{1,0:T(8,128)(2,1)}, u32[]{:S(2)}, u32[]{:S(2)}) collective-permute-start(bf16[152,3584]{1,0:T(8,128)(2,1)} %bitcast), channel_id=1, source_target_pairs={{0,32},{32,0},{1,33},{33,1},{2,34},{34,2},{3,35},{35,3},{4,36},{36... | collective-permute-start | bytes 3268616 | tf_op jit(solution)/shard_map/ppermute | solution.py:14
  16.8 26.8 %collective-permute-start.1 = (bf16[152,3584]{1,0:T(8,128)(2,1)}, bf16[152,3584]{1,0:T(8,128)(2,1)}, u32[]{:S(2)}, u32[]{:S(2)}) collective-permute-start(bf16[152,3584]{1,0:T(8,128)(2,1)} %bitcast), channel_id=1, source_target_pairs={{0,64},{64,0},{1,65},{65,1},{2,66},{66,2},{3,67},{67,3},{4,68},{68... | collective-permute-start | bytes 3268616 | tf_op jit(solution)/shard_map/ppermute | solution.py:14
  18.5 35.5 %all-to-all-start = ((bf16[8,16,3712]{2,1,0:T(8,128)(2,1)}), bf16[8,16,3712]{2,1,0:T(8,128)(2,1)S(1)}, u32[]{:S(2)}, u32[]{:S(2)}) async-start(bf16[8,16,3712]{2,1,0:T(8,128)(2,1)} %broadcast_in_dim.142), calls=%async_computation | async-start | bytes 1900544 | tf_op jit(solution)/shard_map/all_to_all | solution.py:30
  54.0 10.1 %collective-permute-start.6 = (bf16[152,3584]{1,0:T(8,128)(2,1)}, bf16[152,3584]{1,0:T(8,128)(2,1)}, u32[]{:S(2)}, u32[]{:S(2)}) collective-permute-start(bf16[152,3584]{1,0:T(8,128)(2,1)} %collective-permute-done.1), channel_id=1, source_target_pairs={{0,32},{32,0},{1,33},{33,1},{2,34},{34,2},{3,35},{35,3},{4,36},{36... | collective-permute-start | bytes 3268616 | tf_op jit(solution)/shard_map/ppermute | solution.py:14
  55.5 31.1 %all-to-all-start.1 = ((bf16[4,64,3712]{2,1,0:T(8,128)(2,1)}), bf16[4,64,3712]{2,1,0:T(8,128)(2,1)S(1)}, u32[]{:S(2)}, u32[]{:S(2)}) async-start(bf16[4,64,3712]{2,1,0:T(8,128)(2,1)} %broadcast_in_dim.144), calls=%async_computation.1 | async-start | bytes 3801088 | tf_op jit(solution)/shard_map/all_to_all | solution.py:30
  60.4 26.2 %collective-permute-start.5 = (bf16[152,3584]{1,0:T(8,128)(2,1)}, bf16[152,3584]{1,0:T(8,128)(2,1)}, u32[]{:S(2)}, u32[]{:S(2)}) collective-permute-start(bf16[152,3584]{1,0:T(8,128)(2,1)} %bitcast.39), channel_id=1, source_target_pairs={{0,64},{64,0},{1,65},{65,1},{2,66},{66,2},{3,67},{67,3},{4,68},{68... | collective-permute-start | bytes 3268616 | tf_op jit(solution)/shard_map/ppermute | solution.py:14
  86.6 9.9 %collective-permute-start.7 = (bf16[152,3584]{1,0:T(8,128)(2,1)}, bf16[152,3584]{1,0:T(8,128)(2,1)}, u32[]{:S(2)}, u32[]{:S(2)}) collective-permute-start(bf16[152,3584]{1,0:T(8,128)(2,1)} %collective-permute-done.5), channel_id=1, source_target_pairs={{0,32},{32,0},{1,33},{33,1},{2,34},{34,2},{3,35},{35,3},{4,36},{36... | collective-permute-start | bytes 3268616 | tf_op jit(solution)/shard_map/ppermute | solution.py:14
  88.0 31.1 %all-to-all-start.2 = ((bf16[4,64,3584]{2,1,0:T(8,128)(2,1)}), bf16[4,64,3584]{2,1,0:T(8,128)(2,1)}, u32[]{:S(2)}, u32[]{:S(2)}) async-start(bf16[4,64,3584]{2,1,0:T(8,128)(2,1)} %broadcast_in_dim.146), calls=%async_computation.2 | async-start | bytes 3670016 | tf_op jit(solution)/shard_map/all_to_all | solution.py:30
  92.8 26.3 %collective-permute-start.8 = (bf16[152,3584]{1,0:T(8,128)(2,1)}, bf16[152,3584]{1,0:T(8,128)(2,1)S(1)}, u32[]{:S(2)}, u32[]{:S(2)}) collective-permute-start(bf16[152,3584]{1,0:T(8,128)(2,1)} %bitcast.42), channel_id=1, source_target_pairs={{0,64},{64,0},{1,65},{65,1},{2,66},{66,2},{3,67},{67,3},{4,68},{68... | collective-permute-start | bytes 3268616 | tf_op jit(solution)/shard_map/ppermute | solution.py:14
  119.3 21.9 %collective-permute-start.11 = (bf16[256,1536]{1,0:T(8,128)(2,1)}, bf16[256,1536]{1,0:T(8,128)(2,1)S(1)}, u32[]{:S(2)}, u32[]{:S(2)}) collective-permute-start(bf16[256,1536]{1,0:T(8,128)(2,1)} %convolution_convert_fusion.8), channel_id=1, source_target_pairs={{0,128},{128,0},{1,129},{129,1},{2,130},{130,2},{3,131},{131,3},{4... | collective-permute-start | bytes 2359304 | tf_op jit(solution)/shard_map/ppermute | solution.py:14
  144.7 13.2 %collective-permute-start.12 = (bf16[304,3584]{1,0:T(8,128)(2,1)S(1)}, bf16[304,3584]{1,0:T(8,128)(2,1)S(1)}, u32[]{:S(2)}, u32[]{:S(2)}) collective-permute-start(bf16[304,3584]{1,0:T(8,128)(2,1)S(1)} %convolution_convert_fusion.4), channel_id=1, source_target_pairs={{0,32},{32,0},{1,33},{33,1},{2,34},{34,2},{3,35},{35,3},{4,36},{36... | collective-permute-start | bytes 6537224 | tf_op jit(solution)/shard_map/ppermute | solution.py:14
  144.8 13.0 %collective-permute-start.10 = (bf16[256,768]{1,0:T(8,128)(2,1)S(1)}, bf16[256,768]{1,0:T(8,128)(2,1)S(1)}, u32[]{:S(2)}, u32[]{:S(2)}) collective-permute-start(bf16[256,768]{1,0:T(8,128)(2,1)S(1)} %convolution_convert_fusion.9), channel_id=1, source_target_pairs={{0,128},{128,0},{1,129},{129,1},{2,130},{130,2},{3,131},{131,3},{4... | collective-permute-start | bytes 1179656 | tf_op jit(solution)/shard_map/ppermute | solution.py:14
  163.0 30.8 %collective-permute-start.13 = (bf16[304,3584]{1,0:T(8,128)(2,1)}, bf16[304,3584]{1,0:T(8,128)(2,1)}, u32[]{:S(2)}, u32[]{:S(2)}) collective-permute-start(bf16[304,3584]{1,0:T(8,128)(2,1)} %convolution_convert_fusion.2), channel_id=1, source_target_pairs={{0,32},{32,0},{1,33},{33,1},{2,34},{34,2},{3,35},{35,3},{4,36},{36... | collective-permute-start | bytes 6537224 | tf_op jit(solution)/shard_map/ppermute | solution.py:14
  163.0 33.6 %collective-permute-start.14 = (bf16[152,3584]{1,0:T(8,128)(2,1)}, bf16[152,3584]{1,0:T(8,128)(2,1)}, u32[]{:S(2)}, u32[]{:S(2)}) collective-permute-start(bf16[152,3584]{1,0:T(8,128)(2,1)} %add_convert_fusion.5), channel_id=1, source_target_pairs={{0,64},{64,0},{1,65},{65,1},{2,66},{66,2},{3,67},{67,3},{4,68},{68... | collective-permute-start | bytes 3268616 | tf_op jit(solution)/shard_map/ppermute | solution.py:14
  164.4 27.5 %all-to-all-start.3 = ((bf16[4,64,3584]{2,1,0:T(8,128)(2,1)}), bf16[4,64,3584]{2,1,0:T(8,128)(2,1)}, u32[]{:S(2)}, u32[]{:S(2)}) async-start(bf16[4,64,3584]{2,1,0:T(8,128)(2,1)} %bitcast.36), calls=%async_computation.3 | async-start | bytes 3670016 | tf_op jit(solution)/shard_map/all_to_all | solution.py:19
  171.4 32.4 %collective-permute-start.15 = (bf16[304,3584]{1,0:T(8,128)(2,1)}, bf16[304,3584]{1,0:T(8,128)(2,1)}, u32[]{:S(2)}, u32[]{:S(2)}) collective-permute-start(bf16[304,3584]{1,0:T(8,128)(2,1)} %convolution_convert_fusion), channel_id=1, source_target_pairs={{0,32},{32,0},{1,33},{33,1},{2,34},{34,2},{3,35},{35,3},{4,36},{36... | collective-permute-start | bytes 6537224 | tf_op jit(solution)/shard_map/ppermute | solution.py:14
  196.6 27.7 %all-to-all-start.4 = ((bf16[4,64,3584]{2,1,0:T(8,128)(2,1)}), bf16[4,64,3584]{2,1,0:T(8,128)(2,1)}, u32[]{:S(2)}, u32[]{:S(2)}) async-start(bf16[4,64,3584]{2,1,0:T(8,128)(2,1)} %bitcast.37), calls=%async_computation.4 | async-start | bytes 3670016 | tf_op jit(solution)/shard_map/all_to_all | solution.py:19
  203.1 25.3 %collective-permute-start.16 = (bf16[152,3584]{1,0:T(8,128)(2,1)}, bf16[152,3584]{1,0:T(8,128)(2,1)}, u32[]{:S(2)}, u32[]{:S(2)}) collective-permute-start(bf16[152,3584]{1,0:T(8,128)(2,1)} %add_convert_fusion.4), channel_id=1, source_target_pairs={{0,64},{64,0},{1,65},{65,1},{2,66},{66,2},{3,67},{67,3},{4,68},{68... | collective-permute-start | bytes 3268616 | tf_op jit(solution)/shard_map/ppermute | solution.py:14
  228.5 27.9 %all-to-all-start.5 = ((bf16[8,16,3584]{2,1,0:T(8,128)(2,1)}), bf16[8,16,3584]{2,1,0:T(8,128)(2,1)S(1)}, u32[]{:S(2)}, u32[]{:S(2)}) async-start(bf16[8,16,3584]{2,1,0:T(8,128)(2,1)} %pad_maximum_fusion), calls=%async_computation.5 | async-start | bytes 1835008 | tf_op jit(solution)/shard_map/all_to_all | solution.py:19
  235.1 24.6 %collective-permute-start.19 = (bf16[152,3584]{1,0:T(8,128)(2,1)}, bf16[152,3584]{1,0:T(8,128)(2,1)}, u32[]{:S(2)}, u32[]{:S(2)}) collective-permute-start(bf16[152,3584]{1,0:T(8,128)(2,1)} %add_convert_fusion.3), channel_id=1, source_target_pairs={{0,64},{64,0},{1,65},{65,1},{2,66},{66,2},{3,67},{67,3},{4,68},{68... | collective-permute-start | bytes 3268616 | tf_op jit(solution)/shard_map/ppermute | solution.py:14
  256.5 7.3 %collective-permute-start.18 = (bf16[4,3584]{1,0:T(4,128)(2,1)S(1)}, bf16[4,3584]{1,0:T(4,128)(2,1)S(1)}, u32[]{:S(2)}, u32[]{:S(2)}) collective-permute-start(bf16[4,3584]{1,0:T(4,128)(2,1)S(1)} %get-tuple-element.62), channel_id=1, source_target_pairs={{0,128},{128,0},{1,129},{129,1},{2,130},{130,2},{3,131},{131,3},{4... | collective-permute-start | bytes 86024 | tf_op jit(solution)/shard_map/ppermute | solution.py:14
  (14 other events, 88.1 us)

commit v5 on v4

--- a/solution.py
+++ b/solution.py
@@ -72,13 +72,14 @@
         return jnp.concatenate([both, marks], axis=1)
 
     own, far = columns(data), swap(columns(1 - data), ("dp",))
-    block = join([in_order(data, own[:rows], far[:rows]), in_order(data, own[rows:], far[rows:])])
-    block = gather(block, "z").reshape(depth, 4 * rows, -1)
+    tok = in_order(data, own[:rows], far[:rows])
+    cot = in_order(data, own[rows:, :width], far[rows:, :width])
+    tok = gather(tok, "z").reshape(-1, tok.shape[1])
 
     gate, up, down = expert_gate[0], expert_up[0], expert_down[0]
     units = -(-5 * hidden // 128) * 128
-    _, gate = lax.optimization_barrier((far, gate))
-    gate_x = swap(gate, ("xlo",))
+    _, gate_late = lax.optimization_barrier((far, gate))
+    gate_x = swap(gate_late, ("xlo",))
 
     def columns_of(dense):
         return lax.dynamic_slice_in_dim(dense, data * width, width, axis=1)
@@ -94,15 +95,15 @@
 
     pair = jnp.zeros((2 * units, width), BF)
     pair = place_near(place_near(pair, gate, dense_gate, 0), up, dense_up, units)
+
+    tok, gate_x, pair, up, down = lax.optimization_barrier((tok, gate_x, pair, up, down))
+    up_x = swap(up, ("xlo",))
+    tok = gather(tok, "y").reshape(-1, tok.shape[1])
+    pair = place_far(pair, gate_x, 0)
     last = place_near(jnp.zeros((units, width), BF), down, dense_down, 0)
-
-    block, gate_x, pair, last, up = lax.optimization_barrier((block, gate_x, pair, last, up))
-    up_x = swap(up, ("xlo",))
-    tok = gather(block[:, :2 * rows].reshape(-1, block.shape[2]), "y").reshape(-1, block.shape[2])
-    pair = place_far(pair, gate_x, 0)
-    block, tok, up_x, down, pair = lax.optimization_barrier((block, tok, up_x, down, pair))
+    cot, tok, up_x, down, pair, last = lax.optimization_barrier((cot, tok, up_x, down, pair, last))
     down_x = swap(down, ("xlo",))
-    cot = gather(block[:, 2 * rows:, :width].reshape(-1, width), "y").reshape(-1, width)
+    cot = gather(gather(cot, "z").reshape(-1, width), "y").reshape(-1, width)
     pair = place_far(pair, up_x, units)
 
     weighting = tok[:, width:].astype(F32)
@@ -117,12 +118,10 @@
         scale = jnp.where((unit >= at * hidden) & (unit < (at + 1) * hidden), column, scale)
 
     both = dot(tok, pair, ((1,), (1,))).astype(BF)
-    both, down_x, cot = lax.optimization_barrier((both, down_x, cot))
+    both, down_x = lax.optimization_barrier((both, down_x))
     last = place_far(last, down_x, 0)
     dact = dot(cot, last, ((1,), (1,))).astype(BF)
-    far_both, _ = lax.optimization_barrier((swap(both, ("dp",)), dact))
-    both = both.astype(F32) + far_both.astype(F32)
-    dact = dact.astype(F32) + swap(dact, ("dp",)).astype(F32)
+    both = both.astype(F32) + swap(both, ("dp",)).astype(F32)
     pre, lin = both[:, :units], both[:, units:]
     sig = jax.nn.sigmoid(pre)
     act = (pre * sig * lin * scale).astype(BF)
@@ -140,7 +139,8 @@
 
     down_ours, down_theirs, down_far = far_grads(act, cot)
     mixed, down_far = lax.optimization_barrier((mixed, down_far))
-    dact, _ = lax.optimization_barrier((dact, mixed))
+    far_dact, _ = lax.optimization_barrier((swap(dact, ("dp",)), mixed))
+    dact = dact.astype(F32) + far_dact.astype(F32)
     down_far = swap(down_far, ("xlo",))
     mixed = scatter(mixed, "y").astype(BF)
     slopes = jnp.concatenate([dact * gate_slope, dact * lin_slope], axis=1).astype(BF)

time: 270 us -> 286 us (1.059)
  starting transfers between devices: 49.1 us -> 61.9 us
  waiting for transfers between devices: 118 us -> 121 us
    all_to_all x3 -> x4, starting transfers between devices: 18.2 us -> 25 us  [gather(): return lax.all_to_all(wide, axis, 0, 0, tiled=True)]
    all_to_all x3, starting transfers between devices: 14.2 us -> 18.4 us  [scatter(): lax.all_to_all(part.reshape(size, -1, part.shape[1]), axis, 0, 0, tiled=T...]
    dynamic_update_slice x15, local copies, waits for them, and re-layouts: 33 us -> 29.4 us  [place(): return lax.dynamic_update_slice_in_dim(buffer, part, at, axis=0)]
    all_to_all x3 -> x4, waiting for transfers between devices: 10.5 us -> 12.1 us  [gather(): return lax.all_to_all(wide, axis, 0, 0, tiled=True)]
  transfers between devices with their start and end apart: 26 -> 27, of which waited for: 12 -> 13; matrix products, arithmetic and copies ran while one was open for 33% -> 32% of each run, Pallas kernels for 0% -> 0%
where the time goes in v5:
time: 286 us; the launch traced here: 285 us
  waiting for transfers between devices  121 us (42%)
  starting transfers between devices  61.9 us (22%)
  local copies, waits for them, and re-layouts  36.3 us (13%)
  matrix products  35.3 us (12%)
  other arithmetic  29.5 us (10%)
    ppermute x20, waiting for transfers between devices, swap(): return lax.ppermute(value, axes, [(i, size - 1 - i) for i in range(size)])  65.2 us
    all_to_all x3, waiting for transfers between devices, scatter(): lax.all_to_all(part.reshape(size, -1, part.shape[1]), axis, 0, 0, tiled=T...  43.7 us
    dot_general x10, matrix products, dot(): lax.dot_general(left, right, (dims, ((), ())), preferred_element_type=F32)  35.3 us
    dynamic_update_slice x15, local copies, waits for them, and re-layouts, place(): return lax.dynamic_update_slice_in_dim(buffer, part, at, axis=0)  29.4 us
    all_to_all x4, starting transfers between devices, gather(): return lax.all_to_all(wide, axis, 0, 0, tiled=True)  25 us
    all_to_all x3, starting transfers between devices, scatter(): lax.all_to_all(part.reshape(size, -1, part.shape[1]), axis, 0, 0, tiled=T...  18.4 us
    ppermute x20, starting transfers between devices, swap(): return lax.ppermute(value, axes, [(i, size - 1 - i) for i in range(size)])  18.4 us
    all_to_all x4, waiting for transfers between devices, gather(): return lax.all_to_all(wide, axis, 0, 0, tiled=True)  12.1 us
  transfers between devices with their start and end apart: 27, of which 13 were waited for; matrix products, arithmetic and copies ran while one was open for 32% of the time, Pallas kernels for 0%

profile of v5, /device:TPU:8, one launch (start us, length us, event | category | flops | bytes accessed | tf_op | source)
XLA Modules:
  0.0 285.0 jit_solution(2989232051767153237)
XLA Ops:
  3.0 3.1 %collective-permute-start = (bf16[8,3712]{1,0:T(8,128)(2,1)S(1)}, bf16[8,3712]{1,0:T(8,128)(2,1)S(1)}, u32[]{:S(2)}, u32[]{:S(2)}) collective-permute-start(bf16[8,3712]{1,0:T(8,128)(2,1)S(1)} %get-tuple-element.66), channel_id=1, source_target_pairs={{0,128},{128,0},{1,129},{129,1},{2,130},{130,2},{3,131},{131,3},{4... | collective-permute-start | bytes 178184 | tf_op jit(solution)/shard_map/ppermute | solution.py:14
  6.6 6.1 %dynamic_update_slice.45 = bf16[1536,3584]{1,0:T(8,128)(2,1)} pad(bf16[152,3584]{1,0:T(8,128)(2,1)} %bitcast.44, bf16[]{:T(256)} %constant.28.clone.1), padding=0_1384x0_0 | pad | bytes 12099586 | tf_op jit(solution)/shard_map/dynamic_update_slice | solution.py:38
  13.7 8.5 %all-to-all-start = ((bf16[8,8,3712]{2,1,0:T(8,128)(2,1)}), bf16[8,8,3712]{2,1,0:T(8,128)(2,1)S(1)}, u32[]{:S(2)}, u32[]{:S(2)}) async-start(bf16[8,8,3712]{2,1,0:T(8,128)(2,1)} %broadcast_in_dim.147), calls=%async_computation | async-start | bytes 950272 | tf_op jit(solution)/shard_map/all_to_all | solution.py:30
  32.0 6.8 %all-to-all-done = bf16[8,8,3712]{2,1,0:T(8,128)(2,1)S(1)} async-done(((bf16[8,8,3712]{2,1,0:T(8,128)(2,1)}), bf16[8,8,3712]{2,1,0:T(8,128)(2,1)S(1)}, u32[]{:S(2)}, u32[]{:S(2)}) %all-to-all-start) | async-done | bytes 475168 | tf_op jit(solution)/shard_map/all_to_all | solution.py:30
  38.7 9.4 %collective-permute-done.1 = bf16[152,3584]{1,0:T(8,128)(2,1)S(1)} collective-permute-done((bf16[152,3584]{1,0:T(8,128)(2,1)}, bf16[152,3584]{1,0:T(8,128)(2,1)S(1)}, u32[]{:S(2)}, u32[]{:S(2)}) %collective-permute-start.1) | collective-permute-done | bytes 1089568 | tf_op jit(solution)/shard_map/ppermute | solution.py:14
  49.7 4.9 %all-to-all-start.1 = ((bf16[4,64,3712]{2,1,0:T(8,128)(2,1)}), bf16[4,64,3712]{2,1,0:T(8,128)(2,1)S(1)}, u32[]{:S(2)}, u32[]{:S(2)}) async-start(bf16[4,64,3712]{2,1,0:T(8,128)(2,1)} %broadcast_in_dim.148), calls=%async_computation.1 | async-start | bytes 3801088 | tf_op jit(solution)/shard_map/all_to_all | solution.py:30
  62.7 17.8 %collective-permute-done.4 = bf16[152,3584]{1,0:T(8,128)(2,1)} collective-permute-done((bf16[152,3584]{1,0:T(8,128)(2,1)S(1)}, bf16[152,3584]{1,0:T(8,128)(2,1)}, u32[]{:S(2)}, u32[]{:S(2)}) %collective-permute-start.4) | collective-permute-done | bytes 1089568 | tf_op jit(solution)/shard_map/ppermute | solution.py:14
  81.3 6.8 %all-to-all-start.2 = ((bf16[8,8,3584]{2,1,0:T(8,128)(2,1)}), bf16[8,8,3584]{2,1,0:T(8,128)(2,1)S(1)}, u32[]{:S(2)}, u32[]{:S(2)}) async-start(bf16[8,8,3584]{2,1,0:T(8,128)(2,1)} %broadcast_in_dim.149), calls=%async_computation.2 | async-start | bytes 917504 | tf_op jit(solution)/shard_map/all_to_all | solution.py:30
  92.1 7.2 %convolution_convert_fusion.8 = bf16[256,1536]{1,0:T(8,128)(2,1)S(1)} fusion(bf16[1536,3584]{1,0:T(8,128)(2,1)} %constant_dynamic-update-slice_fusion.9, bf16[256,3712]{1,0:T(8,128)(2,1)S(1)} %bitcast.26), kind=kOutput, calls=%fused_computation.8 | convolution fusion | flops 2818965504 | bytes 13631488 | tf_op jit(solution)/shard_map/dot_general | solution.py:51
  99.3 15.3 %collective-permute-done.8 = bf16[152,3584]{1,0:T(8,128)(2,1)} collective-permute-done((bf16[152,3584]{1,0:T(8,128)(2,1)}, bf16[152,3584]{1,0:T(8,128)(2,1)}, u32[]{:S(2)}, u32[]{:S(2)}) %collective-permute-start.8) | collective-permute-done | bytes 1089568 | tf_op jit(solution)/shard_map/ppermute | solution.py:14
  117.0 4.8 %all-to-all-start.3 = ((bf16[4,64,3584]{2,1,0:T(8,128)(2,1)}), bf16[4,64,3584]{2,1,0:T(8,128)(2,1)}, u32[]{:S(2)}, u32[]{:S(2)}) async-start(bf16[4,64,3584]{2,1,0:T(8,128)(2,1)} %broadcast_in_dim.151), calls=%async_computation.3 | async-start | bytes 3670016 | tf_op jit(solution)/shard_map/all_to_all | solution.py:30
  122.3 12.8 %collective-permute-done.11 = bf16[256,1536]{1,0:T(8,128)(2,1)} collective-permute-done((bf16[256,1536]{1,0:T(8,128)(2,1)S(1)}, bf16[256,1536]{1,0:T(8,128)(2,1)}, u32[]{:S(2)}, u32[]{:S(2)}) %collective-permute-start.11) | collective-permute-done | bytes 786464 | tf_op jit(solution)/shard_map/ppermute | solution.py:14
  138.0 5.4 %all-to-all-done.3 = bf16[4,64,3584]{2,1,0:T(8,128)(2,1)} async-done(((bf16[4,64,3584]{2,1,0:T(8,128)(2,1)}), bf16[4,64,3584]{2,1,0:T(8,128)(2,1)}, u32[]{:S(2)}, u32[]{:S(2)}) %all-to-all-start.3) | async-done | bytes 1835040 | tf_op jit(solution)/shard_map/all_to_all | solution.py:30
  150.6 3.1 %constant_dynamic-update-slice_fusion.6 = bf16[768,3584]{1,0:T(8,128)(2,1)} fusion(bf16[768,3584]{1,0:T(8,128)(2,1)} %constant_dynamic-update-slice_fusion.8, bf16[152,3584]{1,0:T(8,128)(2,1)} %collective-permute-done.9), kind=kLoop, calls=%fused_computation.86 | loop fusion | bytes 2179072 | tf_op jit(solution)/shard_map/dynamic_update_slice | solution.py:38
  153.7 4.9 %convolution_convert_fusion.9 = bf16[256,768]{1,0:T(8,128)(2,1)S(1)} fusion(bf16[256,3584]{1,0:T(8,128)(2,1)} %bitcast.6, bf16[768,3584]{1,0:T(8,128)(2,1)} %constant_dynamic-update-slice_fusion.6), kind=kOutput, calls=%fused_computation.17 | convolution fusion | flops 1409482752 | bytes 7733248 | tf_op jit(solution)/shard_map/dot_general | solution.py:51
  165.6 6.0 %collective-permute-done.10 = bf16[256,768]{1,0:T(8,128)(2,1)S(1)} collective-permute-done((bf16[256,768]{1,0:T(8,128)(2,1)S(1)}, bf16[256,768]{1,0:T(8,128)(2,1)S(1)}, u32[]{:S(2)}, u32[]{:S(2)}) %collective-permute-start.10) | collective-permute-done | bytes 393248 | tf_op jit(solution)/shard_map/ppermute | solution.py:14
  175.9 6.0 %all-to-all-start.4 = ((bf16[4,64,3584]{2,1,0:T(8,128)(2,1)}), bf16[4,64,3584]{2,1,0:T(8,128)(2,1)}, u32[]{:S(2)}, u32[]{:S(2)}) async-start(bf16[4,64,3584]{2,1,0:T(8,128)(2,1)} %bitcast.35), calls=%async_computation.4 | async-start | bytes 3670016 | tf_op jit(solution)/shard_map/all_to_all | solution.py:19
  185.3 8.3 %convolution_convert_fusion.7 = bf16[256,3584]{1,0:T(8,128)(2,1)} fusion(bf16[1536,3584]{1,0:T(8,128)(2,1)} %constant_dynamic-update-slice_fusion.9, bf16[256,768]{1,0:T(8,128)(2,1)S(1)} %copy-done.8, bf16[256,768]{1,0:T(8,128)(2,1)S(1)} %copy-done.10), kind=kOutput, calls=%fused_computation.7 | convolution fusion | flops 2821062656 | bytes 13631488 | tf_op jit(solution)/shard_map/dot_general | solution.py:51
  195.7 9.1 %all-to-all-done.4 = bf16[4,64,3584]{2,1,0:T(8,128)(2,1)} async-done(((bf16[4,64,3584]{2,1,0:T(8,128)(2,1)}), bf16[4,64,3584]{2,1,0:T(8,128)(2,1)}, u32[]{:S(2)}, u32[]{:S(2)}) %all-to-all-start.4) | async-done | bytes 1835040 | tf_op jit(solution)/shard_map/all_to_all | solution.py:19
  209.4 5.9 %all-to-all-start.5 = ((bf16[4,64,3584]{2,1,0:T(8,128)(2,1)}), bf16[4,64,3584]{2,1,0:T(8,128)(2,1)}, u32[]{:S(2)}, u32[]{:S(2)}) async-start(bf16[4,64,3584]{2,1,0:T(8,128)(2,1)} %bitcast.36), calls=%async_computation.5 | async-start | bytes 3670016 | tf_op jit(solution)/shard_map/all_to_all | solution.py:19
  220.0 17.5 %all-to-all-done.5 = bf16[4,64,3584]{2,1,0:T(8,128)(2,1)} async-done(((bf16[4,64,3584]{2,1,0:T(8,128)(2,1)}), bf16[4,64,3584]{2,1,0:T(8,128)(2,1)}, u32[]{:S(2)}, u32[]{:S(2)}) %all-to-all-start.5) | async-done | bytes 1835040 | tf_op jit(solution)/shard_map/all_to_all | solution.py:19
  241.7 6.6 %all-to-all-start.6 = ((bf16[8,16,3584]{2,1,0:T(8,128)(2,1)}), bf16[8,16,3584]{2,1,0:T(8,128)(2,1)S(1)}, u32[]{:S(2)}, u32[]{:S(2)}) async-start(bf16[8,16,3584]{2,1,0:T(8,128)(2,1)} %pad_maximum_fusion), calls=%async_computation.6 | async-start | bytes 1835008 | tf_op jit(solution)/shard_map/all_to_all | solution.py:19
  248.3 3.1 %fusion.2 = bf16[1,152,3584]{2,1,0:T(8,128)(2,1)} fusion(bf16[152,3584]{1,0:T(8,128)(2,1)} %collective-permute-done.14, bf16[304,3584]{1,0:T(8,128)(2,1)} %copy-done.7, bf16[304,3584]{1,0:T(8,128)(2,1)S(1)} %copy-done.4), kind=kLoop, calls=%fused_computation.20 | loop fusion | flops 3268608 | bytes 4358144 | tf_op jit(solution)/shard_map/broadcast_in_dim | solution.py:138
  255.6 17.2 %all-to-all-done.6 = bf16[8,16,3584]{2,1,0:T(8,128)(2,1)S(1)} async-done(((bf16[8,16,3584]{2,1,0:T(8,128)(2,1)}), bf16[8,16,3584]{2,1,0:T(8,128)(2,1)S(1)}, u32[]{:S(2)}, u32[]{:S(2)}) %all-to-all-start.6) | async-done | bytes 917536 | tf_op jit(solution)/shard_map/all_to_all | solution.py:19
  (126 shorter events, 87.5 us)
Async XLA Ops:
  3.0 9.8 %collective-permute-start = (bf16[8,3712]{1,0:T(8,128)(2,1)S(1)}, bf16[8,3712]{1,0:T(8,128)(2,1)S(1)}, u32[]{:S(2)}, u32[]{:S(2)}) collective-permute-start(bf16[8,3712]{1,0:T(8,128)(2,1)S(1)} %get-tuple-element.66), channel_id=1, source_target_pairs={{0,128},{128,0},{1,129},{129,1},{2,130},{130,2},{3,131},{131,3},{4... | collective-permute-start | bytes 178184 | tf_op jit(solution)/shard_map/ppermute | solution.py:14
  6.1 16.7 %collective-permute-start.2 = (bf16[152,3584]{1,0:T(8,128)(2,1)}, bf16[152,3584]{1,0:T(8,128)(2,1)}, u32[]{:S(2)}, u32[]{:S(2)}) collective-permute-start(bf16[152,3584]{1,0:T(8,128)(2,1)} %bitcast.43), channel_id=1, source_target_pairs={{0,32},{32,0},{1,33},{33,1},{2,34},{34,2},{3,35},{35,3},{4,36},{36... | collective-permute-start | bytes 3268616 | tf_op jit(solution)/shard_map/ppermute | solution.py:14
  6.1 22.4 %collective-permute-start.3 = (bf16[152,3584]{1,0:T(8,128)(2,1)}, bf16[152,3584]{1,0:T(8,128)(2,1)}, u32[]{:S(2)}, u32[]{:S(2)}) collective-permute-start(bf16[152,3584]{1,0:T(8,128)(2,1)} %bitcast.38), channel_id=1, source_target_pairs={{0,32},{32,0},{1,33},{33,1},{2,34},{34,2},{3,35},{35,3},{4,36},{36... | collective-permute-start | bytes 3268616 | tf_op jit(solution)/shard_map/ppermute | solution.py:14
  13.7 25.1 %all-to-all-start = ((bf16[8,8,3712]{2,1,0:T(8,128)(2,1)}), bf16[8,8,3712]{2,1,0:T(8,128)(2,1)S(1)}, u32[]{:S(2)}, u32[]{:S(2)}) async-start(bf16[8,8,3712]{2,1,0:T(8,128)(2,1)} %broadcast_in_dim.147), calls=%async_computation | async-start | bytes 950272 | tf_op jit(solution)/shard_map/all_to_all | solution.py:30
  22.1 26.0 %collective-permute-start.1 = (bf16[152,3584]{1,0:T(8,128)(2,1)}, bf16[152,3584]{1,0:T(8,128)(2,1)S(1)}, u32[]{:S(2)}, u32[]{:S(2)}) collective-permute-start(bf16[152,3584]{1,0:T(8,128)(2,1)} %bitcast.45), channel_id=1, source_target_pairs={{0,64},{64,0},{1,65},{65,1},{2,66},{66,2},{3,67},{67,3},{4,68},{68... | collective-permute-start | bytes 3268616 | tf_op jit(solution)/shard_map/ppermute | solution.py:14
  48.1 9.8 %collective-permute-start.6 = (bf16[152,3584]{1,0:T(8,128)(2,1)}, bf16[152,3584]{1,0:T(8,128)(2,1)}, u32[]{:S(2)}, u32[]{:S(2)}) collective-permute-start(bf16[152,3584]{1,0:T(8,128)(2,1)} %bitcast.40), channel_id=1, source_target_pairs={{0,32},{32,0},{1,33},{33,1},{2,34},{34,2},{3,35},{35,3},{4,36},{36... | collective-permute-start | bytes 3268616 | tf_op jit(solution)/shard_map/ppermute | solution.py:14
  49.7 30.8 %all-to-all-start.1 = ((bf16[4,64,3712]{2,1,0:T(8,128)(2,1)}), bf16[4,64,3712]{2,1,0:T(8,128)(2,1)S(1)}, u32[]{:S(2)}, u32[]{:S(2)}) async-start(bf16[4,64,3712]{2,1,0:T(8,128)(2,1)} %broadcast_in_dim.148), calls=%async_computation.1 | async-start | bytes 3801088 | tf_op jit(solution)/shard_map/all_to_all | solution.py:30
  54.7 25.8 %collective-permute-start.4 = (bf16[152,3584]{1,0:T(8,128)(2,1)S(1)}, bf16[152,3584]{1,0:T(8,128)(2,1)}, u32[]{:S(2)}, u32[]{:S(2)}) collective-permute-start(bf16[152,3584]{1,0:T(8,128)(2,1)S(1)} %bitcast.39), channel_id=1, source_target_pairs={{0,64},{64,0},{1,65},{65,1},{2,66},{66,2},{3,67},{67,3},{4,68},{68... | collective-permute-start | bytes 3268616 | tf_op jit(solution)/shard_map/ppermute | solution.py:14
  80.5 10.5 %collective-permute-start.7 = (bf16[152,3584]{1,0:T(8,128)(2,1)}, bf16[152,3584]{1,0:T(8,128)(2,1)S(1)}, u32[]{:S(2)}, u32[]{:S(2)}) collective-permute-start(bf16[152,3584]{1,0:T(8,128)(2,1)} %collective-permute-done.4), channel_id=1, source_target_pairs={{0,32},{32,0},{1,33},{33,1},{2,34},{34,2},{3,35},{35,3},{4,36},{36... | collective-permute-start | bytes 3268616 | tf_op jit(solution)/shard_map/ppermute | solution.py:14
  81.3 34.2 %all-to-all-start.2 = ((bf16[8,8,3584]{2,1,0:T(8,128)(2,1)}), bf16[8,8,3584]{2,1,0:T(8,128)(2,1)S(1)}, u32[]{:S(2)}, u32[]{:S(2)}) async-start(bf16[8,8,3584]{2,1,0:T(8,128)(2,1)} %broadcast_in_dim.149), calls=%async_computation.2 | async-start | bytes 917504 | tf_op jit(solution)/shard_map/all_to_all | solution.py:30
  88.2 26.5 %collective-permute-start.8 = (bf16[152,3584]{1,0:T(8,128)(2,1)}, bf16[152,3584]{1,0:T(8,128)(2,1)}, u32[]{:S(2)}, u32[]{:S(2)}) collective-permute-start(bf16[152,3584]{1,0:T(8,128)(2,1)} %bitcast.41), channel_id=1, source_target_pairs={{0,64},{64,0},{1,65},{65,1},{2,66},{66,2},{3,67},{67,3},{4,68},{68... | collective-permute-start | bytes 3268616 | tf_op jit(solution)/shard_map/ppermute | solution.py:14
  114.7 20.5 %collective-permute-start.11 = (bf16[256,1536]{1,0:T(8,128)(2,1)S(1)}, bf16[256,1536]{1,0:T(8,128)(2,1)}, u32[]{:S(2)}, u32[]{:S(2)}) collective-permute-start(bf16[256,1536]{1,0:T(8,128)(2,1)S(1)} %convolution_convert_fusion.8), channel_id=1, source_target_pairs={{0,128},{128,0},{1,129},{129,1},{2,130},{130,2},{3,131},{131,3},{4... | collective-permute-start | bytes 2359304 | tf_op jit(solution)/shard_map/ppermute | solution.py:14
  117.0 26.4 %all-to-all-start.3 = ((bf16[4,64,3584]{2,1,0:T(8,128)(2,1)}), bf16[4,64,3584]{2,1,0:T(8,128)(2,1)}, u32[]{:S(2)}, u32[]{:S(2)}) async-start(bf16[4,64,3584]{2,1,0:T(8,128)(2,1)} %broadcast_in_dim.151), calls=%async_computation.3 | async-start | bytes 3670016 | tf_op jit(solution)/shard_map/all_to_all | solution.py:30
  122.0 28.6 %collective-permute-start.9 = (bf16[152,3584]{1,0:T(8,128)(2,1)}, bf16[152,3584]{1,0:T(8,128)(2,1)}, u32[]{:S(2)}, u32[]{:S(2)}) collective-permute-start(bf16[152,3584]{1,0:T(8,128)(2,1)} %collective-permute-done.8), channel_id=1, source_target_pairs={{0,32},{32,0},{1,33},{33,1},{2,34},{34,2},{3,35},{35,3},{4,36},{36... | collective-permute-start | bytes 3268616 | tf_op jit(solution)/shard_map/ppermute | solution.py:14
  145.8 18.3 %collective-permute-start.12 = (bf16[304,3584]{1,0:T(8,128)(2,1)S(1)}, bf16[304,3584]{1,0:T(8,128)(2,1)S(1)}, u32[]{:S(2)}, u32[]{:S(2)}) collective-permute-start(bf16[304,3584]{1,0:T(8,128)(2,1)S(1)} %convolution_convert_fusion.4), channel_id=1, source_target_pairs={{0,32},{32,0},{1,33},{33,1},{2,34},{34,2},{3,35},{35,3},{4,36},{36... | collective-permute-start | bytes 6537224 | tf_op jit(solution)/shard_map/ppermute | solution.py:14
  158.5 13.1 %collective-permute-start.10 = (bf16[256,768]{1,0:T(8,128)(2,1)S(1)}, bf16[256,768]{1,0:T(8,128)(2,1)S(1)}, u32[]{:S(2)}, u32[]{:S(2)}) collective-permute-start(bf16[256,768]{1,0:T(8,128)(2,1)S(1)} %convolution_convert_fusion.9), channel_id=1, source_target_pairs={{0,128},{128,0},{1,129},{129,1},{2,130},{130,2},{3,131},{131,3},{4... | collective-permute-start | bytes 1179656 | tf_op jit(solution)/shard_map/ppermute | solution.py:14
  175.9 30.8 %collective-permute-start.13 = (bf16[304,3584]{1,0:T(8,128)(2,1)}, bf16[304,3584]{1,0:T(8,128)(2,1)}, u32[]{:S(2)}, u32[]{:S(2)}) collective-permute-start(bf16[304,3584]{1,0:T(8,128)(2,1)} %convolution_convert_fusion.2), channel_id=1, source_target_pairs={{0,32},{32,0},{1,33},{33,1},{2,34},{34,2},{3,35},{35,3},{4,36},{36... | collective-permute-start | bytes 6537224 | tf_op jit(solution)/shard_map/ppermute | solution.py:14
  175.9 28.9 %all-to-all-start.4 = ((bf16[4,64,3584]{2,1,0:T(8,128)(2,1)}), bf16[4,64,3584]{2,1,0:T(8,128)(2,1)}, u32[]{:S(2)}, u32[]{:S(2)}) async-start(bf16[4,64,3584]{2,1,0:T(8,128)(2,1)} %bitcast.35), calls=%async_computation.4 | async-start | bytes 3670016 | tf_op jit(solution)/shard_map/all_to_all | solution.py:19
  181.9 27.6 %collective-permute-start.14 = (bf16[152,3584]{1,0:T(8,128)(2,1)}, bf16[152,3584]{1,0:T(8,128)(2,1)}, u32[]{:S(2)}, u32[]{:S(2)}) collective-permute-start(bf16[152,3584]{1,0:T(8,128)(2,1)} %add_convert_fusion.5), channel_id=1, source_target_pairs={{0,64},{64,0},{1,65},{65,1},{2,66},{66,2},{3,67},{67,3},{4,68},{68... | collective-permute-start | bytes 3268616 | tf_op jit(solution)/shard_map/ppermute | solution.py:14
  185.3 32.0 %collective-permute-start.15 = (bf16[304,3584]{1,0:T(8,128)(2,1)}, bf16[304,3584]{1,0:T(8,128)(2,1)}, u32[]{:S(2)}, u32[]{:S(2)}) collective-permute-start(bf16[304,3584]{1,0:T(8,128)(2,1)} %convolution_convert_fusion), channel_id=1, source_target_pairs={{0,32},{32,0},{1,33},{33,1},{2,34},{34,2},{3,35},{35,3},{4,36},{36... | collective-permute-start | bytes 6537224 | tf_op jit(solution)/shard_map/ppermute | solution.py:14
  209.4 28.0 %all-to-all-start.5 = ((bf16[4,64,3584]{2,1,0:T(8,128)(2,1)}), bf16[4,64,3584]{2,1,0:T(8,128)(2,1)}, u32[]{:S(2)}, u32[]{:S(2)}) async-start(bf16[4,64,3584]{2,1,0:T(8,128)(2,1)} %bitcast.36), calls=%async_computation.5 | async-start | bytes 3670016 | tf_op jit(solution)/shard_map/all_to_all | solution.py:19
  216.1 25.6 %collective-permute-start.16 = (bf16[152,3584]{1,0:T(8,128)(2,1)}, bf16[152,3584]{1,0:T(8,128)(2,1)}, u32[]{:S(2)}, u32[]{:S(2)}) collective-permute-start(bf16[152,3584]{1,0:T(8,128)(2,1)} %add_convert_fusion.4), channel_id=1, source_target_pairs={{0,64},{64,0},{1,65},{65,1},{2,66},{66,2},{3,67},{67,3},{4,68},{68... | collective-permute-start | bytes 3268616 | tf_op jit(solution)/shard_map/ppermute | solution.py:14
  241.7 31.0 %all-to-all-start.6 = ((bf16[8,16,3584]{2,1,0:T(8,128)(2,1)}), bf16[8,16,3584]{2,1,0:T(8,128)(2,1)S(1)}, u32[]{:S(2)}, u32[]{:S(2)}) async-start(bf16[8,16,3584]{2,1,0:T(8,128)(2,1)} %pad_maximum_fusion), calls=%async_computation.6 | async-start | bytes 1835008 | tf_op jit(solution)/shard_map/all_to_all | solution.py:19
  251.4 24.6 %collective-permute-start.19 = (bf16[152,3584]{1,0:T(8,128)(2,1)}, bf16[152,3584]{1,0:T(8,128)(2,1)}, u32[]{:S(2)}, u32[]{:S(2)}) collective-permute-start(bf16[152,3584]{1,0:T(8,128)(2,1)} %add_convert_fusion.3), channel_id=1, source_target_pairs={{0,64},{64,0},{1,65},{65,1},{2,66},{66,2},{3,67},{67,3},{4,68},{68... | collective-permute-start | bytes 3268616 | tf_op jit(solution)/shard_map/ppermute | solution.py:14
  (21 other events, 138.5 us)

commit v6 on v4

--- a/solution.py
+++ b/solution.py
@@ -94,14 +94,16 @@
 
     pair = jnp.zeros((2 * units, width), BF)
     pair = place_near(place_near(pair, gate, dense_gate, 0), up, dense_up, units)
+    up_late, _ = lax.optimization_barrier((up, gate_x))
+    up_x = swap(up_late, ("xlo",))
+    down_late, _ = lax.optimization_barrier((down, up_x))
+    down_x = swap(down_late, ("xlo",))
+
+    block, pair, down = lax.optimization_barrier((block, pair, down))
+    tok = gather(block[:, :2 * rows].reshape(-1, block.shape[2]), "y").reshape(-1, block.shape[2])
     last = place_near(jnp.zeros((units, width), BF), down, dense_down, 0)
-
-    block, gate_x, pair, last, up = lax.optimization_barrier((block, gate_x, pair, last, up))
-    up_x = swap(up, ("xlo",))
-    tok = gather(block[:, :2 * rows].reshape(-1, block.shape[2]), "y").reshape(-1, block.shape[2])
     pair = place_far(pair, gate_x, 0)
-    block, tok, up_x, down, pair = lax.optimization_barrier((block, tok, up_x, down, pair))
-    down_x = swap(down, ("xlo",))
+    block, tok, pair, last = lax.optimization_barrier((block, tok, pair, last))
     cot = gather(block[:, 2 * rows:, :width].reshape(-1, width), "y").reshape(-1, width)
     pair = place_far(pair, up_x, units)
 

time: 270 us -> 264 us (0.978)
  waiting for transfers between devices: 118 us -> 100 us
  starting transfers between devices: 49.1 us -> 60.3 us
    ppermute x20, waiting for transfers between devices: 62.7 us -> 33 us  [swap(): return lax.ppermute(value, axes, [(i, size - 1 - i) for i in range(size)])]
    all_to_all x3, waiting for transfers between devices: 10.5 us -> 23.2 us  [gather(): return lax.all_to_all(wide, axis, 0, 0, tiled=True)]
    ppermute x20, starting transfers between devices: 16.8 us -> 23.3 us  [swap(): return lax.ppermute(value, axes, [(i, size - 1 - i) for i in range(size)])]
    all_to_all x3, starting transfers between devices: 14.2 us -> 17.9 us  [scatter(): lax.all_to_all(part.reshape(size, -1, part.shape[1]), axis, 0, 0, tiled=T...]
  transfers between devices with their start and end apart: 26 -> 26, of which waited for: 12 -> 13; matrix products, arithmetic and copies ran while one was open for 33% -> 34% of each run, Pallas kernels for 0% -> 0%
where the time goes in v6:
time: 264 us; the launch traced here: 262 us
  waiting for transfers between devices  100 us (38%)
  starting transfers between devices  60.3 us (23%)
  local copies, waits for them, and re-layouts  38 us (14%)
  matrix products  36.2 us (14%)
  other arithmetic  26.8 us (10%)
    all_to_all x3, waiting for transfers between devices, scatter(): lax.all_to_all(part.reshape(size, -1, part.shape[1]), axis, 0, 0, tiled=T...  44 us
    dot_general x10, matrix products, dot(): lax.dot_general(left, right, (dims, ((), ())), preferred_element_type=F32)  36.2 us
    dynamic_update_slice x15, local copies, waits for them, and re-layouts, place(): return lax.dynamic_update_slice_in_dim(buffer, part, at, axis=0)  34.1 us
    ppermute x20, waiting for transfers between devices, swap(): return lax.ppermute(value, axes, [(i, size - 1 - i) for i in range(size)])  33 us
    ppermute x20, starting transfers between devices, swap(): return lax.ppermute(value, axes, [(i, size - 1 - i) for i in range(size)])  23.3 us
    all_to_all x3, waiting for transfers between devices, gather(): return lax.all_to_all(wide, axis, 0, 0, tiled=True)  23.2 us
    all_to_all x3, starting transfers between devices, gather(): return lax.all_to_all(wide, axis, 0, 0, tiled=True)  19.2 us
    all_to_all x3, starting transfers between devices, scatter(): lax.all_to_all(part.reshape(size, -1, part.shape[1]), axis, 0, 0, tiled=T...  17.9 us
  transfers between devices with their start and end apart: 26, of which 13 were waited for; matrix products, arithmetic and copies ran while one was open for 34% of the time, Pallas kernels for 0%

profile of v6, /device:TPU:8, one launch (start us, length us, event | category | flops | bytes accessed | tf_op | source)
XLA Modules:
  0.0 262.5 jit_solution(11977038985104144647)
XLA Ops:
  3.0 3.1 %collective-permute-start = (bf16[8,3712]{1,0:T(8,128)(2,1)S(1)}, bf16[8,3712]{1,0:T(8,128)(2,1)S(1)}, u32[]{:S(2)}, u32[]{:S(2)}) collective-permute-start(bf16[8,3712]{1,0:T(8,128)(2,1)S(1)} %get-tuple-element.70), channel_id=1, source_target_pairs={{0,128},{128,0},{1,129},{129,1},{2,130},{130,2},{3,131},{131,3},{4... | collective-permute-start | bytes 178184 | tf_op jit(solution)/shard_map/ppermute | solution.py:14
  11.4 8.5 %all-to-all-start = ((bf16[8,16,3712]{2,1,0:T(8,128)(2,1)}), bf16[8,16,3712]{2,1,0:T(8,128)(2,1)S(1)}, u32[]{:S(2)}, u32[]{:S(2)}) async-start(bf16[8,16,3712]{2,1,0:T(8,128)(2,1)} %broadcast_in_dim.142), calls=%async_computation | async-start | bytes 1900544 | tf_op jit(solution)/shard_map/all_to_all | solution.py:30
  19.9 6.1 %dynamic_update_slice.45 = bf16[1536,3584]{1,0:T(8,128)(2,1)} pad(bf16[152,3584]{1,0:T(8,128)(2,1)} %bitcast.43, bf16[]{:T(256)} %constant.27.clone.1), padding=0_1384x0_0 | pad | bytes 12099586 | tf_op jit(solution)/shard_map/dynamic_update_slice | solution.py:38
  26.1 9.5 %collective-permute-done.3 = bf16[152,3584]{1,0:T(8,128)(2,1)} collective-permute-done((bf16[152,3584]{1,0:T(8,128)(2,1)}, bf16[152,3584]{1,0:T(8,128)(2,1)}, u32[]{:S(2)}, u32[]{:S(2)}) %collective-permute-start.3) | collective-permute-done | bytes 1089568 | tf_op jit(solution)/shard_map/ppermute | solution.py:14
  47.0 4.0 %dynamic_update_slice.53 = bf16[768,3584]{1,0:T(8,128)(2,1)} pad(bf16[152,3584]{1,0:T(8,128)(2,1)} %bitcast.39, bf16[]{:T(256)} %constant.27.clone.1), padding=0_616x0_0 | pad | bytes 6594562 | tf_op jit(solution)/shard_map/dynamic_update_slice | solution.py:38
  52.4 4.9 %all-to-all-start.1 = ((bf16[4,64,3712]{2,1,0:T(8,128)(2,1)}), bf16[4,64,3712]{2,1,0:T(8,128)(2,1)S(1)}, u32[]{:S(2)}, u32[]{:S(2)}) async-start(bf16[4,64,3712]{2,1,0:T(8,128)(2,1)} %broadcast_in_dim.144), calls=%async_computation.1 | async-start | bytes 3801088 | tf_op jit(solution)/shard_map/all_to_all | solution.py:30
  68.7 12.0 %all-to-all-done.1 = bf16[4,64,3712]{2,1,0:T(8,128)(2,1)S(1)} async-done(((bf16[4,64,3712]{2,1,0:T(8,128)(2,1)}), bf16[4,64,3712]{2,1,0:T(8,128)(2,1)S(1)}, u32[]{:S(2)}, u32[]{:S(2)}) %all-to-all-start.1) | async-done | bytes 1900576 | tf_op jit(solution)/shard_map/all_to_all | solution.py:30
  82.1 5.8 %all-to-all-start.2 = ((bf16[4,64,3584]{2,1,0:T(8,128)(2,1)}), bf16[4,64,3584]{2,1,0:T(8,128)(2,1)}, u32[]{:S(2)}, u32[]{:S(2)}) async-start(bf16[4,64,3584]{2,1,0:T(8,128)(2,1)} %broadcast_in_dim.146), calls=%async_computation.2 | async-start | bytes 3670016 | tf_op jit(solution)/shard_map/all_to_all | solution.py:30
  92.5 8.0 %convolution_convert_fusion.8 = bf16[256,1536]{1,0:T(8,128)(2,1)} fusion(bf16[1536,3584]{1,0:T(8,128)(2,1)} %constant_dynamic-update-slice_fusion.9, bf16[256,3712]{1,0:T(8,128)(2,1)S(1)} %bitcast.28), kind=kOutput, calls=%fused_computation.8 | convolution fusion | flops 2818965504 | bytes 13631488 | tf_op jit(solution)/shard_map/dot_general | solution.py:51
  100.5 9.4 %all-to-all-done.2 = bf16[4,64,3584]{2,1,0:T(8,128)(2,1)} async-done(((bf16[4,64,3584]{2,1,0:T(8,128)(2,1)}), bf16[4,64,3584]{2,1,0:T(8,128)(2,1)}, u32[]{:S(2)}, u32[]{:S(2)}) %all-to-all-start.2) | async-done | bytes 1835040 | tf_op jit(solution)/shard_map/all_to_all | solution.py:30
  116.6 4.8 %convolution_convert_fusion.9 = bf16[256,768]{1,0:T(8,128)(2,1)S(1)} fusion(bf16[256,3584]{1,0:T(8,128)(2,1)} %bitcast.6, bf16[768,3584]{1,0:T(8,128)(2,1)} %constant_dynamic-update-slice_fusion.6), kind=kOutput, calls=%fused_computation.17 | convolution fusion | flops 1409482752 | bytes 7733248 | tf_op jit(solution)/shard_map/dot_general | solution.py:51
  121.4 10.7 %collective-permute-done.11 = bf16[256,1536]{1,0:T(8,128)(2,1)S(1)} collective-permute-done((bf16[256,1536]{1,0:T(8,128)(2,1)}, bf16[256,1536]{1,0:T(8,128)(2,1)S(1)}, u32[]{:S(2)}, u32[]{:S(2)}) %collective-permute-start.11) | collective-permute-done | bytes 786464 | tf_op jit(solution)/shard_map/ppermute | solution.py:14
  143.6 5.0 %collective-permute-done.10 = bf16[256,768]{1,0:T(8,128)(2,1)S(1)} collective-permute-done((bf16[256,768]{1,0:T(8,128)(2,1)S(1)}, bf16[256,768]{1,0:T(8,128)(2,1)S(1)}, u32[]{:S(2)}, u32[]{:S(2)}) %collective-permute-start.10) | collective-permute-done | bytes 393248 | tf_op jit(solution)/shard_map/ppermute | solution.py:14
  154.3 5.8 %all-to-all-start.3 = ((bf16[4,64,3584]{2,1,0:T(8,128)(2,1)}), bf16[4,64,3584]{2,1,0:T(8,128)(2,1)}, u32[]{:S(2)}, u32[]{:S(2)}) async-start(bf16[4,64,3584]{2,1,0:T(8,128)(2,1)} %bitcast.36), calls=%async_computation.3 | async-start | bytes 3670016 | tf_op jit(solution)/shard_map/all_to_all | solution.py:19
  162.3 8.3 %convolution_convert_fusion.7 = bf16[256,3584]{1,0:T(8,128)(2,1)} fusion(bf16[1536,3584]{1,0:T(8,128)(2,1)} %constant_dynamic-update-slice_fusion.9, bf16[256,768]{1,0:T(8,128)(2,1)S(1)} %get-tuple-element.58, bf16[256,768]{1,0:T(8,128)(2,1)S(1)} %get-tuple-element.57), kind=kOutput, calls=%fused_computation.7 | convolution fusion | flops 2821062656 | bytes 13631488 | tf_op jit(solution)/shard_map/dot_general | solution.py:51
  172.7 10.2 %all-to-all-done.3 = bf16[4,64,3584]{2,1,0:T(8,128)(2,1)} async-done(((bf16[4,64,3584]{2,1,0:T(8,128)(2,1)}), bf16[4,64,3584]{2,1,0:T(8,128)(2,1)}, u32[]{:S(2)}, u32[]{:S(2)}) %all-to-all-start.3) | async-done | bytes 1835040 | tf_op jit(solution)/shard_map/all_to_all | solution.py:19
  187.6 5.8 %all-to-all-start.4 = ((bf16[4,64,3584]{2,1,0:T(8,128)(2,1)}), bf16[4,64,3584]{2,1,0:T(8,128)(2,1)}, u32[]{:S(2)}, u32[]{:S(2)}) async-start(bf16[4,64,3584]{2,1,0:T(8,128)(2,1)} %bitcast.37), calls=%async_computation.4 | async-start | bytes 3670016 | tf_op jit(solution)/shard_map/all_to_all | solution.py:19
  198.3 17.1 %all-to-all-done.4 = bf16[4,64,3584]{2,1,0:T(8,128)(2,1)} async-done(((bf16[4,64,3584]{2,1,0:T(8,128)(2,1)}), bf16[4,64,3584]{2,1,0:T(8,128)(2,1)}, u32[]{:S(2)}, u32[]{:S(2)}) %all-to-all-start.4) | async-done | bytes 1835040 | tf_op jit(solution)/shard_map/all_to_all | solution.py:19
  219.6 6.3 %all-to-all-start.5 = ((bf16[8,16,3584]{2,1,0:T(8,128)(2,1)}), bf16[8,16,3584]{2,1,0:T(8,128)(2,1)S(1)}, u32[]{:S(2)}, u32[]{:S(2)}) async-start(bf16[8,16,3584]{2,1,0:T(8,128)(2,1)} %pad_maximum_fusion), calls=%async_computation.5 | async-start | bytes 1835008 | tf_op jit(solution)/shard_map/all_to_all | solution.py:19
  225.9 3.1 %fusion.2 = bf16[1,152,3584]{2,1,0:T(8,128)(2,1)} fusion(bf16[152,3584]{1,0:T(8,128)(2,1)} %collective-permute-done.14, bf16[304,3584]{1,0:T(8,128)(2,1)} %copy-done.6, bf16[304,3584]{1,0:T(8,128)(2,1)S(1)} %copy-done.4), kind=kLoop, calls=%fused_computation.20 | loop fusion | flops 3268608 | bytes 4358144 | tf_op jit(solution)/shard_map/broadcast_in_dim | solution.py:141
  230.5 3.0 %fusion = bf16[1,152,3584]{2,1,0:T(8,128)(2,1)} fusion(bf16[152,3584]{1,0:T(8,128)(2,1)} %collective-permute-done.16, bf16[304,3584]{1,0:T(8,128)(2,1)} %collective-permute-done.13, bf16[304,3584]{1,0:T(8,128)(2,1)S(1)} %copy-done.2), kind=kLoop, calls=%fused_computation.18 | loop fusion | flops 3268608 | bytes 4358144 | tf_op jit(solution)/shard_map/broadcast_in_dim | solution.py:141
  233.5 16.7 %all-to-all-done.5 = bf16[8,16,3584]{2,1,0:T(8,128)(2,1)S(1)} async-done(((bf16[8,16,3584]{2,1,0:T(8,128)(2,1)}), bf16[8,16,3584]{2,1,0:T(8,128)(2,1)S(1)}, u32[]{:S(2)}, u32[]{:S(2)}) %all-to-all-start.5) | async-done | bytes 917536 | tf_op jit(solution)/shard_map/all_to_all | solution.py:19
  250.4 3.1 %collective-permute-start.18 = (bf16[4,3584]{1,0:T(4,128)(2,1)S(1)}, bf16[4,3584]{1,0:T(4,128)(2,1)S(1)}, u32[]{:S(2)}, u32[]{:S(2)}) collective-permute-start(bf16[4,3584]{1,0:T(4,128)(2,1)S(1)} %get-tuple-element.60), channel_id=1, source_target_pairs={{0,128},{128,0},{1,129},{129,1},{2,130},{130,2},{3,131},{131,3},{4... | collective-permute-start | bytes 86024 | tf_op jit(solution)/shard_map/ppermute | solution.py:14
  256.5 3.0 %collective-permute-start.17 = (bf16[4,3584]{1,0:T(4,128)(2,1)S(1)}, bf16[4,3584]{1,0:T(4,128)(2,1)S(1)}, u32[]{:S(2)}, u32[]{:S(2)}) collective-permute-start(bf16[4,3584]{1,0:T(4,128)(2,1)S(1)} %get-tuple-element.62), channel_id=1, source_target_pairs={{0,128},{128,0},{1,129},{129,1},{2,130},{130,2},{3,131},{131,3},{4... | collective-permute-start | bytes 86024 | tf_op jit(solution)/shard_map/ppermute | solution.py:14
  (110 shorter events, 87.3 us)
Async XLA Ops:
  3.0 5.8 %collective-permute-start = (bf16[8,3712]{1,0:T(8,128)(2,1)S(1)}, bf16[8,3712]{1,0:T(8,128)(2,1)S(1)}, u32[]{:S(2)}, u32[]{:S(2)}) collective-permute-start(bf16[8,3712]{1,0:T(8,128)(2,1)S(1)} %get-tuple-element.70), channel_id=1, source_target_pairs={{0,128},{128,0},{1,129},{129,1},{2,130},{130,2},{3,131},{131,3},{4... | collective-permute-start | bytes 178184 | tf_op jit(solution)/shard_map/ppermute | solution.py:14
  6.1 36.8 %collective-permute-start.2 = (bf16[152,3584]{1,0:T(8,128)(2,1)}, bf16[152,3584]{1,0:T(8,128)(2,1)S(1)}, u32[]{:S(2)}, u32[]{:S(2)}) collective-permute-start(bf16[152,3584]{1,0:T(8,128)(2,1)} %bitcast.1), channel_id=1, source_target_pairs={{0,32},{32,0},{1,33},{33,1},{2,34},{34,2},{3,35},{35,3},{4,36},{36... | collective-permute-start | bytes 3268616 | tf_op jit(solution)/shard_map/ppermute | solution.py:14
  8.8 28.3 %collective-permute-start.1 = (bf16[152,3584]{1,0:T(8,128)(2,1)}, bf16[152,3584]{1,0:T(8,128)(2,1)}, u32[]{:S(2)}, u32[]{:S(2)}) collective-permute-start(bf16[152,3584]{1,0:T(8,128)(2,1)} %bitcast.41), channel_id=1, source_target_pairs={{0,32},{32,0},{1,33},{33,1},{2,34},{34,2},{3,35},{35,3},{4,36},{36... | collective-permute-start | bytes 3268616 | tf_op jit(solution)/shard_map/ppermute | solution.py:14
  8.8 26.8 %collective-permute-start.3 = (bf16[152,3584]{1,0:T(8,128)(2,1)}, bf16[152,3584]{1,0:T(8,128)(2,1)}, u32[]{:S(2)}, u32[]{:S(2)}) collective-permute-start(bf16[152,3584]{1,0:T(8,128)(2,1)} %bitcast.42), channel_id=1, source_target_pairs={{0,64},{64,0},{1,65},{65,1},{2,66},{66,2},{3,67},{67,3},{4,68},{68... | collective-permute-start | bytes 3268616 | tf_op jit(solution)/shard_map/ppermute | solution.py:14
  11.4 35.5 %all-to-all-start = ((bf16[8,16,3712]{2,1,0:T(8,128)(2,1)}), bf16[8,16,3712]{2,1,0:T(8,128)(2,1)S(1)}, u32[]{:S(2)}, u32[]{:S(2)}) async-start(bf16[8,16,3712]{2,1,0:T(8,128)(2,1)} %broadcast_in_dim.142), calls=%async_computation | async-start | bytes 1900544 | tf_op jit(solution)/shard_map/all_to_all | solution.py:30
  35.6 26.0 %collective-permute-start.6 = (bf16[152,3584]{1,0:T(8,128)(2,1)}, bf16[152,3584]{1,0:T(8,128)(2,1)}, u32[]{:S(2)}, u32[]{:S(2)}) collective-permute-start(bf16[152,3584]{1,0:T(8,128)(2,1)} %bitcast.1), channel_id=1, source_target_pairs={{0,64},{64,0},{1,65},{65,1},{2,66},{66,2},{3,67},{67,3},{4,68},{68... | collective-permute-start | bytes 3268616 | tf_op jit(solution)/shard_map/ppermute | solution.py:14
  40.5 22.6 %collective-permute-start.4 = (bf16[152,3584]{1,0:T(8,128)(2,1)}, bf16[152,3584]{1,0:T(8,128)(2,1)}, u32[]{:S(2)}, u32[]{:S(2)}) collective-permute-start(bf16[152,3584]{1,0:T(8,128)(2,1)} %collective-permute-done.3), channel_id=1, source_target_pairs={{0,32},{32,0},{1,33},{33,1},{2,34},{34,2},{3,35},{35,3},{4,36},{36... | collective-permute-start | bytes 3268616 | tf_op jit(solution)/shard_map/ppermute | solution.py:14
  46.9 18.4 %collective-permute-start.5 = (bf16[152,3584]{1,0:T(8,128)(2,1)}, bf16[152,3584]{1,0:T(8,128)(2,1)}, u32[]{:S(2)}, u32[]{:S(2)}) collective-permute-start(bf16[152,3584]{1,0:T(8,128)(2,1)} %bitcast.38), channel_id=1, source_target_pairs={{0,32},{32,0},{1,33},{33,1},{2,34},{34,2},{3,35},{35,3},{4,36},{36... | collective-permute-start | bytes 3268616 | tf_op jit(solution)/shard_map/ppermute | solution.py:14
  52.4 28.3 %all-to-all-start.1 = ((bf16[4,64,3712]{2,1,0:T(8,128)(2,1)}), bf16[4,64,3712]{2,1,0:T(8,128)(2,1)S(1)}, u32[]{:S(2)}, u32[]{:S(2)}) async-start(bf16[4,64,3712]{2,1,0:T(8,128)(2,1)} %broadcast_in_dim.144), calls=%async_computation.1 | async-start | bytes 3801088 | tf_op jit(solution)/shard_map/all_to_all | solution.py:30
  61.5 39.0 %collective-permute-start.8 = (bf16[152,3584]{1,0:T(8,128)(2,1)}, bf16[152,3584]{1,0:T(8,128)(2,1)}, u32[]{:S(2)}, u32[]{:S(2)}) collective-permute-start(bf16[152,3584]{1,0:T(8,128)(2,1)} %bitcast.40), channel_id=1, source_target_pairs={{0,64},{64,0},{1,65},{65,1},{2,66},{66,2},{3,67},{67,3},{4,68},{68... | collective-permute-start | bytes 3268616 | tf_op jit(solution)/shard_map/ppermute | solution.py:14
  63.0 27.2 %collective-permute-start.7 = (bf16[152,3584]{1,0:T(8,128)(2,1)}, bf16[152,3584]{1,0:T(8,128)(2,1)}, u32[]{:S(2)}, u32[]{:S(2)}) collective-permute-start(bf16[152,3584]{1,0:T(8,128)(2,1)} %collective-permute-done.6), channel_id=1, source_target_pairs={{0,32},{32,0},{1,33},{33,1},{2,34},{34,2},{3,35},{35,3},{4,36},{36... | collective-permute-start | bytes 3268616 | tf_op jit(solution)/shard_map/ppermute | solution.py:14
  82.1 27.8 %all-to-all-start.2 = ((bf16[4,64,3584]{2,1,0:T(8,128)(2,1)}), bf16[4,64,3584]{2,1,0:T(8,128)(2,1)}, u32[]{:S(2)}, u32[]{:S(2)}) async-start(bf16[4,64,3584]{2,1,0:T(8,128)(2,1)} %broadcast_in_dim.146), calls=%async_computation.2 | async-start | bytes 3670016 | tf_op jit(solution)/shard_map/all_to_all | solution.py:30
  110.1 21.9 %collective-permute-start.11 = (bf16[256,1536]{1,0:T(8,128)(2,1)}, bf16[256,1536]{1,0:T(8,128)(2,1)S(1)}, u32[]{:S(2)}, u32[]{:S(2)}) collective-permute-start(bf16[256,1536]{1,0:T(8,128)(2,1)} %convolution_convert_fusion.8), channel_id=1, source_target_pairs={{0,128},{128,0},{1,129},{129,1},{2,130},{130,2},{3,131},{131,3},{4... | collective-permute-start | bytes 2359304 | tf_op jit(solution)/shard_map/ppermute | solution.py:14
  135.5 13.2 %collective-permute-start.12 = (bf16[304,3584]{1,0:T(8,128)(2,1)S(1)}, bf16[304,3584]{1,0:T(8,128)(2,1)S(1)}, u32[]{:S(2)}, u32[]{:S(2)}) collective-permute-start(bf16[304,3584]{1,0:T(8,128)(2,1)S(1)} %convolution_convert_fusion.4), channel_id=1, source_target_pairs={{0,32},{32,0},{1,33},{33,1},{2,34},{34,2},{3,35},{35,3},{4,36},{36... | collective-permute-start | bytes 6537224 | tf_op jit(solution)/shard_map/ppermute | solution.py:14
  135.6 13.0 %collective-permute-start.10 = (bf16[256,768]{1,0:T(8,128)(2,1)S(1)}, bf16[256,768]{1,0:T(8,128)(2,1)S(1)}, u32[]{:S(2)}, u32[]{:S(2)}) collective-permute-start(bf16[256,768]{1,0:T(8,128)(2,1)S(1)} %convolution_convert_fusion.9), channel_id=1, source_target_pairs={{0,128},{128,0},{1,129},{129,1},{2,130},{130,2},{3,131},{131,3},{4... | collective-permute-start | bytes 1179656 | tf_op jit(solution)/shard_map/ppermute | solution.py:14
  153.8 31.0 %collective-permute-start.13 = (bf16[304,3584]{1,0:T(8,128)(2,1)}, bf16[304,3584]{1,0:T(8,128)(2,1)}, u32[]{:S(2)}, u32[]{:S(2)}) collective-permute-start(bf16[304,3584]{1,0:T(8,128)(2,1)} %convolution_convert_fusion.2), channel_id=1, source_target_pairs={{0,32},{32,0},{1,33},{33,1},{2,34},{34,2},{3,35},{35,3},{4,36},{36... | collective-permute-start | bytes 6537224 | tf_op jit(solution)/shard_map/ppermute | solution.py:14
  153.8 33.8 %collective-permute-start.14 = (bf16[152,3584]{1,0:T(8,128)(2,1)}, bf16[152,3584]{1,0:T(8,128)(2,1)}, u32[]{:S(2)}, u32[]{:S(2)}) collective-permute-start(bf16[152,3584]{1,0:T(8,128)(2,1)} %add_convert_fusion.5), channel_id=1, source_target_pairs={{0,64},{64,0},{1,65},{65,1},{2,66},{66,2},{3,67},{67,3},{4,68},{68... | collective-permute-start | bytes 3268616 | tf_op jit(solution)/shard_map/ppermute | solution.py:14
  154.3 28.7 %all-to-all-start.3 = ((bf16[4,64,3584]{2,1,0:T(8,128)(2,1)}), bf16[4,64,3584]{2,1,0:T(8,128)(2,1)}, u32[]{:S(2)}, u32[]{:S(2)}) async-start(bf16[4,64,3584]{2,1,0:T(8,128)(2,1)} %bitcast.36), calls=%async_computation.3 | async-start | bytes 3670016 | tf_op jit(solution)/shard_map/all_to_all | solution.py:19
  162.3 33.4 %collective-permute-start.15 = (bf16[304,3584]{1,0:T(8,128)(2,1)}, bf16[304,3584]{1,0:T(8,128)(2,1)}, u32[]{:S(2)}, u32[]{:S(2)}) collective-permute-start(bf16[304,3584]{1,0:T(8,128)(2,1)} %convolution_convert_fusion), channel_id=1, source_target_pairs={{0,32},{32,0},{1,33},{33,1},{2,34},{34,2},{3,35},{35,3},{4,36},{36... | collective-permute-start | bytes 6537224 | tf_op jit(solution)/shard_map/ppermute | solution.py:14
  187.6 27.8 %all-to-all-start.4 = ((bf16[4,64,3584]{2,1,0:T(8,128)(2,1)}), bf16[4,64,3584]{2,1,0:T(8,128)(2,1)}, u32[]{:S(2)}, u32[]{:S(2)}) async-start(bf16[4,64,3584]{2,1,0:T(8,128)(2,1)} %bitcast.37), calls=%async_computation.4 | async-start | bytes 3670016 | tf_op jit(solution)/shard_map/all_to_all | solution.py:19
  194.2 25.5 %collective-permute-start.16 = (bf16[152,3584]{1,0:T(8,128)(2,1)}, bf16[152,3584]{1,0:T(8,128)(2,1)}, u32[]{:S(2)}, u32[]{:S(2)}) collective-permute-start(bf16[152,3584]{1,0:T(8,128)(2,1)} %add_convert_fusion.4), channel_id=1, source_target_pairs={{0,64},{64,0},{1,65},{65,1},{2,66},{66,2},{3,67},{67,3},{4,68},{68... | collective-permute-start | bytes 3268616 | tf_op jit(solution)/shard_map/ppermute | solution.py:14
  219.6 30.6 %all-to-all-start.5 = ((bf16[8,16,3584]{2,1,0:T(8,128)(2,1)}), bf16[8,16,3584]{2,1,0:T(8,128)(2,1)S(1)}, u32[]{:S(2)}, u32[]{:S(2)}) async-start(bf16[8,16,3584]{2,1,0:T(8,128)(2,1)} %pad_maximum_fusion), calls=%async_computation.5 | async-start | bytes 1835008 | tf_op jit(solution)/shard_map/all_to_all | solution.py:19
  229.0 24.5 %collective-permute-start.19 = (bf16[152,3584]{1,0:T(8,128)(2,1)}, bf16[152,3584]{1,0:T(8,128)(2,1)}, u32[]{:S(2)}, u32[]{:S(2)}) collective-permute-start(bf16[152,3584]{1,0:T(8,128)(2,1)} %add_convert_fusion.3), channel_id=1, source_target_pairs={{0,64},{64,0},{1,65},{65,1},{2,66},{66,2},{3,67},{67,3},{4,68},{68... | collective-permute-start | bytes 3268616 | tf_op jit(solution)/shard_map/ppermute | solution.py:14
  250.4 9.1 %collective-permute-start.18 = (bf16[4,3584]{1,0:T(4,128)(2,1)S(1)}, bf16[4,3584]{1,0:T(4,128)(2,1)S(1)}, u32[]{:S(2)}, u32[]{:S(2)}) collective-permute-start(bf16[4,3584]{1,0:T(4,128)(2,1)S(1)} %get-tuple-element.60), channel_id=1, source_target_pairs={{0,128},{128,0},{1,129},{129,1},{2,130},{130,2},{3,131},{131,3},{4... | collective-permute-start | bytes 86024 | tf_op jit(solution)/shard_map/ppermute | solution.py:14
  (13 other events, 106.5 us)

commit v7 on v6

--- a/solution.py
+++ b/solution.py
@@ -94,7 +94,7 @@
 
     pair = jnp.zeros((2 * units, width), BF)
     pair = place_near(place_near(pair, gate, dense_gate, 0), up, dense_up, units)
-    up_late, _ = lax.optimization_barrier((up, gate_x))
+    up_late, _, _ = lax.optimization_barrier((up, gate_x, pair))
     up_x = swap(up_late, ("xlo",))
     down_late, _ = lax.optimization_barrier((down, up_x))
     down_x = swap(down_late, ("xlo",))

time: 264 us -> 261 us (0.989)
    ppermute x20, waiting for transfers between devices: 33 us -> 24.7 us  [swap(): return lax.ppermute(value, axes, [(i, size - 1 - i) for i in range(size)])]
    all_to_all x3, waiting for transfers between devices: 23.2 us -> 31.2 us  [gather(): return lax.all_to_all(wide, axis, 0, 0, tiled=True)]
    all_to_all x3, starting transfers between devices: 17.9 us -> 15.2 us  [scatter(): lax.all_to_all(part.reshape(size, -1, part.shape[1]), axis, 0, 0, tiled=T...]
  transfers between devices with their start and end apart: 26 -> 26, of which waited for: 13 -> 13; matrix products, arithmetic and copies ran while one was open for 34% -> 35% of each run, Pallas kernels for 0% -> 0%
where the time goes in v7:
time: 261 us; the launch traced here: 260 us
  waiting for transfers between devices  100 us (38%)
  starting transfers between devices  57.7 us (22%)
  local copies, waits for them, and re-layouts  38.2 us (15%)
  matrix products  36.2 us (14%)
  other arithmetic  26.8 us (10%)
    all_to_all x3, waiting for transfers between devices, scatter(): lax.all_to_all(part.reshape(size, -1, part.shape[1]), axis, 0, 0, tiled=T...  44.2 us
    dot_general x10, matrix products, dot(): lax.dot_general(left, right, (dims, ((), ())), preferred_element_type=F32)  36.2 us
    dynamic_update_slice x15, local copies, waits for them, and re-layouts, place(): return lax.dynamic_update_slice_in_dim(buffer, part, at, axis=0)  34.3 us
    all_to_all x3, waiting for transfers between devices, gather(): return lax.all_to_all(wide, axis, 0, 0, tiled=True)  31.2 us
    ppermute x20, waiting for transfers between devices, swap(): return lax.ppermute(value, axes, [(i, size - 1 - i) for i in range(size)])  24.7 us
    ppermute x20, starting transfers between devices, swap(): return lax.ppermute(value, axes, [(i, size - 1 - i) for i in range(size)])  23.3 us
    all_to_all x3, starting transfers between devices, gather(): return lax.all_to_all(wide, axis, 0, 0, tiled=True)  19.2 us
    all_to_all x3, starting transfers between devices, scatter(): lax.all_to_all(part.reshape(size, -1, part.shape[1]), axis, 0, 0, tiled=T...  15.2 us
  transfers between devices with their start and end apart: 26, of which 13 were waited for; matrix products, arithmetic and copies ran while one was open for 35% of the time, Pallas kernels for 0%

profile of v7, /device:TPU:8, one launch (start us, length us, event | category | flops | bytes accessed | tf_op | source)
XLA Modules:
  0.0 260.0 jit_solution(5361179535682273480)
XLA Ops:
  3.0 3.1 %collective-permute-start = (bf16[8,3712]{1,0:T(8,128)(2,1)S(1)}, bf16[8,3712]{1,0:T(8,128)(2,1)S(1)}, u32[]{:S(2)}, u32[]{:S(2)}) collective-permute-start(bf16[8,3712]{1,0:T(8,128)(2,1)S(1)} %get-tuple-element.70), channel_id=1, source_target_pairs={{0,128},{128,0},{1,129},{129,1},{2,130},{130,2},{3,131},{131,3},{4... | collective-permute-start | bytes 178184 | tf_op jit(solution)/shard_map/ppermute | solution.py:14
  11.4 8.5 %all-to-all-start = ((bf16[8,16,3712]{2,1,0:T(8,128)(2,1)}), bf16[8,16,3712]{2,1,0:T(8,128)(2,1)S(1)}, u32[]{:S(2)}, u32[]{:S(2)}) async-start(bf16[8,16,3712]{2,1,0:T(8,128)(2,1)} %broadcast_in_dim.142), calls=%async_computation | async-start | bytes 1900544 | tf_op jit(solution)/shard_map/all_to_all | solution.py:30
  19.9 6.1 %dynamic_update_slice.45 = bf16[1536,3584]{1,0:T(8,128)(2,1)} pad(bf16[152,3584]{1,0:T(8,128)(2,1)} %bitcast.43, bf16[]{:T(256)} %constant.27.clone.1), padding=0_1384x0_0 | pad | bytes 12099586 | tf_op jit(solution)/shard_map/dynamic_update_slice | solution.py:38
  37.0 9.9 %all-to-all-done = bf16[8,16,3712]{2,1,0:T(8,128)(2,1)S(1)} async-done(((bf16[8,16,3712]{2,1,0:T(8,128)(2,1)}), bf16[8,16,3712]{2,1,0:T(8,128)(2,1)S(1)}, u32[]{:S(2)}, u32[]{:S(2)}) %all-to-all-start) | async-done | bytes 950304 | tf_op jit(solution)/shard_map/all_to_all | solution.py:30
  47.0 4.0 %dynamic_update_slice.53 = bf16[768,3584]{1,0:T(8,128)(2,1)} pad(bf16[152,3584]{1,0:T(8,128)(2,1)} %bitcast.39, bf16[]{:T(256)} %constant.27.clone.1), padding=0_616x0_0 | pad | bytes 6594562 | tf_op jit(solution)/shard_map/dynamic_update_slice | solution.py:38
  52.4 4.9 %all-to-all-start.1 = ((bf16[4,64,3712]{2,1,0:T(8,128)(2,1)}), bf16[4,64,3712]{2,1,0:T(8,128)(2,1)S(1)}, u32[]{:S(2)}, u32[]{:S(2)}) async-start(bf16[4,64,3712]{2,1,0:T(8,128)(2,1)} %broadcast_in_dim.144), calls=%async_computation.1 | async-start | bytes 3801088 | tf_op jit(solution)/shard_map/all_to_all | solution.py:30
  68.7 12.0 %all-to-all-done.1 = bf16[4,64,3712]{2,1,0:T(8,128)(2,1)S(1)} async-done(((bf16[4,64,3712]{2,1,0:T(8,128)(2,1)}), bf16[4,64,3712]{2,1,0:T(8,128)(2,1)S(1)}, u32[]{:S(2)}, u32[]{:S(2)}) %all-to-all-start.1) | async-done | bytes 1900576 | tf_op jit(solution)/shard_map/all_to_all | solution.py:30
  82.1 5.8 %all-to-all-start.2 = ((bf16[4,64,3584]{2,1,0:T(8,128)(2,1)}), bf16[4,64,3584]{2,1,0:T(8,128)(2,1)}, u32[]{:S(2)}, u32[]{:S(2)}) async-start(bf16[4,64,3584]{2,1,0:T(8,128)(2,1)} %broadcast_in_dim.146), calls=%async_computation.2 | async-start | bytes 3670016 | tf_op jit(solution)/shard_map/all_to_all | solution.py:30
  92.5 8.0 %convolution_convert_fusion.8 = bf16[256,1536]{1,0:T(8,128)(2,1)} fusion(bf16[1536,3584]{1,0:T(8,128)(2,1)} %constant_dynamic-update-slice_fusion.9, bf16[256,3712]{1,0:T(8,128)(2,1)S(1)} %bitcast.28), kind=kOutput, calls=%fused_computation.8 | convolution fusion | flops 2818965504 | bytes 13631488 | tf_op jit(solution)/shard_map/dot_general | solution.py:51
  100.5 9.4 %all-to-all-done.2 = bf16[4,64,3584]{2,1,0:T(8,128)(2,1)} async-done(((bf16[4,64,3584]{2,1,0:T(8,128)(2,1)}), bf16[4,64,3584]{2,1,0:T(8,128)(2,1)}, u32[]{:S(2)}, u32[]{:S(2)}) %all-to-all-start.2) | async-done | bytes 1835040 | tf_op jit(solution)/shard_map/all_to_all | solution.py:30
  116.6 4.8 %convolution_convert_fusion.9 = bf16[256,768]{1,0:T(8,128)(2,1)S(1)} fusion(bf16[256,3584]{1,0:T(8,128)(2,1)} %bitcast.6, bf16[768,3584]{1,0:T(8,128)(2,1)} %constant_dynamic-update-slice_fusion.6), kind=kOutput, calls=%fused_computation.17 | convolution fusion | flops 1409482752 | bytes 7733248 | tf_op jit(solution)/shard_map/dot_general | solution.py:51
  121.4 10.7 %collective-permute-done.11 = bf16[256,1536]{1,0:T(8,128)(2,1)S(1)} collective-permute-done((bf16[256,1536]{1,0:T(8,128)(2,1)}, bf16[256,1536]{1,0:T(8,128)(2,1)S(1)}, u32[]{:S(2)}, u32[]{:S(2)}) %collective-permute-start.11) | collective-permute-done | bytes 786464 | tf_op jit(solution)/shard_map/ppermute | solution.py:14
  143.6 5.0 %collective-permute-done.10 = bf16[256,768]{1,0:T(8,128)(2,1)S(1)} collective-permute-done((bf16[256,768]{1,0:T(8,128)(2,1)S(1)}, bf16[256,768]{1,0:T(8,128)(2,1)S(1)}, u32[]{:S(2)}, u32[]{:S(2)}) %collective-permute-start.10) | collective-permute-done | bytes 393248 | tf_op jit(solution)/shard_map/ppermute | solution.py:14
  154.3 5.8 %all-to-all-start.3 = ((bf16[4,64,3584]{2,1,0:T(8,128)(2,1)}), bf16[4,64,3584]{2,1,0:T(8,128)(2,1)}, u32[]{:S(2)}, u32[]{:S(2)}) async-start(bf16[4,64,3584]{2,1,0:T(8,128)(2,1)} %bitcast.36), calls=%async_computation.3 | async-start | bytes 3670016 | tf_op jit(solution)/shard_map/all_to_all | solution.py:19
  162.3 8.3 %convolution_convert_fusion.7 = bf16[256,3584]{1,0:T(8,128)(2,1)} fusion(bf16[1536,3584]{1,0:T(8,128)(2,1)} %constant_dynamic-update-slice_fusion.9, bf16[256,768]{1,0:T(8,128)(2,1)S(1)} %get-tuple-element.58, bf16[256,768]{1,0:T(8,128)(2,1)S(1)} %get-tuple-element.57), kind=kOutput, calls=%fused_computation.7 | convolution fusion | flops 2821062656 | bytes 13631488 | tf_op jit(solution)/shard_map/dot_general | solution.py:51
  172.7 10.2 %all-to-all-done.3 = bf16[4,64,3584]{2,1,0:T(8,128)(2,1)} async-done(((bf16[4,64,3584]{2,1,0:T(8,128)(2,1)}), bf16[4,64,3584]{2,1,0:T(8,128)(2,1)}, u32[]{:S(2)}, u32[]{:S(2)}) %all-to-all-start.3) | async-done | bytes 1835040 | tf_op jit(solution)/shard_map/all_to_all | solution.py:19
  187.6 5.8 %all-to-all-start.4 = ((bf16[4,64,3584]{2,1,0:T(8,128)(2,1)}), bf16[4,64,3584]{2,1,0:T(8,128)(2,1)}, u32[]{:S(2)}, u32[]{:S(2)}) async-start(bf16[4,64,3584]{2,1,0:T(8,128)(2,1)} %bitcast.37), calls=%async_computation.4 | async-start | bytes 3670016 | tf_op jit(solution)/shard_map/all_to_all | solution.py:19
  198.3 17.1 %all-to-all-done.4 = bf16[4,64,3584]{2,1,0:T(8,128)(2,1)} async-done(((bf16[4,64,3584]{2,1,0:T(8,128)(2,1)}), bf16[4,64,3584]{2,1,0:T(8,128)(2,1)}, u32[]{:S(2)}, u32[]{:S(2)}) %all-to-all-start.4) | async-done | bytes 1835040 | tf_op jit(solution)/shard_map/all_to_all | solution.py:19
  219.6 3.6 %all-to-all-start.5 = ((bf16[8,16,3584]{2,1,0:T(8,128)(2,1)}), bf16[8,16,3584]{2,1,0:T(8,128)(2,1)S(1)}, u32[]{:S(2)}, u32[]{:S(2)}) async-start(bf16[8,16,3584]{2,1,0:T(8,128)(2,1)} %pad_maximum_fusion), calls=%async_computation.5 | async-start | bytes 1835008 | tf_op jit(solution)/shard_map/all_to_all | solution.py:19
  223.2 3.1 %fusion.2 = bf16[1,152,3584]{2,1,0:T(8,128)(2,1)} fusion(bf16[152,3584]{1,0:T(8,128)(2,1)} %collective-permute-done.14, bf16[304,3584]{1,0:T(8,128)(2,1)} %copy-done.6, bf16[304,3584]{1,0:T(8,128)(2,1)S(1)} %copy-done.4), kind=kLoop, calls=%fused_computation.20 | loop fusion | flops 3268608 | bytes 4358144 | tf_op jit(solution)/shard_map/broadcast_in_dim | solution.py:141
  227.8 3.0 %fusion = bf16[1,152,3584]{2,1,0:T(8,128)(2,1)} fusion(bf16[152,3584]{1,0:T(8,128)(2,1)} %collective-permute-done.16, bf16[304,3584]{1,0:T(8,128)(2,1)} %collective-permute-done.13, bf16[304,3584]{1,0:T(8,128)(2,1)S(1)} %copy-done.2), kind=kLoop, calls=%fused_computation.18 | loop fusion | flops 3268608 | bytes 4358144 | tf_op jit(solution)/shard_map/broadcast_in_dim | solution.py:141
  230.8 16.8 %all-to-all-done.5 = bf16[8,16,3584]{2,1,0:T(8,128)(2,1)S(1)} async-done(((bf16[8,16,3584]{2,1,0:T(8,128)(2,1)}), bf16[8,16,3584]{2,1,0:T(8,128)(2,1)S(1)}, u32[]{:S(2)}, u32[]{:S(2)}) %all-to-all-start.5) | async-done | bytes 917536 | tf_op jit(solution)/shard_map/all_to_all | solution.py:19
  247.9 3.1 %collective-permute-start.18 = (bf16[4,3584]{1,0:T(4,128)(2,1)S(1)}, bf16[4,3584]{1,0:T(4,128)(2,1)S(1)}, u32[]{:S(2)}, u32[]{:S(2)}) collective-permute-start(bf16[4,3584]{1,0:T(4,128)(2,1)S(1)} %get-tuple-element.60), channel_id=1, source_target_pairs={{0,128},{128,0},{1,129},{129,1},{2,130},{130,2},{3,131},{131,3},{4... | collective-permute-start | bytes 86024 | tf_op jit(solution)/shard_map/ppermute | solution.py:14
  253.9 3.1 %collective-permute-start.17 = (bf16[4,3584]{1,0:T(4,128)(2,1)S(1)}, bf16[4,3584]{1,0:T(4,128)(2,1)S(1)}, u32[]{:S(2)}, u32[]{:S(2)}) collective-permute-start(bf16[4,3584]{1,0:T(4,128)(2,1)S(1)} %get-tuple-element.62), channel_id=1, source_target_pairs={{0,128},{128,0},{1,129},{129,1},{2,130},{130,2},{3,131},{131,3},{4... | collective-permute-start | bytes 86024 | tf_op jit(solution)/shard_map/ppermute | solution.py:14
  (110 shorter events, 86.9 us)
Async XLA Ops:
  3.0 5.8 %collective-permute-start = (bf16[8,3712]{1,0:T(8,128)(2,1)S(1)}, bf16[8,3712]{1,0:T(8,128)(2,1)S(1)}, u32[]{:S(2)}, u32[]{:S(2)}) collective-permute-start(bf16[8,3712]{1,0:T(8,128)(2,1)S(1)} %get-tuple-element.70), channel_id=1, source_target_pairs={{0,128},{128,0},{1,129},{129,1},{2,130},{130,2},{3,131},{131,3},{4... | collective-permute-start | bytes 178184 | tf_op jit(solution)/shard_map/ppermute | solution.py:14
  6.1 26.0 %collective-permute-start.2 = (bf16[152,3584]{1,0:T(8,128)(2,1)}, bf16[152,3584]{1,0:T(8,128)(2,1)S(1)}, u32[]{:S(2)}, u32[]{:S(2)}) collective-permute-start(bf16[152,3584]{1,0:T(8,128)(2,1)} %bitcast.1), channel_id=1, source_target_pairs={{0,32},{32,0},{1,33},{33,1},{2,34},{34,2},{3,35},{35,3},{4,36},{36... | collective-permute-start | bytes 3268616 | tf_op jit(solution)/shard_map/ppermute | solution.py:14
  8.8 17.3 %collective-permute-start.1 = (bf16[152,3584]{1,0:T(8,128)(2,1)}, bf16[152,3584]{1,0:T(8,128)(2,1)}, u32[]{:S(2)}, u32[]{:S(2)}) collective-permute-start(bf16[152,3584]{1,0:T(8,128)(2,1)} %bitcast.41), channel_id=1, source_target_pairs={{0,32},{32,0},{1,33},{33,1},{2,34},{34,2},{3,35},{35,3},{4,36},{36... | collective-permute-start | bytes 3268616 | tf_op jit(solution)/shard_map/ppermute | solution.py:14
  8.8 26.8 %collective-permute-start.3 = (bf16[152,3584]{1,0:T(8,128)(2,1)}, bf16[152,3584]{1,0:T(8,128)(2,1)}, u32[]{:S(2)}, u32[]{:S(2)}) collective-permute-start(bf16[152,3584]{1,0:T(8,128)(2,1)} %bitcast.42), channel_id=1, source_target_pairs={{0,64},{64,0},{1,65},{65,1},{2,66},{66,2},{3,67},{67,3},{4,68},{68... | collective-permute-start | bytes 3268616 | tf_op jit(solution)/shard_map/ppermute | solution.py:14
  11.4 35.5 %all-to-all-start = ((bf16[8,16,3712]{2,1,0:T(8,128)(2,1)}), bf16[8,16,3712]{2,1,0:T(8,128)(2,1)S(1)}, u32[]{:S(2)}, u32[]{:S(2)}) async-start(bf16[8,16,3712]{2,1,0:T(8,128)(2,1)} %broadcast_in_dim.142), calls=%async_computation | async-start | bytes 1900544 | tf_op jit(solution)/shard_map/all_to_all | solution.py:30
  35.6 26.0 %collective-permute-start.6 = (bf16[152,3584]{1,0:T(8,128)(2,1)}, bf16[152,3584]{1,0:T(8,128)(2,1)}, u32[]{:S(2)}, u32[]{:S(2)}) collective-permute-start(bf16[152,3584]{1,0:T(8,128)(2,1)} %bitcast.1), channel_id=1, source_target_pairs={{0,64},{64,0},{1,65},{65,1},{2,66},{66,2},{3,67},{67,3},{4,68},{68... | collective-permute-start | bytes 3268616 | tf_op jit(solution)/shard_map/ppermute | solution.py:14
  37.0 26.0 %collective-permute-start.4 = (bf16[152,3584]{1,0:T(8,128)(2,1)}, bf16[152,3584]{1,0:T(8,128)(2,1)}, u32[]{:S(2)}, u32[]{:S(2)}) collective-permute-start(bf16[152,3584]{1,0:T(8,128)(2,1)} %collective-permute-done.3), channel_id=1, source_target_pairs={{0,32},{32,0},{1,33},{33,1},{2,34},{34,2},{3,35},{35,3},{4,36},{36... | collective-permute-start | bytes 3268616 | tf_op jit(solution)/shard_map/ppermute | solution.py:14
  46.9 18.4 %collective-permute-start.5 = (bf16[152,3584]{1,0:T(8,128)(2,1)}, bf16[152,3584]{1,0:T(8,128)(2,1)}, u32[]{:S(2)}, u32[]{:S(2)}) collective-permute-start(bf16[152,3584]{1,0:T(8,128)(2,1)} %bitcast.38), channel_id=1, source_target_pairs={{0,32},{32,0},{1,33},{33,1},{2,34},{34,2},{3,35},{35,3},{4,36},{36... | collective-permute-start | bytes 3268616 | tf_op jit(solution)/shard_map/ppermute | solution.py:14
  52.4 28.3 %all-to-all-start.1 = ((bf16[4,64,3712]{2,1,0:T(8,128)(2,1)}), bf16[4,64,3712]{2,1,0:T(8,128)(2,1)S(1)}, u32[]{:S(2)}, u32[]{:S(2)}) async-start(bf16[4,64,3712]{2,1,0:T(8,128)(2,1)} %broadcast_in_dim.144), calls=%async_computation.1 | async-start | bytes 3801088 | tf_op jit(solution)/shard_map/all_to_all | solution.py:30
  61.5 39.0 %collective-permute-start.8 = (bf16[152,3584]{1,0:T(8,128)(2,1)}, bf16[152,3584]{1,0:T(8,128)(2,1)}, u32[]{:S(2)}, u32[]{:S(2)}) collective-permute-start(bf16[152,3584]{1,0:T(8,128)(2,1)} %bitcast.40), channel_id=1, source_target_pairs={{0,64},{64,0},{1,65},{65,1},{2,66},{66,2},{3,67},{67,3},{4,68},{68... | collective-permute-start | bytes 3268616 | tf_op jit(solution)/shard_map/ppermute | solution.py:14
  63.0 27.2 %collective-permute-start.7 = (bf16[152,3584]{1,0:T(8,128)(2,1)}, bf16[152,3584]{1,0:T(8,128)(2,1)}, u32[]{:S(2)}, u32[]{:S(2)}) collective-permute-start(bf16[152,3584]{1,0:T(8,128)(2,1)} %collective-permute-done.6), channel_id=1, source_target_pairs={{0,32},{32,0},{1,33},{33,1},{2,34},{34,2},{3,35},{35,3},{4,36},{36... | collective-permute-start | bytes 3268616 | tf_op jit(solution)/shard_map/ppermute | solution.py:14
  82.1 27.8 %all-to-all-start.2 = ((bf16[4,64,3584]{2,1,0:T(8,128)(2,1)}), bf16[4,64,3584]{2,1,0:T(8,128)(2,1)}, u32[]{:S(2)}, u32[]{:S(2)}) async-start(bf16[4,64,3584]{2,1,0:T(8,128)(2,1)} %broadcast_in_dim.146), calls=%async_computation.2 | async-start | bytes 3670016 | tf_op jit(solution)/shard_map/all_to_all | solution.py:30
  110.1 21.9 %collective-permute-start.11 = (bf16[256,1536]{1,0:T(8,128)(2,1)}, bf16[256,1536]{1,0:T(8,128)(2,1)S(1)}, u32[]{:S(2)}, u32[]{:S(2)}) collective-permute-start(bf16[256,1536]{1,0:T(8,128)(2,1)} %convolution_convert_fusion.8), channel_id=1, source_target_pairs={{0,128},{128,0},{1,129},{129,1},{2,130},{130,2},{3,131},{131,3},{4... | collective-permute-start | bytes 2359304 | tf_op jit(solution)/shard_map/ppermute | solution.py:14
  135.5 13.2 %collective-permute-start.12 = (bf16[304,3584]{1,0:T(8,128)(2,1)S(1)}, bf16[304,3584]{1,0:T(8,128)(2,1)S(1)}, u32[]{:S(2)}, u32[]{:S(2)}) collective-permute-start(bf16[304,3584]{1,0:T(8,128)(2,1)S(1)} %convolution_convert_fusion.4), channel_id=1, source_target_pairs={{0,32},{32,0},{1,33},{33,1},{2,34},{34,2},{3,35},{35,3},{4,36},{36... | collective-permute-start | bytes 6537224 | tf_op jit(solution)/shard_map/ppermute | solution.py:14
  135.6 13.0 %collective-permute-start.10 = (bf16[256,768]{1,0:T(8,128)(2,1)S(1)}, bf16[256,768]{1,0:T(8,128)(2,1)S(1)}, u32[]{:S(2)}, u32[]{:S(2)}) collective-permute-start(bf16[256,768]{1,0:T(8,128)(2,1)S(1)} %convolution_convert_fusion.9), channel_id=1, source_target_pairs={{0,128},{128,0},{1,129},{129,1},{2,130},{130,2},{3,131},{131,3},{4... | collective-permute-start | bytes 1179656 | tf_op jit(solution)/shard_map/ppermute | solution.py:14
  153.8 31.0 %collective-permute-start.13 = (bf16[304,3584]{1,0:T(8,128)(2,1)}, bf16[304,3584]{1,0:T(8,128)(2,1)}, u32[]{:S(2)}, u32[]{:S(2)}) collective-permute-start(bf16[304,3584]{1,0:T(8,128)(2,1)} %convolution_convert_fusion.2), channel_id=1, source_target_pairs={{0,32},{32,0},{1,33},{33,1},{2,34},{34,2},{3,35},{35,3},{4,36},{36... | collective-permute-start | bytes 6537224 | tf_op jit(solution)/shard_map/ppermute | solution.py:14
  153.8 33.8 %collective-permute-start.14 = (bf16[152,3584]{1,0:T(8,128)(2,1)}, bf16[152,3584]{1,0:T(8,128)(2,1)}, u32[]{:S(2)}, u32[]{:S(2)}) collective-permute-start(bf16[152,3584]{1,0:T(8,128)(2,1)} %add_convert_fusion.5), channel_id=1, source_target_pairs={{0,64},{64,0},{1,65},{65,1},{2,66},{66,2},{3,67},{67,3},{4,68},{68... | collective-permute-start | bytes 3268616 | tf_op jit(solution)/shard_map/ppermute | solution.py:14
  154.3 28.7 %all-to-all-start.3 = ((bf16[4,64,3584]{2,1,0:T(8,128)(2,1)}), bf16[4,64,3584]{2,1,0:T(8,128)(2,1)}, u32[]{:S(2)}, u32[]{:S(2)}) async-start(bf16[4,64,3584]{2,1,0:T(8,128)(2,1)} %bitcast.36), calls=%async_computation.3 | async-start | bytes 3670016 | tf_op jit(solution)/shard_map/all_to_all | solution.py:19
  162.3 33.4 %collective-permute-start.15 = (bf16[304,3584]{1,0:T(8,128)(2,1)}, bf16[304,3584]{1,0:T(8,128)(2,1)}, u32[]{:S(2)}, u32[]{:S(2)}) collective-permute-start(bf16[304,3584]{1,0:T(8,128)(2,1)} %convolution_convert_fusion), channel_id=1, source_target_pairs={{0,32},{32,0},{1,33},{33,1},{2,34},{34,2},{3,35},{35,3},{4,36},{36... | collective-permute-start | bytes 6537224 | tf_op jit(solution)/shard_map/ppermute | solution.py:14
  187.6 27.8 %all-to-all-start.4 = ((bf16[4,64,3584]{2,1,0:T(8,128)(2,1)}), bf16[4,64,3584]{2,1,0:T(8,128)(2,1)}, u32[]{:S(2)}, u32[]{:S(2)}) async-start(bf16[4,64,3584]{2,1,0:T(8,128)(2,1)} %bitcast.37), calls=%async_computation.4 | async-start | bytes 3670016 | tf_op jit(solution)/shard_map/all_to_all | solution.py:19
  194.2 25.5 %collective-permute-start.16 = (bf16[152,3584]{1,0:T(8,128)(2,1)}, bf16[152,3584]{1,0:T(8,128)(2,1)}, u32[]{:S(2)}, u32[]{:S(2)}) collective-permute-start(bf16[152,3584]{1,0:T(8,128)(2,1)} %add_convert_fusion.4), channel_id=1, source_target_pairs={{0,64},{64,0},{1,65},{65,1},{2,66},{66,2},{3,67},{67,3},{4,68},{68... | collective-permute-start | bytes 3268616 | tf_op jit(solution)/shard_map/ppermute | solution.py:14
  219.6 28.0 %all-to-all-start.5 = ((bf16[8,16,3584]{2,1,0:T(8,128)(2,1)}), bf16[8,16,3584]{2,1,0:T(8,128)(2,1)S(1)}, u32[]{:S(2)}, u32[]{:S(2)}) async-start(bf16[8,16,3584]{2,1,0:T(8,128)(2,1)} %pad_maximum_fusion), calls=%async_computation.5 | async-start | bytes 1835008 | tf_op jit(solution)/shard_map/all_to_all | solution.py:19
  226.3 24.7 %collective-permute-start.19 = (bf16[152,3584]{1,0:T(8,128)(2,1)}, bf16[152,3584]{1,0:T(8,128)(2,1)}, u32[]{:S(2)}, u32[]{:S(2)}) collective-permute-start(bf16[152,3584]{1,0:T(8,128)(2,1)} %add_convert_fusion.3), channel_id=1, source_target_pairs={{0,64},{64,0},{1,65},{65,1},{2,66},{66,2},{3,67},{67,3},{4,68},{68... | collective-permute-start | bytes 3268616 | tf_op jit(solution)/shard_map/ppermute | solution.py:14
  247.9 9.2 %collective-permute-start.18 = (bf16[4,3584]{1,0:T(4,128)(2,1)S(1)}, bf16[4,3584]{1,0:T(4,128)(2,1)S(1)}, u32[]{:S(2)}, u32[]{:S(2)}) collective-permute-start(bf16[4,3584]{1,0:T(4,128)(2,1)S(1)} %get-tuple-element.60), channel_id=1, source_target_pairs={{0,128},{128,0},{1,129},{129,1},{2,130},{130,2},{3,131},{131,3},{4... | collective-permute-start | bytes 86024 | tf_op jit(solution)/shard_map/ppermute | solution.py:14
  (13 other events, 93.1 us)
